TPU v7x, 32 devices: a whole 2x2x4 slice. The times are simulated.
32 devices in a mesh: dp: 4 (over y, core), pipe: 2 (over x), tensor: 4 (over z).
Axes of the slice: x: 2, y: 2, z: 4, core: 2. Of those that a mesh axis runs over, the one named last changes fastest.
Arguments:
- hidden: bfloat16 [1536, 2048], P(('dp', 'pipe'), 'tensor'), parts along dimension 0, may hold values from -20 to 20
- weight: bfloat16 [2048, 9216], P(None, ('pipe', 'tensor')), may hold values from -16 to 16
- targets: int32 [1536], P('dp'), parts along dimension 0, may hold values from 0 to 9215
- row_weight: float32 [1536], P('dp'), parts along dimension 0, may hold values from 2 to 20
Outputs:
- grad_hidden: bfloat16 [1536, 2048], P(('dp', 'pipe'), 'tensor'), parts along dimension 0
- row_loss: float32 [1536], P('dp'), parts along dimension 0
There are 4 independent parts, one for each index of `dp`. A program takes and returns all parts, laid end to end along the dimension named above; an argument that names none is the same for every part. Nothing has to cross between parts.
All inputs are finite; a program needn't handle non-finite values.
Results may differ from a plain program's by a relative error of at most 0.0051.
Values may be sent and summed in bfloat16 or wider, within the bound.
No kernel may reach another device: no remote copies, remote signals or barrier semaphores. Data moves between devices by JAX's collectives and lax.ppermute only.
A program may use at most 64 MiB of HBM per device.

v0:
```python
import jax
import jax.numpy as jnp
from jax import lax
from jax.sharding import PartitionSpec as P


def per_device(hidden, weight, targets, row_weight):
    features = lax.all_gather(hidden, "tensor", axis=1, tiled=True)
    logits = jnp.dot(
        lax.all_gather(features, "pipe", axis=0, tiled=True),
        weight,
        preferred_element_type=jnp.float32,
    )
    vocab_dev = weight.shape[1]
    offset = (
        lax.axis_index("pipe") * lax.axis_size("tensor") + lax.axis_index("tensor")
    ) * vocab_dev
    columns = lax.broadcasted_iota(jnp.int32, logits.shape, 1) + offset
    is_target = columns == targets[:, None]
    local_label = jnp.sum(jnp.where(is_target, logits, jnp.zeros_like(logits)), axis=1)
    local_max = jnp.max(logits, axis=1)
    row_max = lax.pmax(local_max, ("pipe", "tensor"))
    shifted = jnp.exp(logits - row_max[:, None])
    sum_exp, label_logit = lax.psum((jnp.sum(shifted, axis=1), local_label), ("pipe", "tensor"))
    row_loss = jnp.log(sum_exp) + row_max - label_logit
    dlogits = (
        row_weight[:, None] * (shifted / sum_exp[:, None] - is_target.astype(jnp.float32))
    ).astype(jnp.bfloat16)
    contract = (((1,), (1,)), ((), ()))
    partial_sum = lax.dot_general(dlogits, weight, contract, preferred_element_type=jnp.float32)
    own_features = lax.psum_scatter(partial_sum, "tensor", scatter_dimension=1, tiled=True)
    grad_hidden = lax.psum_scatter(own_features, "pipe", scatter_dimension=0, tiled=True)
    return (grad_hidden.astype(jnp.bfloat16), row_loss)


def solution(mesh):
    in_specs = (P(("dp", "pipe"), "tensor"), P(None, ("pipe", "tensor")), P("dp"), P("dp"))
    out_specs = (P(("dp", "pipe"), "tensor"), P("dp"))
    return jax.shard_map(
        per_device, mesh=mesh, in_specs=in_specs, out_specs=out_specs, check_vma=False
    )
```

profile of v0, /device:TPU:0, one launch (start us, length us, event | category | flops | bytes accessed | tf_op | source)
XLA Modules:
  0.0 194.2 jit_solution(13686621387531697931)
XLA Ops:
  7.2 0.0 all-gather.2.cloned.1.call-start
  7.2 21.8 %all_gather.6 = bf16[192,2048]{1,0:T(8,128)(2,1)} all-gather(bf16[192,512]{1,0:T(8,128)(2,1)} %param.4), channel_id=1, replica_groups=mesh['dp'=4,'pipe'=2,'tensor'=4] {'tensor'}, dimensions={1}, use_global_device_ids=true | all-gather | bytes 983040 | tf_op jit(solution)/shard_map/all_gather | solution.py:8
  29.0 0.0 all-gather.2.cloned.1.call-update
  29.1 0.0 reduce-scatter.3.cloned.1.call-start
  29.1 0.0 copy-start
  29.1 27.0 %all-gather.2.cloned.1.call-done = bf16[384,2048]{1,0:T(8,128)(2,1)} async-done(((bf16[192,2048]{1,0:T(8,128)(2,1)}), bf16[384,2048]{1,0:T(8,128)(2,1)}) %all-gather.2.cloned.1.call-update) | async-done | bytes 1572880 | tf_op jit(solution)/shard_map/all_gather | solution.py:10
  56.2 5.1 %fusion.12 = (f32[384]{0:T(512)S(1)}, f32[384,1152]{1,0:T(8,128)S(1)}) fusion(bf16[384,2048]{1,0:T(8,128)(2,1)} %all-gather.2.cloned.1.call-done, bf16[2048,1152]{1,0:T(8,128)(2,1)} %param.5), kind=kOutput, calls=%fused_computation.16 | convolution fusion | flops 1812381312 | bytes 8062464 | tf_op jit(solution)/shard_map/dot_general | solution.py:9
  61.3 0.0 copy-start.1
  61.3 20.5 %pmax.7 = f32[384]{0:T(512)S(1)} all-reduce(f32[384]{0:T(512)S(1)} %get-tuple-element.6), channel_id=1, replica_groups=mesh['dp'=4,'pipe'=2,'tensor'=4] {'pipe','tensor'}, use_global_device_ids=true, to_apply=%region_1.2 | all-reduce | flops 384 | bytes 3072 | tf_op jit(solution)/shard_map/pmax | solution.py:22
  81.8 0.0 copy-done
  81.8 0.6 fusion.3
  82.4 17.2 %all-reduce = (f32[384]{0:T(512)S(1)}, f32[384]{0:T(512)S(1)}) all-reduce(f32[384]{0:T(512)S(1)} %get-tuple-element.3, f32[384]{0:T(512)S(1)} %get-tuple-element.2), channel_id=1, replica_groups=mesh['dp'=4,'pipe'=2,'tensor'=4] {'pipe','tensor'}, use_global_device_ids=true, to_apply=%region_3.4 | all-reduce | flops 768 | bytes 6144 | tf_op jit(solution)/shard_map/psum | solution.py:24
  99.6 0.0 copy-done.1
  99.6 6.7 %fusion.5 = f32[384,2048]{1,0:T(8,128)} fusion(bf16[2048,1152]{1,0:T(8,128)(2,1)} %param.5, f32[384,1152]{1,0:T(8,128)S(1)} %get-tuple-element.7, s32[1152]{0:T(1024)S(1)} %iota_add_fusion, f32[384]{0:T(512)S(1)} %get-tuple-element.4, f32[384]{0:T(512)S(1)} %pmax.7, f32[384]{0:T(512)S(1)} %copy-done.1, s32[384]{0:T(512)S(1)} %copy-done), kind=kOutput, calls=%fused_computation.8 | convolution fusion | flops 1815035904 | bytes 9644544 | tf_op jit(solution)/shard_map/dot_general | solution.py:30
  106.3 0.0 reduce-scatter.3.cloned.1.call-update
  106.3 0.0 reduce-scatter.5.cloned.1.call-start
  106.4 59.9 %reduce-scatter.3.cloned.1.call-done = f32[384,512]{1,0:T(8,128)} async-done(((f32[384,2048]{1,0:T(8,128)}), f32[384,512]{1,0:T(8,128)}) %reduce-scatter.3.cloned.1.call-update) | async-done | bytes 786448 | tf_op jit(solution)/shard_map/reduce_scatter | solution.py:31
  166.3 0.0 reduce-scatter.5.cloned.1.call-update
  166.3 0.6 add_subtract_fusion
  166.9 19.1 %reduce-scatter.5.cloned.1.call-done = f32[192,512]{1,0:T(8,128)} async-done(((f32[384,512]{1,0:T(8,128)}), f32[192,512]{1,0:T(8,128)}) %reduce-scatter.5.cloned.1.call-update) | async-done | bytes 393232 | tf_op jit(solution)/shard_map/reduce_scatter | solution.py:32
  186.0 1.7 convert_element_type.11
  (1 shorter events, 0.0 us)
Async XLA Ops:
  7.2 49.0 %all-gather.2.cloned.1.call-start = ((), (), s32[]{:S(2)}) async-start(), calls=%async_computation.2 | async-start | bytes 2359296 | tf_op jit(solution)/shard_map/all_gather | solution.py:10
  29.1 137.2 %reduce-scatter.3.cloned.1.call-start = ((), (), s32[]{:S(2)}) async-start(), calls=%async_computation.3 | async-start | bytes 3932160 | tf_op jit(solution)/shard_map/reduce_scatter | solution.py:31
  29.1 52.7 %copy-start = (s32[384]{0:T(512)S(1)}, s32[384]{0:T(512)}, u32[]{:S(2)}) copy-start(s32[384]{0:T(512)} %param.6) | copy-start | bytes 4612
  61.3 38.4 %copy-start.1 = (f32[384]{0:T(512)S(1)}, f32[384]{0:T(512)}, u32[]{:S(2)}) copy-start(f32[384]{0:T(512)} %param.7) | copy-start | bytes 4612
  106.3 79.7 %reduce-scatter.5.cloned.1.call-start = ((), (), s32[]{:S(2)}) async-start(), calls=%async_computation.4 | async-start | bytes 1179648 | tf_op jit(solution)/shard_map/reduce_scatter | solution.py:32
Sparse Core Ops, SparseCore 0:
  29.2 26.9 all-gather.1
  106.4 59.7 reduce-scatter.2
  168.5 17.4 reduce-scatter.4
where the time goes:
time: 195 us; the launch traced here: 194 us
  waiting for transfers between devices  106 us (54%)
  blocking collectives  59.6 us (31%)
  between operations  13.8 us (7%)
  matrix products  11.8 us (6%)
  other arithmetic  2.89 us (1%)
    reduce_scatter x1, waiting for transfers between devices, per_device(): lax.psum_scatter(partial_sum, 'tensor', scatter_dimension=1, tiled=True)  59.9 us
    all_gather x1, waiting for transfers between devices, per_device(): lax.all_gather(features, 'pipe', axis=0, tiled=True)  27 us
    all_gather x1, blocking collectives, per_device(): features = lax.all_gather(hidden, 'tensor', axis=1, tiled=True)  21.8 us
    pmax x1, blocking collectives, per_device(): row_max = lax.pmax(local_max, ('pipe', 'tensor'))  20.5 us
    reduce_scatter x1, waiting for transfers between devices, per_device(): lax.psum_scatter(own_features, 'pipe', scatter_dimension=0, tiled=True)  19.1 us
    psum x1, blocking collectives, per_device(): lax.psum((jnp.sum(shifted, axis=1), local_label), ('pipe', 'tensor'))  17.2 us
    dot_general x1, matrix products, per_device(): lax.dot_general(dlogits, weight, contract, preferred_element_type=jnp.flo...  6.66 us
    dot_general x1, matrix products, per_device(): jnp.dot(lax.all_gather(features, 'pipe', axis=0, tiled=True), weight, pre...  5.11 us
  transfers between devices with their start and end apart: 3, of which 3 were waited for; matrix products, arithmetic and copies ran while one was open for 0% of the time, Pallas kernels for 0%

commit v1 on v0

v1 whole, which is shorter than its diff:
```python
import jax
import jax.numpy as jnp
from jax import lax
from jax.sharding import PartitionSpec as P

CHUNKS = 1


def partners(n, k):
    if n & (n - 1):
        return [(i, (i + k) % n) for i in range(n)]
    return [(i, i ^ k) for i in range(n)]


def source(me, n, k):
    if n & (n - 1):
        return lax.rem(me - k + n, n)
    return me ^ k


def target(me, n, k):
    if n & (n - 1):
        return lax.rem(me + k, n)
    return me ^ k


def merge(a, b):
    top = jnp.maximum(a[0], b[0])
    total = a[1] * jnp.exp(a[0] - top) + b[1] * jnp.exp(b[0] - top)
    return jnp.stack([top, total, a[2] + b[2]])


def per_device(hidden, weight, targets, row_weight):
    pipes, tensors = lax.axis_size("pipe"), lax.axis_size("tensor")
    px, tz = lax.axis_index("pipe"), lax.axis_index("tensor")
    rows, width = hidden.shape
    vocab_dev = weight.shape[1]
    offset = (px * tensors + tz) * vocab_dev
    bf16, f32 = jnp.bfloat16, jnp.float32

    w_in = [lax.dynamic_slice_in_dim(weight, source(tz, tensors, k) * width, width, 0) for k in range(tensors)]
    if tensors & (tensors - 1):
        w_out = [lax.dynamic_slice_in_dim(weight, target(tz, tensors, k) * width, width, 0) for k in range(tensors)]
    else:
        w_out = w_in

    def tensor_permute(a, k):
        return a if k == 0 else lax.ppermute(a, "tensor", partners(tensors, k))

    def pipe_permute(a, j):
        return a if j == 0 else lax.ppermute(a, "pipe", partners(pipes, j))

    step = rows // CHUNKS
    local_targets = [targets.reshape(pipes, rows)[source(px, pipes, j)] for j in range(pipes)]
    local_scale = [row_weight.reshape(pipes, rows)[source(px, pipes, j)] for j in range(pipes)]
    columns = lax.broadcasted_iota(jnp.int32, (step, vocab_dev), 1) + offset
    grads, losses = [], []
    for c in range(CHUNKS):
        piece = hidden[c * step : (c + 1) * step]
        arrived = [tensor_permute(piece, k) for k in range(tensors)]
        logits, stats = [], []
        for j in range(pipes):
            acc = 0
            for k in range(tensors):
                acc += jnp.dot(pipe_permute(arrived[k], j), w_in[k], preferred_element_type=f32)
            logits.append(acc)
            t = local_targets[j][c * step : (c + 1) * step]
            m = jnp.max(acc, axis=1)
            s = jnp.sum(jnp.exp(acc - m[:, None]), axis=1)
            label = jnp.sum(jnp.where(columns == t[:, None], acc, 0.0), axis=1)
            stats.append(jnp.stack([m, s, label]))
        mine = jnp.stack(stats)
        if pipes == 2:
            other = pipe_permute(mine, 1)[::-1]
            mine = jax.vmap(merge)(mine, other)
        else:
            whole = jnp.zeros_like(mine)
            for j in range(pipes):
                whole = whole.at[source(px, pipes, j)].set(mine[j])
            every = lax.all_gather(whole, "pipe")
            whole = every[0]
            for p in range(1, pipes):
                whole = jax.vmap(merge)(whole, every[p])
            mine = jnp.stack([whole[source(px, pipes, j)] for j in range(pipes)])
        total = mine
        for k in range(1, tensors):
            total = jax.vmap(merge)(total, tensor_permute(mine, k))
        dlogits = []
        loss = jnp.zeros((pipes, step), f32)
        for j in range(pipes):
            m, s, label = total[j]
            t = local_targets[j][c * step : (c + 1) * step]
            g = local_scale[j][c * step : (c + 1) * step]
            hit = (columns == t[:, None]).astype(f32)
            dlogits.append((g[:, None] * (jnp.exp(logits[j] - m[:, None]) / s[:, None] - hit)).astype(bf16))
            loss = loss.at[source(px, pipes, j)].set(jnp.log(s) + m - label)
        losses.append(loss)
        contract = (((1,), (1,)), ((), ()))
        sums = [None] * tensors
        for k in list(range(tensors - 1, -1, -1)):
            acc = 0
            for j in range(pipes - 1, -1, -1):
                part = lax.dot_general(dlogits[j], w_out[k], contract, preferred_element_type=f32)
                if j:
                    part = lax.ppermute(part.astype(bf16), "pipe", [(b, a) for a, b in partners(pipes, j)]).astype(f32)
                acc += part
            if k:
                acc = tensor_permute(acc.astype(bf16), k).astype(f32)
            sums[k] = acc
        grads.append(sum(sums[1:], sums[0]).astype(bf16))
    grad = jnp.concatenate(grads, axis=0)
    row_loss = jnp.concatenate(losses, axis=1).reshape(-1)
    return grad, row_loss


def solution(mesh):
    in_specs = (P(("dp", "pipe"), "tensor"), P(None, ("pipe", "tensor")), P("dp"), P("dp"))
    out_specs = (P(("dp", "pipe"), "tensor"), P("dp"))
    return jax.shard_map(
        per_device, mesh=mesh, in_specs=in_specs, out_specs=out_specs, check_vma=False
    )
```

time: 195 us -> 77.4 us (0.40)
  waiting for transfers between devices: 106 us -> 25.2 us
  blocking collectives: 59.6 us -> 0 us
  starting transfers between devices: 0.12 us -> 22.6 us
  between operations: 13.8 us -> 0.95 us
  matrix products: 11.8 us -> 22.3 us
    reduce_scatter x2 -> x0, waiting for transfers between devices: 79 us -> none  [the longest x1 59.9 us: per_device(): lax.psum_scatter(partial_sum, 'tensor', scatter_dimension=1, tiled=True)]
    all_gather x1 -> x0, waiting for transfers between devices: 27 us -> none  [per_device(): lax.all_gather(features, 'pipe', axis=0, tiled=True)]
    ppermute x0 -> x18, waiting for transfers between devices: none -> 25.2 us  [the longest x9 21.1 us: tensor_permute(): return a if k == 0 else lax.ppermute(a, 'tensor', partners(tensors, k))]
    ppermute x0 -> x18, starting transfers between devices: none -> 22.6 us  [the longest x9 12.3 us: tensor_permute(): return a if k == 0 else lax.ppermute(a, 'tensor', partners(tensors, k))]
    all_gather x1 -> x0, blocking collectives: 21.8 us -> none  [per_device(): features = lax.all_gather(hidden, 'tensor', axis=1, tiled=True)]
    pmax x1 -> x0, blocking collectives: 20.5 us -> none  [per_device(): row_max = lax.pmax(local_max, ('pipe', 'tensor'))]
    psum x1 -> x0, blocking collectives: 17.2 us -> none  [per_device(): lax.psum((jnp.sum(shifted, axis=1), local_label), ('pipe', 'tensor'))]
    dot_general x2 -> x16, matrix products: 11.8 us -> 22.3 us  [the longest x8 14.5 us: per_device(): lax.dot_general(dlogits[j], w_out[k], contract, preferred_element_type=f32)]
  transfers between devices with their start and end apart: 3 -> 18, of which waited for: 3 -> 9; matrix products, arithmetic and copies ran while one was open for 0% -> 23% of each run, Pallas kernels for 0% -> 0%
where the time goes in v1:
time: 77.4 us; the launch traced here: 76.9 us
  waiting for transfers between devices  25.2 us (33%)
  starting transfers between devices  22.6 us (29%)
  matrix products  22.3 us (29%)
  other arithmetic  4.23 us (5%)
  local copies, waits for them, and re-layouts  1.63 us (2%)
  between operations  0.95 us (1%)
    ppermute x9, waiting for transfers between devices, tensor_permute(): return a if k == 0 else lax.ppermute(a, 'tensor', partners(tensors, k))  21.1 us
    dot_general x8, matrix products, per_device(): lax.dot_general(dlogits[j], w_out[k], contract, preferred_element_type=f32)  14.5 us
    ppermute x9, starting transfers between devices, tensor_permute(): return a if k == 0 else lax.ppermute(a, 'tensor', partners(tensors, k))  12.3 us
    dot_general x8, matrix products, per_device(): jnp.dot(pipe_permute(arrived[k], j), w_in[k], preferred_element_type=f32)  7.74 us
    ppermute x5, starting transfers between devices, pipe_permute(): return a if j == 0 else lax.ppermute(a, 'pipe', partners(pipes, j))  6.16 us
    ppermute x4, starting transfers between devices, per_device(): lax.ppermute(part.astype(bf16), 'pipe', [(b, a) for a, b in partners(pipe...  4.12 us
    ppermute x4, waiting for transfers between devices, per_device(): lax.ppermute(part.astype(bf16), 'pipe', [(b, a) for a, b in partners(pipe...  2.78 us
    another operation x3, other arithmetic  2.05 us
  transfers between devices with their start and end apart: 18, of which 9 were waited for; matrix products, arithmetic and copies ran while one was open for 23% of the time, Pallas kernels for 0%

profile of v1, /device:TPU:0, one launch (start us, length us, event | category | flops | bytes accessed | tf_op | source)
XLA Modules:
  0.0 76.9 jit_solution(8197429497623224235)
XLA Ops:
  0.6 3.0 %collective-permute-start = (bf16[192,512]{1,0:T(8,128)(2,1)}, bf16[192,512]{1,0:T(8,128)(2,1)S(1)}, u32[]{:S(2)}, u32[]{:S(2)}) collective-permute-start(bf16[192,512]{1,0:T(8,128)(2,1)} %param.8), channel_id=1, source_target_pairs={{0,4},{4,0},{1,5},{5,1},{2,6},{6,2},{3,7},{7,3},{8,12},{12,8},{9,1... | collective-permute-start | bytes 589832 | tf_op jit(solution)/shard_map/ppermute | solution.py:51
  3.6 1.6 %collective-permute-start.1 = (bf16[192,512]{1,0:T(8,128)(2,1)}, bf16[192,512]{1,0:T(8,128)(2,1)S(1)}, u32[]{:S(2)}, u32[]{:S(2)}) collective-permute-start(bf16[192,512]{1,0:T(8,128)(2,1)} %param.8), channel_id=1, source_target_pairs={{0,1},{1,0},{2,3},{3,2},{4,5},{5,4},{6,7},{7,6},{8,9},{9,8},{10,11... | collective-permute-start | bytes 589832 | tf_op jit(solution)/shard_map/ppermute | solution.py:48
  5.2 2.5 %collective-permute-start.5 = (bf16[192,512]{1,0:T(8,128)(2,1)}, bf16[192,512]{1,0:T(8,128)(2,1)S(1)}, u32[]{:S(2)}, u32[]{:S(2)}) collective-permute-start(bf16[192,512]{1,0:T(8,128)(2,1)} %param.8), channel_id=1, source_target_pairs={{0,3},{1,2},{2,1},{3,0},{4,7},{5,6},{6,5},{7,4},{8,11},{9,10},{10,... | collective-permute-start | bytes 589832 | tf_op jit(solution)/shard_map/ppermute | solution.py:48
  7.8 0.8 reshape.509
  8.6 1.9 %fusion.40 = f32[1152,192]{0,1:T(8,128)S(1)} fusion(bf16[192,512]{1,0:T(8,128)(2,1)} %param.8, bf16[2048,1152]{1,0:T(8,128)(2,1)} %param.9, s32[]{:T(128)S(6)} %select_n.34), kind=kOutput, calls=%fused_computation.56 | convolution fusion | flops 226492416 | bytes 2260996 | tf_op jit(solution)/shard_map/dot_general | solution.py:65
  10.9 0.5 collective-permute-start.2
  11.4 6.6 %collective-permute-done.5 = bf16[192,512]{1,0:T(8,128)(2,1)S(1)} collective-permute-done((bf16[192,512]{1,0:T(8,128)(2,1)}, bf16[192,512]{1,0:T(8,128)(2,1)S(1)}, u32[]{:S(2)}, u32[]{:S(2)}) %collective-permute-start.5) | collective-permute-done | bytes 196640 | tf_op jit(solution)/shard_map/ppermute | solution.py:48
  18.0 0.5 collective-permute-start.6
  18.5 6.5 %collective-permute-done.3 = bf16[192,512]{1,0:T(8,128)(2,1)S(1)} collective-permute-done((bf16[192,512]{1,0:T(8,128)(2,1)}, bf16[192,512]{1,0:T(8,128)(2,1)S(1)}, u32[]{:S(2)}, u32[]{:S(2)}) %collective-permute-start.3) | collective-permute-done | bytes 196640 | tf_op jit(solution)/shard_map/ppermute | solution.py:48
  25.0 0.5 collective-permute-start.4
  25.6 1.7 %fusion.23 = f32[1152,192]{0,1:T(8,128)S(1)} fusion(bf16[192,512]{1,0:T(8,128)(2,1)S(1)} %collective-permute-done.5, bf16[2048,1152]{1,0:T(8,128)(2,1)} %param.9, s32[]{:T(128)S(6)} %select_n.37), kind=kOutput, calls=%fused_computation.39 | convolution fusion | flops 226492416 | bytes 2260996 | tf_op jit(solution)/shard_map/dot_general | solution.py:65
  27.3 1.7 %convolution_add_fusion.1 = f32[1152,192]{0,1:T(8,128)S(1)} fusion(f32[1152,192]{0,1:T(8,128)S(1)} %fusion.40, bf16[192,512]{1,0:T(8,128)(2,1)S(1)} %collective-permute-done.1, bf16[2048,1152]{1,0:T(8,128)(2,1)} %param.9, s32[]{:T(128)S(6)} %select_n.35), kind=kOutput, calls=%fused_computation.1 | convolution fusion | flops 226713600 | bytes 3145732 | tf_op jit(solution)/shard_map/dot_general | solution.py:65
  29.0 0.5 fusion.93
  29.5 0.4 fusion.38
  30.0 0.4 convolution_add_fusion.3
  30.5 0.4 fusion.21
  30.9 0.5 fusion.94
  31.5 0.6 fusion.11
  32.1 1.6 %collective-permute-start.7 = (f32[2,3,192]{2,1,0:T(4,128)S(1)}, f32[2,3,192]{2,1,0:T(4,128)S(1)}, u32[]{:S(2)}, u32[]{:S(2)}) collective-permute-start(f32[2,3,192]{2,1,0:T(4,128)S(1)} %pad_maximum_fusion), channel_id=1, source_target_pairs={{0,4},{4,0},{1,5},{5,1},{2,6},{6,2},{3,7},{7,3},{8,12},{12,8},{9,1... | collective-permute-start | bytes 13832 | tf_op jit(solution)/shard_map/ppermute | solution.py:51
  33.6 0.8 %and_reduce_fusion = (pred[]{:T(512)}, pred[]{:T(512)}) fusion(s32[2]{0:T(128)S(1)} %copy-done.2, s32[1]{0:T(128)} %constant.69.clone.1, s32[1]{0:T(128)} %bitcast.44, s32[1]{0:T(128)} %bitcast.42), kind=kLoop, calls=%fused_computation.137 | loop fusion | flops 18 | bytes 22 | tf_op jit(solution)/shard_map/reduce.3
  34.5 1.3 %collective-permute-done.7 = f32[2,3,192]{2,1,0:T(4,128)S(1)} collective-permute-done((f32[2,3,192]{2,1,0:T(4,128)S(1)}, f32[2,3,192]{2,1,0:T(4,128)S(1)}, u32[]{:S(2)}, u32[]{:S(2)}) %collective-permute-start.7) | collective-permute-done | bytes 4640 | tf_op jit(solution)/shard_map/ppermute | solution.py:51
  35.9 1.5 %collective-permute-start.8 = (f32[2,3,192]{2,1,0:T(4,128)S(1)}, f32[2,3,192]{2,1,0:T(4,128)S(1)}, u32[]{:S(2)}, u32[]{:S(2)}) collective-permute-start(f32[2,3,192]{2,1,0:T(4,128)S(1)} %maximum_bitcast_fusion), channel_id=1, source_target_pairs={{0,1},{1,0},{2,3},{3,2},{4,5},{5,4},{6,7},{7,6},{8,9},{9,8},{10,11... | collective-permute-start | bytes 13832 | tf_op jit(solution)/shard_map/ppermute | solution.py:48
  37.4 1.7 %collective-permute-start.9 = (f32[2,3,192]{2,1,0:T(4,128)S(1)}, f32[2,3,192]{2,1,0:T(4,128)S(1)}, u32[]{:S(2)}, u32[]{:S(2)}) collective-permute-start(f32[2,3,192]{2,1,0:T(4,128)S(1)} %maximum_bitcast_fusion), channel_id=1, source_target_pairs={{0,2},{1,3},{2,0},{3,1},{4,6},{5,7},{6,4},{7,5},{8,10},{9,11},{10,... | collective-permute-start | bytes 13832 | tf_op jit(solution)/shard_map/ppermute | solution.py:48
  39.1 1.2 %collective-permute-start.10 = (f32[2,3,192]{2,1,0:T(4,128)S(1)}, f32[2,3,192]{2,1,0:T(4,128)S(1)}, u32[]{:S(2)}, u32[]{:S(2)}) collective-permute-start(f32[2,3,192]{2,1,0:T(4,128)S(1)} %maximum_bitcast_fusion), channel_id=1, source_target_pairs={{0,3},{1,2},{2,1},{3,0},{4,7},{5,6},{6,5},{7,4},{8,11},{9,10},{10,... | collective-permute-start | bytes 13832 | tf_op jit(solution)/shard_map/ppermute | solution.py:48
  40.4 1.6 %collective-permute-done.9 = f32[2,3,192]{2,1,0:T(4,128)S(1)} collective-permute-done((f32[2,3,192]{2,1,0:T(4,128)S(1)}, f32[2,3,192]{2,1,0:T(4,128)S(1)}, u32[]{:S(2)}, u32[]{:S(2)}) %collective-permute-start.9) | collective-permute-done | bytes 4640 | tf_op jit(solution)/shard_map/ppermute | solution.py:48
  42.0 2.6 %collective-permute-done.10 = f32[2,3,192]{2,1,0:T(4,128)S(1)} collective-permute-done((f32[2,3,192]{2,1,0:T(4,128)S(1)}, f32[2,3,192]{2,1,0:T(4,128)S(1)}, u32[]{:S(2)}, u32[]{:S(2)}) %collective-permute-start.10) | collective-permute-done | bytes 4640 | tf_op jit(solution)/shard_map/ppermute | solution.py:48
  44.6 0.6 fusion.87
  45.3 0.6 fusion.5
  45.9 1.8 %convolution_convert_fusion.2 = bf16[192,512]{1,0:T(8,128)(2,1)S(1)} fusion(bf16[192,1152]{1,0:T(8,128)(2,1)S(1)} %get-tuple-element.46, bf16[2048,1152]{1,0:T(8,128)(2,1)} %param.9, s32[]{:T(128)S(6)} %select_n.35), kind=kOutput, calls=%fused_computation.8 | convolution fusion | flops 226590720 | bytes 1818628 | tf_op jit(solution)/shard_map/dot_general | solution.py:103
  47.7 1.8 %convolution_convert_fusion.1 = bf16[192,512]{1,0:T(8,128)(2,1)S(1)} fusion(bf16[192,1152]{1,0:T(8,128)(2,1)S(1)} %get-tuple-element.46, bf16[2048,1152]{1,0:T(8,128)(2,1)} %param.9, s32[]{:T(128)S(6)} %select_n.36), kind=kOutput, calls=%fused_computation.7 | convolution fusion | flops 226590720 | bytes 1818628 | tf_op jit(solution)/shard_map/dot_general | solution.py:103
  49.5 1.8 %convolution_convert_fusion = bf16[192,512]{1,0:T(8,128)(2,1)S(1)} fusion(bf16[192,1152]{1,0:T(8,128)(2,1)S(1)} %get-tuple-element.46, bf16[2048,1152]{1,0:T(8,128)(2,1)} %param.9, s32[]{:T(128)S(6)} %select_n.37), kind=kOutput, calls=%fused_computation.6 | convolution fusion | flops 226590720 | bytes 1818628 | tf_op jit(solution)/shard_map/dot_general | solution.py:103
  51.4 0.6 broadcast_select_fusion
  52.1 0.7 reshape.511
  52.8 1.5 %collective-permute-start.12 = (bf16[192,512]{1,0:T(8,128)(2,1)S(1)}, bf16[192,512]{1,0:T(8,128)(2,1)S(1)}, u32[]{:S(2)}, u32[]{:S(2)}) collective-permute-start(bf16[192,512]{1,0:T(8,128)(2,1)S(1)} %convolution_convert_fusion.2), channel_id=1, source_target_pairs={{4,0},{0,4},{5,1},{1,5},{6,2},{2,6},{7,3},{3,7},{12,8},{8,12},{13,... | collective-permute-start | bytes 589832 | tf_op jit(solution)/shard_map/ppermute | solution.py:105
  54.3 0.5 collective-permute-start.14
  54.8 1.5 %collective-permute-start.16 = (bf16[192,512]{1,0:T(8,128)(2,1)S(1)}, bf16[192,512]{1,0:T(8,128)(2,1)S(1)}, u32[]{:S(2)}, u32[]{:S(2)}) collective-permute-start(bf16[192,512]{1,0:T(8,128)(2,1)S(1)} %convolution_convert_fusion), channel_id=1, source_target_pairs={{4,0},{0,4},{5,1},{1,5},{6,2},{2,6},{7,3},{3,7},{12,8},{8,12},{13,... | collective-permute-start | bytes 589832 | tf_op jit(solution)/shard_map/ppermute | solution.py:105
  56.3 1.8 %convolution_convert_fusion.3 = bf16[192,512]{1,0:T(8,128)(2,1)S(1)} fusion(bf16[192,1152]{1,0:T(8,128)(2,1)S(1)} %get-tuple-element.46, bf16[2048,1152]{1,0:T(8,128)(2,1)} %param.9, s32[]{:T(128)S(6)} %select_n.34), kind=kOutput, calls=%fused_computation.9 | convolution fusion | flops 226590720 | bytes 1818628 | tf_op jit(solution)/shard_map/dot_general | solution.py:103
  58.1 0.6 collective-permute-start.11
  58.7 1.9 %collective-permute-done.12 = bf16[192,512]{1,0:T(8,128)(2,1)S(1)} collective-permute-done((bf16[192,512]{1,0:T(8,128)(2,1)S(1)}, bf16[192,512]{1,0:T(8,128)(2,1)S(1)}, u32[]{:S(2)}, u32[]{:S(2)}) %collective-permute-start.12) | collective-permute-done | bytes 196640 | tf_op jit(solution)/shard_map/ppermute | solution.py:105
  60.6 1.8 %add_convert_fusion.3 = bf16[192,512]{1,0:T(8,128)(2,1)S(1)} fusion(bf16[192,512]{1,0:T(8,128)(2,1)S(1)} %collective-permute-done.12, bf16[192,1152]{1,0:T(8,128)(2,1)S(1)} %get-tuple-element.45, bf16[2048,1152]{1,0:T(8,128)(2,1)} %param.9, s32[]{:T(128)S(6)} %select_n.35), kind=kOutput, calls=%fused_computation.61 | convolution fusion | flops 226787328 | bytes 2015236 | tf_op jit(solution)/shard_map/dot_general | solution.py:103
  62.5 0.9 %collective-permute-done.14 = bf16[192,512]{1,0:T(8,128)(2,1)S(1)} collective-permute-done((bf16[192,512]{1,0:T(8,128)(2,1)S(1)}, bf16[192,512]{1,0:T(8,128)(2,1)S(1)}, u32[]{:S(2)}, u32[]{:S(2)}) %collective-permute-start.14) | collective-permute-done | bytes 196640 | tf_op jit(solution)/shard_map/ppermute | solution.py:105
  63.4 1.8 %add_convert_fusion.2 = bf16[192,512]{1,0:T(8,128)(2,1)S(1)} fusion(bf16[192,512]{1,0:T(8,128)(2,1)S(1)} %collective-permute-done.14, bf16[192,1152]{1,0:T(8,128)(2,1)S(1)} %get-tuple-element.45, bf16[2048,1152]{1,0:T(8,128)(2,1)} %param.9, s32[]{:T(128)S(6)} %select_n.36), kind=kOutput, calls=%fused_computation.60 | convolution fusion | flops 226787328 | bytes 2015236 | tf_op jit(solution)/shard_map/dot_general | solution.py:103
  65.2 1.0 %collective-permute-start.15 = (bf16[192,512]{1,0:T(8,128)(2,1)S(1)}, bf16[192,512]{1,0:T(8,128)(2,1)S(1)}, u32[]{:S(2)}, u32[]{:S(2)}) collective-permute-start(bf16[192,512]{1,0:T(8,128)(2,1)S(1)} %add_convert_fusion.2), channel_id=1, source_target_pairs={{0,2},{1,3},{2,0},{3,1},{4,6},{5,7},{6,4},{7,5},{8,10},{9,11},{10,... | collective-permute-start | bytes 589832 | tf_op jit(solution)/shard_map/ppermute | solution.py:48
  66.2 1.8 %add_convert_fusion.1 = bf16[192,512]{1,0:T(8,128)(2,1)S(1)} fusion(bf16[192,512]{1,0:T(8,128)(2,1)S(1)} %collective-permute-done.16, bf16[192,1152]{1,0:T(8,128)(2,1)S(1)} %get-tuple-element.45, bf16[2048,1152]{1,0:T(8,128)(2,1)} %param.9, s32[]{:T(128)S(6)} %select_n.37), kind=kOutput, calls=%fused_computation.59 | convolution fusion | flops 226787328 | bytes 2015236 | tf_op jit(solution)/shard_map/dot_general | solution.py:103
  68.0 2.7 %collective-permute-start.17 = (bf16[192,512]{1,0:T(8,128)(2,1)S(1)}, bf16[192,512]{1,0:T(8,128)(2,1)S(1)}, u32[]{:S(2)}, u32[]{:S(2)}) collective-permute-start(bf16[192,512]{1,0:T(8,128)(2,1)S(1)} %add_convert_fusion.1), channel_id=1, source_target_pairs={{0,3},{1,2},{2,1},{3,0},{4,7},{5,6},{6,5},{7,4},{8,11},{9,10},{10,... | collective-permute-start | bytes 589832 | tf_op jit(solution)/shard_map/ppermute | solution.py:48
  70.7 1.8 %fusion.35 = f32[192,512]{1,0:T(8,128)S(1)} fusion(bf16[192,1152]{1,0:T(8,128)(2,1)S(1)} %get-tuple-element.45, bf16[2048,1152]{1,0:T(8,128)(2,1)} %param.9, s32[]{:T(128)S(6)} %select_n.34), kind=kOutput, calls=%fused_computation.51 | convolution fusion | flops 226492416 | bytes 2015236 | tf_op jit(solution)/shard_map/dot_general | solution.py:103
  72.5 3.6 %collective-permute-done.15 = bf16[192,512]{1,0:T(8,128)(2,1)S(1)} collective-permute-done((bf16[192,512]{1,0:T(8,128)(2,1)S(1)}, bf16[192,512]{1,0:T(8,128)(2,1)S(1)}, u32[]{:S(2)}, u32[]{:S(2)}) %collective-permute-start.15) | collective-permute-done | bytes 196640 | tf_op jit(solution)/shard_map/ppermute | solution.py:48
  76.1 0.8 %add_convert_fusion = bf16[192,512]{1,0:T(8,128)(2,1)} fusion(bf16[192,512]{1,0:T(8,128)(2,1)S(1)} %collective-permute-done.17, bf16[192,512]{1,0:T(8,128)(2,1)S(1)} %collective-permute-done.15, bf16[192,512]{1,0:T(8,128)(2,1)S(1)} %collective-permute-done.13, f32[192,512]{1,0:T(8,128)S(1)} %fusion.35, bf16[192,512]{1,0:T(8,128)(2,1)S(1)} %collective-permute-done.11), kind=kLoop, calls=%fused_computation.58 | loop fusion | flops 884736 | bytes 1376256 | tf_op jit(solution)/shard_map/convert_element_type | solution.py:110
  (40 shorter events, 0.9 us)
Async XLA Ops:
  0.6 28.9 %collective-permute-start = (bf16[192,512]{1,0:T(8,128)(2,1)}, bf16[192,512]{1,0:T(8,128)(2,1)S(1)}, u32[]{:S(2)}, u32[]{:S(2)}) collective-permute-start(bf16[192,512]{1,0:T(8,128)(2,1)} %param.8), channel_id=1, source_target_pairs={{0,4},{4,0},{1,5},{5,1},{2,6},{6,2},{3,7},{7,3},{8,12},{12,8},{9,1... | collective-permute-start | bytes 589832 | tf_op jit(solution)/shard_map/ppermute | solution.py:51
  3.6 7.2 %collective-permute-start.1 = (bf16[192,512]{1,0:T(8,128)(2,1)}, bf16[192,512]{1,0:T(8,128)(2,1)S(1)}, u32[]{:S(2)}, u32[]{:S(2)}) collective-permute-start(bf16[192,512]{1,0:T(8,128)(2,1)} %param.8), channel_id=1, source_target_pairs={{0,1},{1,0},{2,3},{3,2},{4,5},{5,4},{6,7},{7,6},{8,9},{9,8},{10,11... | collective-permute-start | bytes 589832 | tf_op jit(solution)/shard_map/ppermute | solution.py:48
  5.2 12.8 %collective-permute-start.5 = (bf16[192,512]{1,0:T(8,128)(2,1)}, bf16[192,512]{1,0:T(8,128)(2,1)S(1)}, u32[]{:S(2)}, u32[]{:S(2)}) collective-permute-start(bf16[192,512]{1,0:T(8,128)(2,1)} %param.8), channel_id=1, source_target_pairs={{0,3},{1,2},{2,1},{3,0},{4,7},{5,6},{6,5},{7,4},{8,11},{9,10},{10,... | collective-permute-start | bytes 589832 | tf_op jit(solution)/shard_map/ppermute | solution.py:48
  7.7 17.3 %collective-permute-start.3 = (bf16[192,512]{1,0:T(8,128)(2,1)}, bf16[192,512]{1,0:T(8,128)(2,1)S(1)}, u32[]{:S(2)}, u32[]{:S(2)}) collective-permute-start(bf16[192,512]{1,0:T(8,128)(2,1)} %param.8), channel_id=1, source_target_pairs={{0,2},{1,3},{2,0},{3,1},{4,6},{5,7},{6,4},{7,5},{8,10},{9,11},{10,... | collective-permute-start | bytes 589832 | tf_op jit(solution)/shard_map/ppermute | solution.py:48
  8.6 20.4 %copy-start = (bf16[2048,1152]{1,0:T(8,128)(2,1)S(1)}, bf16[2048,1152]{1,0:T(8,128)(2,1)}, u32[]{:S(2)}) copy-start(bf16[2048,1152]{1,0:T(8,128)(2,1)} %param.9) | copy-start | bytes 14155780
  10.9 19.1 %collective-permute-start.2 = (bf16[192,512]{1,0:T(8,128)(2,1)S(1)}, bf16[192,512]{1,0:T(8,128)(2,1)S(1)}, u32[]{:S(2)}, u32[]{:S(2)}) collective-permute-start(bf16[192,512]{1,0:T(8,128)(2,1)S(1)} %collective-permute-done.1), channel_id=1, source_target_pairs={{0,4},{4,0},{1,5},{5,1},{2,6},{6,2},{3,7},{7,3},{8,12},{12,8},{9,1... | collective-permute-start | bytes 589832 | tf_op jit(solution)/shard_map/ppermute | solution.py:51
  18.0 12.4 %collective-permute-start.6 = (bf16[192,512]{1,0:T(8,128)(2,1)S(1)}, bf16[192,512]{1,0:T(8,128)(2,1)S(1)}, u32[]{:S(2)}, u32[]{:S(2)}) collective-permute-start(bf16[192,512]{1,0:T(8,128)(2,1)S(1)} %collective-permute-done.5), channel_id=1, source_target_pairs={{0,4},{4,0},{1,5},{5,1},{2,6},{6,2},{3,7},{7,3},{8,12},{12,8},{9,1... | collective-permute-start | bytes 589832 | tf_op jit(solution)/shard_map/ppermute | solution.py:51
  25.0 5.9 %collective-permute-start.4 = (bf16[192,512]{1,0:T(8,128)(2,1)S(1)}, bf16[192,512]{1,0:T(8,128)(2,1)S(1)}, u32[]{:S(2)}, u32[]{:S(2)}) collective-permute-start(bf16[192,512]{1,0:T(8,128)(2,1)S(1)} %collective-permute-done.3), channel_id=1, source_target_pairs={{0,4},{4,0},{1,5},{5,1},{2,6},{6,2},{3,7},{7,3},{8,12},{12,8},{9,1... | collective-permute-start | bytes 589832 | tf_op jit(solution)/shard_map/ppermute | solution.py:51
  30.4 3.2 %copy-start.2 = (s32[2]{0:T(128)S(1)}, s32[2]{0:T(128)}, u32[]{:S(2)}) copy-start(s32[2]{0:T(128)} %constant.70.clone.1) | copy-start | bytes 28
  30.4 4.0 %copy-start.1 = (f32[384]{0:T(512)S(1)}, f32[384]{0:T(512)}, u32[]{:S(2)}) copy-start(f32[384]{0:T(512)} %param.11) | copy-start | bytes 4612
  32.1 3.7 %collective-permute-start.7 = (f32[2,3,192]{2,1,0:T(4,128)S(1)}, f32[2,3,192]{2,1,0:T(4,128)S(1)}, u32[]{:S(2)}, u32[]{:S(2)}) collective-permute-start(f32[2,3,192]{2,1,0:T(4,128)S(1)} %pad_maximum_fusion), channel_id=1, source_target_pairs={{0,4},{4,0},{1,5},{5,1},{2,6},{6,2},{3,7},{7,3},{8,12},{12,8},{9,1... | collective-permute-start | bytes 13832 | tf_op jit(solution)/shard_map/ppermute | solution.py:51
  35.9 4.5 %collective-permute-start.8 = (f32[2,3,192]{2,1,0:T(4,128)S(1)}, f32[2,3,192]{2,1,0:T(4,128)S(1)}, u32[]{:S(2)}, u32[]{:S(2)}) collective-permute-start(f32[2,3,192]{2,1,0:T(4,128)S(1)} %maximum_bitcast_fusion), channel_id=1, source_target_pairs={{0,1},{1,0},{2,3},{3,2},{4,5},{5,4},{6,7},{7,6},{8,9},{9,8},{10,11... | collective-permute-start | bytes 13832 | tf_op jit(solution)/shard_map/ppermute | solution.py:48
  37.4 4.6 %collective-permute-start.9 = (f32[2,3,192]{2,1,0:T(4,128)S(1)}, f32[2,3,192]{2,1,0:T(4,128)S(1)}, u32[]{:S(2)}, u32[]{:S(2)}) collective-permute-start(f32[2,3,192]{2,1,0:T(4,128)S(1)} %maximum_bitcast_fusion), channel_id=1, source_target_pairs={{0,2},{1,3},{2,0},{3,1},{4,6},{5,7},{6,4},{7,5},{8,10},{9,11},{10,... | collective-permute-start | bytes 13832 | tf_op jit(solution)/shard_map/ppermute | solution.py:48
  39.1 5.4 %collective-permute-start.10 = (f32[2,3,192]{2,1,0:T(4,128)S(1)}, f32[2,3,192]{2,1,0:T(4,128)S(1)}, u32[]{:S(2)}, u32[]{:S(2)}) collective-permute-start(f32[2,3,192]{2,1,0:T(4,128)S(1)} %maximum_bitcast_fusion), channel_id=1, source_target_pairs={{0,3},{1,2},{2,1},{3,0},{4,7},{5,6},{6,5},{7,4},{8,11},{9,10},{10,... | collective-permute-start | bytes 13832 | tf_op jit(solution)/shard_map/ppermute | solution.py:48
  52.8 7.8 %collective-permute-start.12 = (bf16[192,512]{1,0:T(8,128)(2,1)S(1)}, bf16[192,512]{1,0:T(8,128)(2,1)S(1)}, u32[]{:S(2)}, u32[]{:S(2)}) collective-permute-start(bf16[192,512]{1,0:T(8,128)(2,1)S(1)} %convolution_convert_fusion.2), channel_id=1, source_target_pairs={{4,0},{0,4},{5,1},{1,5},{6,2},{2,6},{7,3},{3,7},{12,8},{8,12},{13,... | collective-permute-start | bytes 589832 | tf_op jit(solution)/shard_map/ppermute | solution.py:105
  54.3 9.1 %collective-permute-start.14 = (bf16[192,512]{1,0:T(8,128)(2,1)S(1)}, bf16[192,512]{1,0:T(8,128)(2,1)S(1)}, u32[]{:S(2)}, u32[]{:S(2)}) collective-permute-start(bf16[192,512]{1,0:T(8,128)(2,1)S(1)} %convolution_convert_fusion.1), channel_id=1, source_target_pairs={{4,0},{0,4},{5,1},{1,5},{6,2},{2,6},{7,3},{3,7},{12,8},{8,12},{13,... | collective-permute-start | bytes 589832 | tf_op jit(solution)/shard_map/ppermute | solution.py:105
  54.8 11.4 %collective-permute-start.16 = (bf16[192,512]{1,0:T(8,128)(2,1)S(1)}, bf16[192,512]{1,0:T(8,128)(2,1)S(1)}, u32[]{:S(2)}, u32[]{:S(2)}) collective-permute-start(bf16[192,512]{1,0:T(8,128)(2,1)S(1)} %convolution_convert_fusion), channel_id=1, source_target_pairs={{4,0},{0,4},{5,1},{1,5},{6,2},{2,6},{7,3},{3,7},{12,8},{8,12},{13,... | collective-permute-start | bytes 589832 | tf_op jit(solution)/shard_map/ppermute | solution.py:105
  58.1 14.4 %collective-permute-start.11 = (bf16[192,512]{1,0:T(8,128)(2,1)S(1)}, bf16[192,512]{1,0:T(8,128)(2,1)S(1)}, u32[]{:S(2)}, u32[]{:S(2)}) collective-permute-start(bf16[192,512]{1,0:T(8,128)(2,1)S(1)} %convolution_convert_fusion.3), channel_id=1, source_target_pairs={{4,0},{0,4},{5,1},{1,5},{6,2},{2,6},{7,3},{3,7},{12,8},{8,12},{13,... | collective-permute-start | bytes 589832 | tf_op jit(solution)/shard_map/ppermute | solution.py:105
  62.4 10.1 %collective-permute-start.13 = (bf16[192,512]{1,0:T(8,128)(2,1)S(1)}, bf16[192,512]{1,0:T(8,128)(2,1)S(1)}, u32[]{:S(2)}, u32[]{:S(2)}) collective-permute-start(bf16[192,512]{1,0:T(8,128)(2,1)S(1)} %add_convert_fusion.3), channel_id=1, source_target_pairs={{0,1},{1,0},{2,3},{3,2},{4,5},{5,4},{6,7},{7,6},{8,9},{9,8},{10,11... | collective-permute-start | bytes 589832 | tf_op jit(solution)/shard_map/ppermute | solution.py:48
  65.2 10.8 %collective-permute-start.15 = (bf16[192,512]{1,0:T(8,128)(2,1)S(1)}, bf16[192,512]{1,0:T(8,128)(2,1)S(1)}, u32[]{:S(2)}, u32[]{:S(2)}) collective-permute-start(bf16[192,512]{1,0:T(8,128)(2,1)S(1)} %add_convert_fusion.2), channel_id=1, source_target_pairs={{0,2},{1,3},{2,0},{3,1},{4,6},{5,7},{6,4},{7,5},{8,10},{9,11},{10,... | collective-permute-start | bytes 589832 | tf_op jit(solution)/shard_map/ppermute | solution.py:48
  68.0 8.1 %collective-permute-start.17 = (bf16[192,512]{1,0:T(8,128)(2,1)S(1)}, bf16[192,512]{1,0:T(8,128)(2,1)S(1)}, u32[]{:S(2)}, u32[]{:S(2)}) collective-permute-start(bf16[192,512]{1,0:T(8,128)(2,1)S(1)} %add_convert_fusion.1), channel_id=1, source_target_pairs={{0,3},{1,2},{2,1},{3,0},{4,7},{5,6},{6,5},{7,4},{8,11},{9,10},{10,... | collective-permute-start | bytes 589832 | tf_op jit(solution)/shard_map/ppermute | solution.py:48

commit v2 on v0

v2 whole, which is shorter than its diff:
```python
import jax
import jax.numpy as jnp
from jax import lax
from jax.experimental import pallas as pl
from jax.experimental.pallas import tpu as pltpu
from jax.sharding import PartitionSpec as P

BF16, F32 = jnp.bfloat16, jnp.float32
ROWS_BY_ROWS = (((1,), (1,)), ((), ()))
VMEM = pl.BlockSpec(memory_space=pltpu.VMEM)
SMEM = pl.BlockSpec(memory_space=pltpu.SMEM)
HBM = pl.BlockSpec(memory_space=pltpu.HBM)
LIMIT = pltpu.CompilerParams(vmem_limit_bytes=24 * 2**20)


def partners(n, k):
    if n & (n - 1):
        return [(i, (i + k) % n) for i in range(n)]
    return [(i, i ^ k) for i in range(n)]


def source(me, n, k):
    if n & (n - 1):
        return lax.rem(me - k + n, n)
    return me ^ k


def target(me, n, k):
    if n & (n - 1):
        return lax.rem(me + k, n)
    return me ^ k


def merge(a, b):
    top = jnp.maximum(a[0], b[0])
    total = a[1] * jnp.exp(a[0] - top) + b[1] * jnp.exp(b[0] - top)
    return jnp.stack([top, total, a[2] + b[2]])


def any_mesh(hidden, weight, targets, row_weight):
    pipes, tensors = lax.axis_size("pipe"), lax.axis_size("tensor")
    px, tz = lax.axis_index("pipe"), lax.axis_index("tensor")
    rows, width = hidden.shape
    vocab_dev = weight.shape[1]
    offset = (px * tensors + tz) * vocab_dev

    w_in = [lax.dynamic_slice_in_dim(weight, source(tz, tensors, k) * width, width, 0) for k in range(tensors)]
    w_out = [lax.dynamic_slice_in_dim(weight, target(tz, tensors, k) * width, width, 0) for k in range(tensors)]

    def tensor_permute(a, k):
        return a if k == 0 else lax.ppermute(a, "tensor", partners(tensors, k))

    def pipe_permute(a, j):
        return a if j == 0 else lax.ppermute(a, "pipe", partners(pipes, j))

    local_targets = [targets.reshape(pipes, rows)[source(px, pipes, j)] for j in range(pipes)]
    local_scale = [row_weight.reshape(pipes, rows)[source(px, pipes, j)] for j in range(pipes)]
    columns = lax.broadcasted_iota(jnp.int32, (rows, vocab_dev), 1) + offset
    arrived = [tensor_permute(hidden, k) for k in range(tensors)]
    logits, stats = [], []
    for j in range(pipes):
        acc = 0
        for k in range(tensors):
            acc += jnp.dot(pipe_permute(arrived[k], j), w_in[k], preferred_element_type=F32)
        logits.append(acc)
        m = jnp.max(acc, axis=1)
        s = jnp.sum(jnp.exp(acc - m[:, None]), axis=1)
        label = jnp.sum(jnp.where(columns == local_targets[j][:, None], acc, 0.0), axis=1)
        stats.append(jnp.stack([m, s, label]))
    mine = jnp.stack(stats)
    whole = jnp.zeros_like(mine)
    for j in range(pipes):
        whole = whole.at[source(px, pipes, j)].set(mine[j])
    every = lax.all_gather(whole, "pipe")
    whole = every[0]
    for p in range(1, pipes):
        whole = jax.vmap(merge)(whole, every[p])
    total = whole
    for k in range(1, tensors):
        total = jax.vmap(merge)(total, tensor_permute(whole, k))
    row_loss = (jnp.log(total[:, 1]) + total[:, 0] - total[:, 2]).reshape(-1)
    dlogits = []
    for j in range(pipes):
        m, s, _ = total[source(px, pipes, j)]
        hit = (columns == local_targets[j][:, None]).astype(F32)
        scaled = jnp.exp(logits[j] - m[:, None]) / s[:, None] - hit
        dlogits.append((local_scale[j][:, None] * scaled).astype(BF16))
    sums = [None] * tensors
    for k in range(tensors - 1, -1, -1):
        acc = 0
        for j in range(pipes - 1, -1, -1):
            part = lax.dot_general(dlogits[j], w_out[k], ROWS_BY_ROWS, preferred_element_type=F32)
            if j:
                part = lax.ppermute(part.astype(BF16), "pipe", [(b, a) for a, b in partners(pipes, j)]).astype(F32)
            acc += part
        if k:
            acc = tensor_permute(acc.astype(BF16), k).astype(F32)
        sums[k] = acc
    return sum(sums[1:], sums[0]).astype(BF16), row_loss


def block(ref, place, k, width):
    return ref[pl.ds(pl.multiple_of(place[k] * width, width), width), :]


def columns_of(row_list):
    rows = row_list[0].shape[1]
    table = jnp.concatenate(row_list + [jnp.zeros((128 - len(row_list), rows), F32)], axis=0)
    table = jnp.transpose(table)
    return [table[:, i : i + 1] for i in range(len(row_list))]


def rows_of(columns):
    lane = lax.broadcasted_iota(jnp.int32, (columns[0].shape[0], 128), 1)
    wide = jnp.zeros(lane.shape, F32)
    for i, column in enumerate(columns):
        wide = jnp.where(lane == i, column, wide)
    return jnp.transpose(wide)[:8, :]


def hits(targets, shape):
    return lax.broadcasted_iota(jnp.int32, shape, 1) == targets[:, :1]


def fetch_kernel(place, weight, targets, scale, kept, mine, other, weights_of, mine_rows, other0, other1, other2, sent, sems):
    rows, width = other0.shape
    other_rows = (other0, other1, other2)
    copies = []
    for k in (3, 2, 1, 0):
        part = pl.ds(pl.multiple_of(place[k] * width, width), width)
        copies.append((k, pltpu.make_async_copy(weight.at[part], kept.at[part], sems.at[k])))
        copies[-1][1].start()
    lower = place[5] == 0
    halves = [(targets[:, :rows] - place[4]).astype(F32), (targets[:, rows:] - place[4]).astype(F32)]
    own = jnp.where(lower, halves[0], halves[1])
    theirs = jnp.where(lower, halves[1], halves[0])
    own, theirs = [column.astype(jnp.int32) for column in columns_of([own, theirs])]
    mine[...] = jnp.broadcast_to(own, mine.shape)
    other[...] = jnp.broadcast_to(theirs, other.shape)
    weights_of[...] = jnp.where(lower, scale[:, :rows], scale[:, rows:])
    entry = lax.broadcasted_iota(jnp.int32, (2 * rows, kept.shape[1]), 1)
    one_hot = (entry == jnp.concatenate([theirs, own], axis=0)).astype(F32).astype(BF16)
    for k, copy in copies:
        copy.wait()
        both = lax.dot_general(one_hot, block(kept, place, k, width), ROWS_BY_ROWS, preferred_element_type=F32)
        both = both.astype(BF16)
        if k == 3:
            sent[...] = both
        else:
            other_rows[k][...] = both[:rows]
            mine_rows[k] = both[rows:]


def stack_kernel(a, b, out):
    rows = a.shape[0]
    out[:rows] = a[...]
    out[rows:] = b[...]


def add_kernel(*refs):
    *ins, out = refs
    out[...] = sum((a[: out.shape[0]] for a in ins[1:]), ins[0][: out.shape[0]])


def softmax_part(acc, targets):
    hit = hits(targets, acc.shape)
    top = jnp.max(acc, axis=1, keepdims=True)
    shifted = jnp.exp(acc - top)
    total = jnp.sum(shifted, axis=1, keepdims=True)
    label = jnp.sum(jnp.where(hit, acc, 0.0), axis=1, keepdims=True)
    return rows_of([top, total, label]), jnp.where(hit, 0.0, shifted).astype(BF16)


def own_kernel(place, kept, targets, a, b, c, d, stats, sums):
    acc = 0
    for k, shard in enumerate((a, b, c, d)):
        acc += jnp.dot(shard[...], block(kept, place, k, shard.shape[1]), preferred_element_type=F32)
    stats[...], others = softmax_part(acc, targets)
    for k in range(sums.shape[0]):
        weights = block(kept, place, k, sums.shape[2])
        sums[k] = lax.dot_general(others, weights, ROWS_BY_ROWS, preferred_element_type=F32)


def start_kernel(place, kept, a, bc, out):
    rows, width = a.shape
    acc = jnp.dot(a[...], block(kept, place, 0, width), preferred_element_type=F32)
    acc += jnp.dot(bc[:rows], block(kept, place, 1, width), preferred_element_type=F32)
    acc += jnp.dot(bc[rows:], block(kept, place, 2, width), preferred_element_type=F32)
    out[...] = acc


def peer_kernel(place, kept, targets, partial, d, block0, block21, block3):
    rows, width = d.shape
    acc = partial[...] + jnp.dot(d[...], block(kept, place, 3, width), preferred_element_type=F32)
    stats, others = softmax_part(acc, targets)
    block3[rows:] = with_tail(stats, width)
    for k, out in ((3, block3.at[:rows]), (2, block21.at[:rows]), (1, block21.at[rows:]), (0, block0)):
        weights = block(kept, place, k, width)
        out[...] = lax.dot_general(others, weights, ROWS_BY_ROWS, preferred_element_type=F32).astype(BF16)


def join(a, b):
    top = jnp.maximum(a[0], b[0])
    return top, a[1] * jnp.exp(a[0] - top) + b[1] * jnp.exp(b[0] - top), a[2] + b[2]


def as_rows(a):
    return a[0:1], a[1:2], a[2:3]


def with_tail(stats, width):
    high = stats.astype(BF16)
    rest = stats - high.astype(F32)
    middle = rest.astype(BF16)
    low = (rest - middle.astype(F32)).astype(BF16)
    pad = jnp.zeros((8, width - stats.shape[1]), F32)
    terms = [jnp.concatenate([term.astype(F32), pad], axis=1) for term in (high, middle, low)]
    return jnp.concatenate(terms + [jnp.zeros_like(terms[0])], axis=0).astype(BF16)


def from_tail(ref, rows):
    tail = ref[rows:].astype(F32)[:, :rows]
    return tail[0:8] + tail[8:16] + tail[16:24]


def pair_kernel(own_stats, got, sums, pair, sent):
    rows = own_stats.shape[1]
    theirs = from_tail(got, rows)
    mine, theirs = as_rows(own_stats[...]), as_rows(theirs)
    both = join(mine, theirs)
    stats = jnp.concatenate(list(both) + [mine[0], theirs[0]] + [jnp.zeros((3, rows), F32)], axis=0)
    pair[...] = stats
    sent[rows:] = with_tail(stats, sent.shape[1])
    near, far = columns_of([jnp.exp(mine[0] - both[0]), jnp.exp(theirs[0] - both[0])])
    sent[:rows] = (near * sums[3] + far * got[:rows].astype(F32)).astype(BF16)


def join_kernel(pair, got, out):
    rows = pair.shape[1]
    near = as_rows(from_tail(got, rows))
    both = join(as_rows(pair[...]), near)
    out[...] = jnp.concatenate(list(both) + [near[0], jnp.zeros((4, rows), F32)], axis=0)


def block_sum(by, sums, got, picked, k):
    return by[0] * sums[k] + by[1] * got[...].astype(F32) + by[3] * picked[k].astype(F32)


def scale_kernel(scale, pair, half, far, sums, got, relayed, picked, near_picked, loss, columns, second, first):
    rows = first.shape[0]
    top, total, label = join(as_rows(half[...]), as_rows(far[...]))
    loss[...] = jnp.log(total) + top - label
    weighted = scale[...] / total
    factors = [weighted * jnp.exp(a - top) for a in (pair[3:4], pair[4:5], half[3:4])]
    missing = scale[...] * (jnp.exp(label - top) / total - 1.0)
    by = columns_of(factors + [missing])
    for i, column in enumerate(by):
        columns[i] = jnp.broadcast_to(column, columns.shape[1:])
    here = block_sum(by, sums, got.at[:rows], picked, 2)
    here += by[2] * relayed[:rows].astype(F32) + by[3] * near_picked[rows:].astype(F32)
    second[...] = here.astype(BF16)
    first[...] = block_sum(by, sums, got.at[rows:], picked, 1).astype(BF16)


def last_kernel(place, columns, sums, got, picked, theirs, first, second, loss, other_loss, out, row_loss):
    by = [columns[i][:, :1] for i in range(4)]
    here = block_sum(by, sums, got, picked, 0) + by[3] * theirs[...].astype(F32)
    out[...] = (here + first[...].astype(F32) + second[...].astype(F32)).astype(BF16)
    lower = place[5] == 0
    row_loss[: out.shape[0]] = jnp.where(lower, loss[...], other_loss[...])[0]
    row_loss[out.shape[0] :] = jnp.where(lower, other_loss[...], loss[...])[0]


def two_by_four(hidden, weight, targets, row_weight):
    tensors = lax.axis_size("tensor")
    px, tz = lax.axis_index("pipe"), lax.axis_index("tensor")
    rows, width = hidden.shape
    vocab_dev = weight.shape[1]

    def along(a, k):
        return lax.ppermute(a, "tensor", partners(tensors, k))

    def across(a):
        return lax.ppermute(a, "pipe", [(0, 1), (1, 0)])

    def after(a, b):
        return lax.optimization_barrier((a, b))[0]

    def call(kernel, outs, ins, *args, scratch=()):
        return pl.pallas_call(
            kernel,
            out_shape=outs,
            in_specs=ins,
            out_specs=jax.tree.map(lambda _: VMEM, outs),
            scratch_shapes=list(scratch),
            compiler_params=LIMIT,
        )(*args)

    def shape(*dims, dtype=F32):
        return jax.ShapeDtypeStruct(dims, dtype)

    place = [tz ^ k for k in range(tensors)] + [(px * tensors + tz) * vocab_dev, px]
    place = jnp.stack(place).astype(jnp.int32)
    piece = shape(rows, width, dtype=BF16)
    two = shape(2 * rows, width, dtype=BF16)
    tailed = shape(rows + 32, width, dtype=BF16)
    wide = shape(rows, 128, dtype=jnp.int32)

    z2 = along(hidden, 2)
    z1 = along(hidden, 1)
    x0 = across(hidden)
    kept, mine, other, scale, mine_rows, *other_rows, sent_rows = call(
        fetch_kernel,
        [pltpu.VMEM(weight.shape, BF16), wide, wide, shape(1, rows),
         shape(3, rows, width, dtype=BF16), piece, piece, piece, two],
        [SMEM, HBM, VMEM, VMEM],
        place, pltpu.with_memory_space_constraint(weight, pltpu.HBM), targets.reshape(1, -1), row_weight.reshape(1, -1),
        scratch=[pltpu.SemaphoreType.DMA((4,))],
    )
    z2 = after(z2, scale)
    z3 = along(z2, 1)
    x12 = across(call(stack_kernel, two, [VMEM] * 2, after(z1, x0), z2))
    x3 = across(z3)

    relayed_rows = along(after(sent_rows, z3), 1)

    own_stats, sums = call(
        own_kernel, [shape(8, rows), shape(tensors, rows, width)], [SMEM] + [VMEM] * 6,
        place, kept, mine, hidden, z1, z2, z3,
    )
    partial = call(start_kernel, shape(rows, vocab_dev), [SMEM] + [VMEM] * 3, place, kept, x0, x12)
    other = after(other, (own_stats, relayed_rows))
    block0, block21, block3 = call(
        peer_kernel, [piece, two, tailed], [SMEM] + [VMEM] * 4, place, kept, other, partial, x3
    )

    far_rows = along(call(add_kernel, piece, [VMEM] * 2, other_rows[2], relayed_rows), 2)
    near_rows = along(after(other_rows[1], partial), 1)
    got3 = across(block3)
    got21 = across(after(block21, got3))
    pair, relayed = call(pair_kernel, [shape(8, rows), tailed], [VMEM] * 3, after(own_stats, near_rows), got3, sums)
    relayed = along(relayed, 1)
    half = call(join_kernel, shape(8, rows), [VMEM] * 2, pair, relayed)
    far = along(half, 2)
    loss, columns, second, first = call(
        scale_kernel,
        [shape(1, rows), shape(4, rows, 128), piece, piece],
        [VMEM] * 9,
        scale, pair, half, after(far, far_rows), sums, got21, relayed, mine_rows, relayed_rows,
    )
    second = along(second, 2)
    got0 = across(block0)
    first = along(after(first, got0), 1)
    picked = call(add_kernel, piece, [VMEM] * 3, other_rows[0], near_rows, far_rows)
    picked = across(after(picked, got0))
    other_loss = across(after(loss, first))
    grad, row_loss = call(
        last_kernel, [piece, shape(2 * rows)], [SMEM] + [VMEM] * 9,
        place, columns, sums, got0, mine_rows, picked, first, second, loss, other_loss,
    )
    return grad, row_loss


def per_device(hidden, weight, targets, row_weight):
    if lax.axis_size("pipe") == 2 and lax.axis_size("tensor") == 4:
        return two_by_four(hidden, weight, targets, row_weight)
    return any_mesh(hidden, weight, targets, row_weight)


def solution(mesh):
    in_specs = (P(("dp", "pipe"), "tensor"), P(None, ("pipe", "tensor")), P("dp"), P("dp"))
    out_specs = (P(("dp", "pipe"), "tensor"), P("dp"))
    return jax.shard_map(
        per_device, mesh=mesh, in_specs=in_specs, out_specs=out_specs, check_vma=False
    )
```

time: 195 us -> 67.8 us (0.35)
  waiting for transfers between devices: 106 us -> 17.2 us
  blocking collectives: 59.6 us -> 0 us
  starting transfers between devices: 0.12 us -> 32.8 us
  Pallas kernels: 0 us -> 15.4 us
  between operations: 13.8 us -> 0.73 us
  matrix products: 11.8 us -> 0 us
  other arithmetic: 2.89 us -> 0 us
    reduce_scatter x2 -> x0, waiting for transfers between devices: 79 us -> none  [the longest x1 59.9 us: per_device(): lax.psum_scatter(partial_sum, 'tensor', scatter_dimension=1, tiled=True)]
    ppermute x0 -> x18, starting transfers between devices: none -> 32.8 us  [the longest x10 23.8 us: along(): return lax.ppermute(a, 'tensor', partners(tensors, k))]
    all_gather x1 -> x0, waiting for transfers between devices: 27 us -> none  [per_device(): lax.all_gather(features, 'pipe', axis=0, tiled=True)]
    all_gather x1 -> x0, blocking collectives: 21.8 us -> none  [per_device(): features = lax.all_gather(hidden, 'tensor', axis=1, tiled=True)]
    pmax x1 -> x0, blocking collectives: 20.5 us -> none  [per_device(): row_max = lax.pmax(local_max, ('pipe', 'tensor'))]
    psum x1 -> x0, blocking collectives: 17.2 us -> none  [per_device(): lax.psum((jnp.sum(shifted, axis=1), local_label), ('pipe', 'tensor'))]
    ppermute x0 -> x18, waiting for transfers between devices: none -> 17.2 us  [the longest x10 13.2 us: along(): return lax.ppermute(a, 'tensor', partners(tensors, k))]
    pallas_call x0 -> x11, Pallas kernels: none -> 15.4 us  [call(): pl.pallas_call(kernel, out_shape=outs, in_specs=ins, out_specs=jax.tree.m...]
  transfers between devices with their start and end apart: 3 -> 18, of which waited for: 3 -> 9; matrix products, arithmetic and copies ran while one was open for 0% -> 2% of each run, Pallas kernels for 0% -> 16%
where the time goes in v2:
time: 67.8 us; the launch traced here: 67.6 us
  starting transfers between devices  32.8 us (48%)
  waiting for transfers between devices  17.2 us (25%)
  Pallas kernels  15.4 us (23%)
  local copies, waits for them, and re-layouts  1.45 us (2%)
  between operations  0.73 us (1%)
    ppermute x10, starting transfers between devices, along(): return lax.ppermute(a, 'tensor', partners(tensors, k))  23.8 us
    pallas_call x11, Pallas kernels, call(): pl.pallas_call(kernel, out_shape=outs, in_specs=ins, out_specs=jax.tree.m...  15.4 us
    ppermute x10, waiting for transfers between devices, along(): return lax.ppermute(a, 'tensor', partners(tensors, k))  13.2 us
    ppermute x8, starting transfers between devices, across(): return lax.ppermute(a, 'pipe', [(0, 1), (1, 0)])  9.01 us
    ppermute x8, waiting for transfers between devices, across(): return lax.ppermute(a, 'pipe', [(0, 1), (1, 0)])  4 us
  transfers between devices with their start and end apart: 18, of which 9 were waited for; matrix products, arithmetic and copies ran while one was open for 2% of the time, Pallas kernels for 16%

profile of v2, /device:TPU:0, one launch (start us, length us, event | category | flops | bytes accessed | tf_op | source)
XLA Modules:
  0.0 67.6 jit_solution(9304099468014190003)
XLA Ops:
  0.6 0.0 copy-start
  0.6 4.1 %collective-permute-start.1 = (bf16[192,512]{1,0:T(8,128)(2,1)}, bf16[192,512]{1,0:T(8,128)(2,1)S(1)}, u32[]{:S(2)}, u32[]{:S(2)}) collective-permute-start(bf16[192,512]{1,0:T(8,128)(2,1)} %a.1), channel_id=1, source_target_pairs={{0,2},{1,3},{2,0},{3,1},{4,6},{5,7},{6,4},{7,5},{8,10},{9,11},{10,... | collective-permute-start | bytes 589832 | tf_op jit(solution)/shard_map/ppermute | solution.py:281
  4.7 1.6 %collective-permute-start = (bf16[192,512]{1,0:T(8,128)(2,1)}, bf16[192,512]{1,0:T(8,128)(2,1)S(1)}, u32[]{:S(2)}, u32[]{:S(2)}) collective-permute-start(bf16[192,512]{1,0:T(8,128)(2,1)} %a.1), channel_id=1, source_target_pairs={{0,1},{1,0},{2,3},{3,2},{4,5},{5,4},{6,7},{7,6},{8,9},{9,8},{10,11... | collective-permute-start | bytes 589832 | tf_op jit(solution)/shard_map/ppermute | solution.py:281
  6.3 1.5 %collective-permute-start.3 = (bf16[192,512]{1,0:T(8,128)(2,1)}, bf16[192,512]{1,0:T(8,128)(2,1)S(1)}, u32[]{:S(2)}, u32[]{:S(2)}) collective-permute-start(bf16[192,512]{1,0:T(8,128)(2,1)} %a.1), channel_id=1, source_target_pairs={{0,4},{4,0},{1,5},{5,1},{2,6},{6,2},{3,7},{7,3},{8,12},{12,8},{9,1... | collective-permute-start | bytes 589832 | tf_op jit(solution)/shard_map/ppermute | solution.py:284
  7.8 0.7 %reshape.10.targets = s32[1,384]{1,0:T(1,128)S(1)} reshape(s32[384]{0:T(512)} %param.6) | data formatting | bytes 3072 | tf_op jit(solution)/shard_map/reshape | solution.py:317
  8.5 0.7 %reshape.11.scale = f32[1,384]{1,0:T(1,128)S(1)} reshape(f32[384]{0:T(512)} %param.7) | data formatting | bytes 3072 | tf_op jit(solution)/shard_map/reshape | solution.py:317
  9.2 0.1 stack.27.place
  9.3 5.0 %shard_map.59 = (bf16[2048,1152]{1,0:T(8,128)(2,1)S(1)}, s32[192,128]{1,0:T(8,128)S(1)}, s32[192,128]{1,0:T(8,128)S(1)}, f32[1,192]{1,0:T(1,128)S(1)}, bf16[3,19...) custom-call(s32[6]{0:T(128)S(1)} %stack.27.place, ...), custom_call_target="tpu_custom_call" | custom-call | tf_op jit(solution)/shard_map/pallas_call | solution.py:290
  14.3 0.0 collective-permute-done.1.c.b
  14.3 0.6 collective-permute-start.2
  14.9 0.0 collective-permute-done.b.a
  14.9 0.0 collective-permute-done.3.a
  14.9 1.6 %collective-permute-start.4 = (bf16[384,512]{1,0:T(8,128)(2,1)S(1)}, bf16[384,512]{1,0:T(8,128)(2,1)S(1)}, u32[]{:S(2)}, u32[]{:S(2)}) collective-permute-start(bf16[384,512]{1,0:T(8,128)(2,1)S(1)} %shard_map.61), channel_id=1, source_target_pairs={{0,4},{4,0},{1,5},{5,1},{2,6},{6,2},{3,7},{7,3},{8,12},{12,8},{9,1... | collective-permute-start | bytes 1179656 | tf_op jit(solution)/shard_map/ppermute | solution.py:284
  16.5 3.7 %collective-permute-done.2.d = bf16[192,512]{1,0:T(8,128)(2,1)S(1)} collective-permute-done((bf16[192,512]{1,0:T(8,128)(2,1)S(1)}, bf16[192,512]{1,0:T(8,128)(2,1)S(1)}, u32[]{:S(2)}, u32[]{:S(2)}) %collective-permute-start.2) | collective-permute-done | bytes 196640 | tf_op jit(solution)/shard_map/ppermute | solution.py:281
  20.2 1.5 %collective-permute-start.6 = (bf16[384,512]{1,0:T(8,128)(2,1)S(1)}, bf16[384,512]{1,0:T(8,128)(2,1)S(1)}, u32[]{:S(2)}, u32[]{:S(2)}) collective-permute-start(bf16[384,512]{1,0:T(8,128)(2,1)S(1)} %get-tuple-element.44), channel_id=1, source_target_pairs={{0,1},{1,0},{2,3},{3,2},{4,5},{5,4},{6,7},{7,6},{8,9},{9,8},{10,11... | collective-permute-start | bytes 1179656 | tf_op jit(solution)/shard_map/ppermute | solution.py:281
  21.7 1.5 %collective-permute-start.7 = (bf16[192,512]{1,0:T(8,128)(2,1)S(1)}, bf16[192,512]{1,0:T(8,128)(2,1)S(1)}, u32[]{:S(2)}, u32[]{:S(2)}) collective-permute-start(bf16[192,512]{1,0:T(8,128)(2,1)S(1)} %collective-permute-done.2.d), channel_id=1, source_target_pairs={{0,4},{4,0},{1,5},{5,1},{2,6},{6,2},{3,7},{7,3},{8,12},{12,8},{9,1... | collective-permute-start | bytes 589832 | tf_op jit(solution)/shard_map/ppermute | solution.py:284
  23.2 0.0 copy-done
  23.2 3.6 %shard_map.60 = (f32[8,192]{1,0:T(8,128)S(1)}, f32[4,192,512]{2,1,0:T(8,128)S(1)}) custom-call(s32[6]{0:T(128)S(1)} %stack.27.place, bf16[2048,1152]{1,0:T(8,128)(2,1)S(1)} %get-tuple-element.34.kept, s32[192,128]{1,0:T(8,128)S(1)} %get-tuple-element.35.targets, bf16[192,512]{1,0:T(8,128)(2,1)S(1)} %copy-done, ...), custom_call_target="tpu_custom_call" | custom-call | tf_op jit(solution)/shard_map/pallas_call | solution.py:290
  26.8 0.2 collective-permute-done.4.bc
  27.0 1.5 %shard_map.62.partial = f32[192,1152]{1,0:T(8,128)S(1)} custom-call(s32[6]{0:T(128)S(1)} %stack.27.place, bf16[2048,1152]{1,0:T(8,128)(2,1)S(1)} %get-tuple-element.34.kept, bf16[192,512]{1,0:T(8,128)(2,1)S(1)} %collective-permute-done.3.a, bf16[384,512]{1,0:T(8,128)(2,1)S(1)} %collective-permute-done.4.bc), custom_call_target="tpu_custom_call" | custom-call | tf_op jit(solution)/shard_map/pallas_call | solution.py:290
  28.5 1.7 %collective-permute-done.6.refs_1_.near_picked = bf16[384,512]{1,0:T(8,128)(2,1)S(1)} collective-permute-done((bf16[384,512]{1,0:T(8,128)(2,1)S(1)}, bf16[384,512]{1,0:T(8,128)(2,1)S(1)}, u32[]{:S(2)}, u32[]{:S(2)}) %collective-permute-start.6) | collective-permute-done | bytes 393248 | tf_op jit(solution)/shard_map/ppermute | solution.py:281
  30.2 0.0 collective-permute-done.7.d
  30.2 2.9 %shard_map.63 = (bf16[192,512]{1,0:T(8,128)(2,1)S(1)}, bf16[384,512]{1,0:T(8,128)(2,1)S(1)}, bf16[224,512]{1,0:T(8,128)(2,1)S(1)}) custom-call(s32[6]{0:T(128)S(1)} %stack.27.place, bf16[2048,1152]{1,0:T(8,128)(2,1)S(1)} %get-tuple-element.34.kept, s32[192,128]{1,0:T(8,128)S(1)} %get-tuple-element.45.targets, f32[192,1152]{1,0:T(8,128)S(1)} %shard_map.62.partial, ...), custom_call_target="tpu_custom_call" | custom-call | tf_op jit(solution)/shard_map/pallas_call | solution.py:290
  33.1 1.6 %collective-permute-start.8 = (bf16[224,512]{1,0:T(8,128)(2,1)S(1)}, bf16[224,512]{1,0:T(8,128)(2,1)S(1)}, u32[]{:S(2)}, u32[]{:S(2)}) collective-permute-start(bf16[224,512]{1,0:T(8,128)(2,1)S(1)} %get-tuple-element.46), channel_id=1, source_target_pairs={{0,4},{4,0},{1,5},{5,1},{2,6},{6,2},{3,7},{7,3},{8,12},{12,8},{9,1... | collective-permute-start | bytes 688136 | tf_op jit(solution)/shard_map/ppermute | solution.py:284
  34.6 1.7 %collective-permute-start.5 = (bf16[192,512]{1,0:T(8,128)(2,1)S(1)}, bf16[192,512]{1,0:T(8,128)(2,1)S(1)}, u32[]{:S(2)}, u32[]{:S(2)}) collective-permute-start(bf16[192,512]{1,0:T(8,128)(2,1)S(1)} %get-tuple-element.40), channel_id=1, source_target_pairs={{0,1},{1,0},{2,3},{3,2},{4,5},{5,4},{6,7},{7,6},{8,9},{9,8},{10,11... | collective-permute-start | bytes 589832 | tf_op jit(solution)/shard_map/ppermute | solution.py:281
  36.4 2.9 %collective-permute-done.8.got = bf16[224,512]{1,0:T(8,128)(2,1)S(1)} collective-permute-done((bf16[224,512]{1,0:T(8,128)(2,1)S(1)}, bf16[224,512]{1,0:T(8,128)(2,1)S(1)}, u32[]{:S(2)}, u32[]{:S(2)}) %collective-permute-start.8) | collective-permute-done | bytes 229408 | tf_op jit(solution)/shard_map/ppermute | solution.py:284
  39.3 1.5 %collective-permute-start.12 = (bf16[384,512]{1,0:T(8,128)(2,1)S(1)}, bf16[384,512]{1,0:T(8,128)(2,1)S(1)}, u32[]{:S(2)}, u32[]{:S(2)}) collective-permute-start(bf16[384,512]{1,0:T(8,128)(2,1)S(1)} %get-tuple-element.53), channel_id=1, source_target_pairs={{0,4},{4,0},{1,5},{5,1},{2,6},{6,2},{3,7},{7,3},{8,12},{12,8},{9,1... | collective-permute-start | bytes 1179656 | tf_op jit(solution)/shard_map/ppermute | solution.py:284
  40.8 0.0 collective-permute-done.5.refs_1_
  40.8 0.3 shard_map.64
  41.1 1.9 %collective-permute-start.9 = (bf16[224,512]{1,0:T(8,128)(2,1)S(1)}, bf16[224,512]{1,0:T(8,128)(2,1)S(1)}, u32[]{:S(2)}, u32[]{:S(2)}) collective-permute-start(bf16[224,512]{1,0:T(8,128)(2,1)S(1)} %get-tuple-element.49), channel_id=1, source_target_pairs={{0,1},{1,0},{2,3},{3,2},{4,5},{5,4},{6,7},{7,6},{8,9},{9,8},{10,11... | collective-permute-start | bytes 688136 | tf_op jit(solution)/shard_map/ppermute | solution.py:281
  43.0 3.3 %collective-permute-start.11 = (bf16[192,512]{1,0:T(8,128)(2,1)S(1)}, bf16[192,512]{1,0:T(8,128)(2,1)S(1)}, u32[]{:S(2)}, u32[]{:S(2)}) collective-permute-start(bf16[192,512]{1,0:T(8,128)(2,1)S(1)} %shard_map.66), channel_id=1, source_target_pairs={{0,2},{1,3},{2,0},{3,1},{4,6},{5,7},{6,4},{7,5},{8,10},{9,11},{10,... | collective-permute-start | bytes 589832 | tf_op jit(solution)/shard_map/ppermute | solution.py:281
  46.4 0.5 collective-permute-start.13
  46.9 1.6 %collective-permute-done.9.got.relayed = bf16[224,512]{1,0:T(8,128)(2,1)S(1)} collective-permute-done((bf16[224,512]{1,0:T(8,128)(2,1)S(1)}, bf16[224,512]{1,0:T(8,128)(2,1)S(1)}, u32[]{:S(2)}, u32[]{:S(2)}) %collective-permute-start.9) | collective-permute-done | bytes 229408 | tf_op jit(solution)/shard_map/ppermute | solution.py:281
  48.5 3.5 %collective-permute-start.10 = (f32[8,192]{1,0:T(8,128)S(1)}, f32[8,192]{1,0:T(8,128)S(1)}, u32[]{:S(2)}, u32[]{:S(2)}) collective-permute-start(f32[8,192]{1,0:T(8,128)S(1)} %shard_map.65.half), channel_id=1, source_target_pairs={{0,2},{1,3},{2,0},{3,1},{4,6},{5,7},{6,4},{7,5},{8,10},{9,11},{10,... | collective-permute-start | bytes 18440 | tf_op jit(solution)/shard_map/ppermute | solution.py:281
  52.0 0.0 collective-permute-done.11.refs_2_
  52.0 1.7 %collective-permute-done.10.far = f32[8,192]{1,0:T(8,128)S(1)} collective-permute-done((f32[8,192]{1,0:T(8,128)S(1)}, f32[8,192]{1,0:T(8,128)S(1)}, u32[]{:S(2)}, u32[]{:S(2)}) %collective-permute-start.10) | collective-permute-done | bytes 6176 | tf_op jit(solution)/shard_map/ppermute | solution.py:281
  53.7 0.0 collective-permute-done.12.got
  53.7 0.5 shard_map.67
  54.2 0.0 collective-permute-done.13.got
  54.2 2.6 %collective-permute-start.15 = (bf16[192,512]{1,0:T(8,128)(2,1)S(1)}, bf16[192,512]{1,0:T(8,128)(2,1)S(1)}, u32[]{:S(2)}, u32[]{:S(2)}) collective-permute-start(bf16[192,512]{1,0:T(8,128)(2,1)S(1)} %get-tuple-element.60), channel_id=1, source_target_pairs={{0,1},{1,0},{2,3},{3,2},{4,5},{5,4},{6,7},{7,6},{8,9},{9,8},{10,11... | collective-permute-start | bytes 589832 | tf_op jit(solution)/shard_map/ppermute | solution.py:281
  56.9 0.5 collective-permute-start.14
  57.4 2.9 %collective-permute-start.16 = (bf16[192,512]{1,0:T(8,128)(2,1)S(1)}, bf16[192,512]{1,0:T(8,128)(2,1)S(1)}, u32[]{:S(2)}, u32[]{:S(2)}) collective-permute-start(bf16[192,512]{1,0:T(8,128)(2,1)S(1)} %get-tuple-element.61), channel_id=1, source_target_pairs={{0,2},{1,3},{2,0},{3,1},{4,6},{5,7},{6,4},{7,5},{8,10},{9,11},{10,... | collective-permute-start | bytes 589832 | tf_op jit(solution)/shard_map/ppermute | solution.py:281
  60.3 1.0 %collective-permute-done.15.first = bf16[192,512]{1,0:T(8,128)(2,1)S(1)} collective-permute-done((bf16[192,512]{1,0:T(8,128)(2,1)S(1)}, bf16[192,512]{1,0:T(8,128)(2,1)S(1)}, u32[]{:S(2)}, u32[]{:S(2)}) %collective-permute-start.15) | collective-permute-done | bytes 196640 | tf_op jit(solution)/shard_map/ppermute | solution.py:281
  61.4 0.4 collective-permute-start.17
  61.7 0.9 %collective-permute-done.14.theirs = bf16[192,512]{1,0:T(8,128)(2,1)S(1)} collective-permute-done((bf16[192,512]{1,0:T(8,128)(2,1)S(1)}, bf16[192,512]{1,0:T(8,128)(2,1)S(1)}, u32[]{:S(2)}, u32[]{:S(2)}) %collective-permute-start.14) | collective-permute-done | bytes 196640 | tf_op jit(solution)/shard_map/ppermute | solution.py:284
  62.6 3.5 %collective-permute-done.16.second = bf16[192,512]{1,0:T(8,128)(2,1)S(1)} collective-permute-done((bf16[192,512]{1,0:T(8,128)(2,1)S(1)}, bf16[192,512]{1,0:T(8,128)(2,1)S(1)}, u32[]{:S(2)}, u32[]{:S(2)}) %collective-permute-start.16) | collective-permute-done | bytes 196640 | tf_op jit(solution)/shard_map/ppermute | solution.py:281
  66.1 0.0 collective-permute-done.17.other_loss
  66.1 1.5 %shard_map.69 = (bf16[192,512]{1,0:T(8,128)(2,1)}, f32[384]{0:T(512)}) custom-call(s32[6]{0:T(128)S(1)} %stack.27.place, f32[4,192,128]{2,1,0:T(8,128)S(1)} %get-tuple-element.55.columns, f32[4,192,512]{2,1,0:T(8,128)S(1)} %get-tuple-element.47.sums, bf16[192,512]{1,0:T(8,128)(2,1)S(1)} %collective-permute-done.13.got, ...), custom_call_target="tpu_custom_call" | custom-call | tf_op jit(solution)/shard_map/pallas_call | solution.py:290
  (4 shorter events, 0.1 us)
Async XLA Ops:
  0.6 22.6 %copy-start = (bf16[192,512]{1,0:T(8,128)(2,1)S(1)}, bf16[192,512]{1,0:T(8,128)(2,1)}, u32[]{:S(2)}) copy-start(bf16[192,512]{1,0:T(8,128)(2,1)} %a.1) | copy-start | bytes 589828
  0.6 13.6 %collective-permute-start.1 = (bf16[192,512]{1,0:T(8,128)(2,1)}, bf16[192,512]{1,0:T(8,128)(2,1)S(1)}, u32[]{:S(2)}, u32[]{:S(2)}) collective-permute-start(bf16[192,512]{1,0:T(8,128)(2,1)} %a.1), channel_id=1, source_target_pairs={{0,2},{1,3},{2,0},{3,1},{4,6},{5,7},{6,4},{7,5},{8,10},{9,11},{10,... | collective-permute-start | bytes 589832 | tf_op jit(solution)/shard_map/ppermute | solution.py:281
  4.7 10.2 %collective-permute-start = (bf16[192,512]{1,0:T(8,128)(2,1)}, bf16[192,512]{1,0:T(8,128)(2,1)S(1)}, u32[]{:S(2)}, u32[]{:S(2)}) collective-permute-start(bf16[192,512]{1,0:T(8,128)(2,1)} %a.1), channel_id=1, source_target_pairs={{0,1},{1,0},{2,3},{3,2},{4,5},{5,4},{6,7},{7,6},{8,9},{9,8},{10,11... | collective-permute-start | bytes 589832 | tf_op jit(solution)/shard_map/ppermute | solution.py:281
  6.3 8.6 %collective-permute-start.3 = (bf16[192,512]{1,0:T(8,128)(2,1)}, bf16[192,512]{1,0:T(8,128)(2,1)S(1)}, u32[]{:S(2)}, u32[]{:S(2)}) collective-permute-start(bf16[192,512]{1,0:T(8,128)(2,1)} %a.1), channel_id=1, source_target_pairs={{0,4},{4,0},{1,5},{5,1},{2,6},{6,2},{3,7},{7,3},{8,12},{12,8},{9,1... | collective-permute-start | bytes 589832 | tf_op jit(solution)/shard_map/ppermute | solution.py:284
  14.3 5.9 %collective-permute-start.2 = (bf16[192,512]{1,0:T(8,128)(2,1)S(1)}, bf16[192,512]{1,0:T(8,128)(2,1)S(1)}, u32[]{:S(2)}, u32[]{:S(2)}) collective-permute-start(bf16[192,512]{1,0:T(8,128)(2,1)S(1)} %collective-permute-done.1.c.b), channel_id=1, source_target_pairs={{0,1},{1,0},{2,3},{3,2},{4,5},{5,4},{6,7},{7,6},{8,9},{9,8},{10,11... | collective-permute-start | bytes 589832 | tf_op jit(solution)/shard_map/ppermute | solution.py:281
  14.9 12.1 %collective-permute-start.4 = (bf16[384,512]{1,0:T(8,128)(2,1)S(1)}, bf16[384,512]{1,0:T(8,128)(2,1)S(1)}, u32[]{:S(2)}, u32[]{:S(2)}) collective-permute-start(bf16[384,512]{1,0:T(8,128)(2,1)S(1)} %shard_map.61), channel_id=1, source_target_pairs={{0,4},{4,0},{1,5},{5,1},{2,6},{6,2},{3,7},{7,3},{8,12},{12,8},{9,1... | collective-permute-start | bytes 1179656 | tf_op jit(solution)/shard_map/ppermute | solution.py:284
  20.2 10.0 %collective-permute-start.6 = (bf16[384,512]{1,0:T(8,128)(2,1)S(1)}, bf16[384,512]{1,0:T(8,128)(2,1)S(1)}, u32[]{:S(2)}, u32[]{:S(2)}) collective-permute-start(bf16[384,512]{1,0:T(8,128)(2,1)S(1)} %get-tuple-element.44), channel_id=1, source_target_pairs={{0,1},{1,0},{2,3},{3,2},{4,5},{5,4},{6,7},{7,6},{8,9},{9,8},{10,11... | collective-permute-start | bytes 1179656 | tf_op jit(solution)/shard_map/ppermute | solution.py:281
  21.7 8.5 %collective-permute-start.7 = (bf16[192,512]{1,0:T(8,128)(2,1)S(1)}, bf16[192,512]{1,0:T(8,128)(2,1)S(1)}, u32[]{:S(2)}, u32[]{:S(2)}) collective-permute-start(bf16[192,512]{1,0:T(8,128)(2,1)S(1)} %collective-permute-done.2.d), channel_id=1, source_target_pairs={{0,4},{4,0},{1,5},{5,1},{2,6},{6,2},{3,7},{7,3},{8,12},{12,8},{9,1... | collective-permute-start | bytes 589832 | tf_op jit(solution)/shard_map/ppermute | solution.py:284
  33.1 6.2 %collective-permute-start.8 = (bf16[224,512]{1,0:T(8,128)(2,1)S(1)}, bf16[224,512]{1,0:T(8,128)(2,1)S(1)}, u32[]{:S(2)}, u32[]{:S(2)}) collective-permute-start(bf16[224,512]{1,0:T(8,128)(2,1)S(1)} %get-tuple-element.46), channel_id=1, source_target_pairs={{0,4},{4,0},{1,5},{5,1},{2,6},{6,2},{3,7},{7,3},{8,12},{12,8},{9,1... | collective-permute-start | bytes 688136 | tf_op jit(solution)/shard_map/ppermute | solution.py:284
  34.6 6.2 %collective-permute-start.5 = (bf16[192,512]{1,0:T(8,128)(2,1)S(1)}, bf16[192,512]{1,0:T(8,128)(2,1)S(1)}, u32[]{:S(2)}, u32[]{:S(2)}) collective-permute-start(bf16[192,512]{1,0:T(8,128)(2,1)S(1)} %get-tuple-element.40), channel_id=1, source_target_pairs={{0,1},{1,0},{2,3},{3,2},{4,5},{5,4},{6,7},{7,6},{8,9},{9,8},{10,11... | collective-permute-start | bytes 589832 | tf_op jit(solution)/shard_map/ppermute | solution.py:281
  39.3 14.4 %collective-permute-start.12 = (bf16[384,512]{1,0:T(8,128)(2,1)S(1)}, bf16[384,512]{1,0:T(8,128)(2,1)S(1)}, u32[]{:S(2)}, u32[]{:S(2)}) collective-permute-start(bf16[384,512]{1,0:T(8,128)(2,1)S(1)} %get-tuple-element.53), channel_id=1, source_target_pairs={{0,4},{4,0},{1,5},{5,1},{2,6},{6,2},{3,7},{7,3},{8,12},{12,8},{9,1... | collective-permute-start | bytes 1179656 | tf_op jit(solution)/shard_map/ppermute | solution.py:284
  41.1 7.4 %collective-permute-start.9 = (bf16[224,512]{1,0:T(8,128)(2,1)S(1)}, bf16[224,512]{1,0:T(8,128)(2,1)S(1)}, u32[]{:S(2)}, u32[]{:S(2)}) collective-permute-start(bf16[224,512]{1,0:T(8,128)(2,1)S(1)} %get-tuple-element.49), channel_id=1, source_target_pairs={{0,1},{1,0},{2,3},{3,2},{4,5},{5,4},{6,7},{7,6},{8,9},{9,8},{10,11... | collective-permute-start | bytes 688136 | tf_op jit(solution)/shard_map/ppermute | solution.py:281
  43.0 8.9 %collective-permute-start.11 = (bf16[192,512]{1,0:T(8,128)(2,1)S(1)}, bf16[192,512]{1,0:T(8,128)(2,1)S(1)}, u32[]{:S(2)}, u32[]{:S(2)}) collective-permute-start(bf16[192,512]{1,0:T(8,128)(2,1)S(1)} %shard_map.66), channel_id=1, source_target_pairs={{0,2},{1,3},{2,0},{3,1},{4,6},{5,7},{6,4},{7,5},{8,10},{9,11},{10,... | collective-permute-start | bytes 589832 | tf_op jit(solution)/shard_map/ppermute | solution.py:281
  46.4 7.9 %collective-permute-start.13 = (bf16[192,512]{1,0:T(8,128)(2,1)S(1)}, bf16[192,512]{1,0:T(8,128)(2,1)S(1)}, u32[]{:S(2)}, u32[]{:S(2)}) collective-permute-start(bf16[192,512]{1,0:T(8,128)(2,1)S(1)} %get-tuple-element.56), channel_id=1, source_target_pairs={{0,4},{4,0},{1,5},{5,1},{2,6},{6,2},{3,7},{7,3},{8,12},{12,8},{9,1... | collective-permute-start | bytes 589832 | tf_op jit(solution)/shard_map/ppermute | solution.py:284
  48.5 5.2 %collective-permute-start.10 = (f32[8,192]{1,0:T(8,128)S(1)}, f32[8,192]{1,0:T(8,128)S(1)}, u32[]{:S(2)}, u32[]{:S(2)}) collective-permute-start(f32[8,192]{1,0:T(8,128)S(1)} %shard_map.65.half), channel_id=1, source_target_pairs={{0,2},{1,3},{2,0},{3,1},{4,6},{5,7},{6,4},{7,5},{8,10},{9,11},{10,... | collective-permute-start | bytes 18440 | tf_op jit(solution)/shard_map/ppermute | solution.py:281
  54.2 7.1 %collective-permute-start.15 = (bf16[192,512]{1,0:T(8,128)(2,1)S(1)}, bf16[192,512]{1,0:T(8,128)(2,1)S(1)}, u32[]{:S(2)}, u32[]{:S(2)}) collective-permute-start(bf16[192,512]{1,0:T(8,128)(2,1)S(1)} %get-tuple-element.60), channel_id=1, source_target_pairs={{0,1},{1,0},{2,3},{3,2},{4,5},{5,4},{6,7},{7,6},{8,9},{9,8},{10,11... | collective-permute-start | bytes 589832 | tf_op jit(solution)/shard_map/ppermute | solution.py:281
  56.9 5.7 %collective-permute-start.14 = (bf16[192,512]{1,0:T(8,128)(2,1)S(1)}, bf16[192,512]{1,0:T(8,128)(2,1)S(1)}, u32[]{:S(2)}, u32[]{:S(2)}) collective-permute-start(bf16[192,512]{1,0:T(8,128)(2,1)S(1)} %shard_map.68), channel_id=1, source_target_pairs={{0,4},{4,0},{1,5},{5,1},{2,6},{6,2},{3,7},{7,3},{8,12},{12,8},{9,1... | collective-permute-start | bytes 589832 | tf_op jit(solution)/shard_map/ppermute | solution.py:284
  57.4 8.7 %collective-permute-start.16 = (bf16[192,512]{1,0:T(8,128)(2,1)S(1)}, bf16[192,512]{1,0:T(8,128)(2,1)S(1)}, u32[]{:S(2)}, u32[]{:S(2)}) collective-permute-start(bf16[192,512]{1,0:T(8,128)(2,1)S(1)} %get-tuple-element.61), channel_id=1, source_target_pairs={{0,2},{1,3},{2,0},{3,1},{4,6},{5,7},{6,4},{7,5},{8,10},{9,11},{10,... | collective-permute-start | bytes 589832 | tf_op jit(solution)/shard_map/ppermute | solution.py:281
  61.4 4.7 %collective-permute-start.17 = (f32[1,192]{1,0:T(1,128)S(1)}, f32[1,192]{1,0:T(1,128)S(1)}, u32[]{:S(2)}, u32[]{:S(2)}) collective-permute-start(f32[1,192]{1,0:T(1,128)S(1)} %get-tuple-element.63.loss), channel_id=1, source_target_pairs={{0,4},{4,0},{1,5},{5,1},{2,6},{6,2},{3,7},{7,3},{8,12},{12,8},{9,1... | collective-permute-start | bytes 2312 | tf_op jit(solution)/shard_map/ppermute | solution.py:284

commit v3 on v2

--- a/solution.py
+++ b/solution.py
@@ -122,15 +122,24 @@
     return lax.broadcasted_iota(jnp.int32, shape, 1) == targets[:, :1]
 
 
-def fetch_kernel(place, weight, targets, scale, kept, mine, other, weights_of, mine_rows, other0, other1, other2, sent, sems):
-    rows, width = other0.shape
-    other_rows = (other0, other1, other2)
-    copies = []
-    for k in (3, 2, 1, 0):
-        part = pl.ds(pl.multiple_of(place[k] * width, width), width)
-        copies.append((k, pltpu.make_async_copy(weight.at[part], kept.at[part], sems.at[k])))
-        copies[-1][1].start()
+def fetch_kernel(place, weight, kept, sem):
+    @pl.when(place[6] == 0)
+    def _():
+        copy = pltpu.make_async_copy(weight, kept, sem)
+        copy.start()
+        copy.wait()
+
+
+def targets_kernel(place, weight, targets, scale, fetched, kept, mine, other, weights_of, sem):
+    copy = pltpu.make_async_copy(weight, kept, sem)
+
+    @pl.when(place[6] == 1)
+    def _():
+        copy.start()
+
+    rows = mine.shape[0]
     lower = place[5] == 0
+    targets, scale = targets[...].reshape(1, -1), scale[...].reshape(1, -1)
     halves = [(targets[:, :rows] - place[4]).astype(F32), (targets[:, rows:] - place[4]).astype(F32)]
     own = jnp.where(lower, halves[0], halves[1])
     theirs = jnp.where(lower, halves[1], halves[0])
@@ -138,10 +147,19 @@
     mine[...] = jnp.broadcast_to(own, mine.shape)
     other[...] = jnp.broadcast_to(theirs, other.shape)
     weights_of[...] = jnp.where(lower, scale[:, :rows], scale[:, rows:])
+
+    @pl.when(place[6] == 1)
+    def _():
+        copy.wait()
+
+
+def pick_kernel(place, kept, mine, other, mine_rows, other0, other1, other2, sent):
+    rows, width = other0.shape
+    other_rows = (other0, other1, other2)
+    column = jnp.concatenate([other[:, :1], mine[:, :1]], axis=0)
     entry = lax.broadcasted_iota(jnp.int32, (2 * rows, kept.shape[1]), 1)
-    one_hot = (entry == jnp.concatenate([theirs, own], axis=0)).astype(F32).astype(BF16)
-    for k, copy in copies:
-        copy.wait()
+    one_hot = (entry == column).astype(F32).astype(BF16)
+    for k in (3, 2, 1, 0):
         both = lax.dot_general(one_hot, block(kept, place, k, width), ROWS_BY_ROWS, preferred_element_type=F32)
         both = both.astype(BF16)
         if k == 3:
@@ -157,9 +175,14 @@
     out[rows:] = b[...]
 
 
-def add_kernel(*refs):
-    *ins, out = refs
-    out[...] = sum((a[: out.shape[0]] for a in ins[1:]), ins[0][: out.shape[0]])
+def add_kernel(a, b, out):
+    rows = a.shape[0]
+    out[:rows] = a[...] + b[:rows]
+    out[rows:] = jnp.zeros((out.shape[0] - rows, out.shape[1]), BF16)
+
+
+def last_rows_kernel(a, b, c, out):
+    out[...] = a[...] + b[...] + c[: out.shape[0]]
 
 
 def softmax_part(acc, targets):
@@ -193,7 +216,7 @@
     rows, width = d.shape
     acc = partial[...] + jnp.dot(d[...], block(kept, place, 3, width), preferred_element_type=F32)
     stats, others = softmax_part(acc, targets)
-    block3[rows:] = with_tail(stats, width)
+    block3[rows:] = with_tail(as_rows(stats), width)
     for k, out in ((3, block3.at[:rows]), (2, block21.at[:rows]), (1, block21.at[rows:]), (0, block0)):
         weights = block(kept, place, k, width)
         out[...] = lax.dot_general(others, weights, ROWS_BY_ROWS, preferred_element_type=F32).astype(BF16)
@@ -209,35 +232,34 @@
 
 
 def with_tail(stats, width):
-    high = stats.astype(BF16)
-    rest = stats - high.astype(F32)
-    middle = rest.astype(BF16)
-    low = (rest - middle.astype(F32)).astype(BF16)
-    pad = jnp.zeros((8, width - stats.shape[1]), F32)
-    terms = [jnp.concatenate([term.astype(F32), pad], axis=1) for term in (high, middle, low)]
-    return jnp.concatenate(terms + [jnp.zeros_like(terms[0])], axis=0).astype(BF16)
+    high = [row.astype(BF16).astype(F32) for row in stats]
+    rest = [row - term for row, term in zip(stats, high)]
+    middle = [row.astype(BF16).astype(F32) for row in rest]
+    low = [row - term for row, term in zip(rest, middle)]
+    rows = jnp.concatenate(high + middle + low + [jnp.zeros((7, stats[0].shape[1]), F32)], axis=0)
+    return jnp.concatenate([rows, jnp.zeros((16, width - rows.shape[1]), F32)], axis=1).astype(BF16)
 
 
 def from_tail(ref, rows):
     tail = ref[rows:].astype(F32)[:, :rows]
-    return tail[0:8] + tail[8:16] + tail[16:24]
+    return [tail[i : i + 1] + tail[i + 3 : i + 4] + tail[i + 6 : i + 7] for i in range(3)]
 
 
 def pair_kernel(own_stats, got, sums, pair, sent):
     rows = own_stats.shape[1]
     theirs = from_tail(got, rows)
-    mine, theirs = as_rows(own_stats[...]), as_rows(theirs)
+    mine = as_rows(own_stats[...])
     both = join(mine, theirs)
     stats = jnp.concatenate(list(both) + [mine[0], theirs[0]] + [jnp.zeros((3, rows), F32)], axis=0)
     pair[...] = stats
-    sent[rows:] = with_tail(stats, sent.shape[1])
+    sent[rows:] = with_tail(both, sent.shape[1])
     near, far = columns_of([jnp.exp(mine[0] - both[0]), jnp.exp(theirs[0] - both[0])])
     sent[:rows] = (near * sums[3] + far * got[:rows].astype(F32)).astype(BF16)
 
 
 def join_kernel(pair, got, out):
     rows = pair.shape[1]
-    near = as_rows(from_tail(got, rows))
+    near = from_tail(got, rows)
     both = join(as_rows(pair[...]), near)
     out[...] = jnp.concatenate(list(both) + [near[0], jnp.zeros((4, rows), F32)], axis=0)
 
@@ -262,10 +284,14 @@
     first[...] = block_sum(by, sums, got.at[rows:], picked, 1).astype(BF16)
 
 
-def last_kernel(place, columns, sums, got, picked, theirs, first, second, loss, other_loss, out, row_loss):
+def second_kernel(columns, sums, got, picked, second, out):
     by = [columns[i][:, :1] for i in range(4)]
-    here = block_sum(by, sums, got, picked, 0) + by[3] * theirs[...].astype(F32)
-    out[...] = (here + first[...].astype(F32) + second[...].astype(F32)).astype(BF16)
+    out[...] = block_sum(by, sums, got, picked, 0) + second[...].astype(F32)
+
+
+def last_kernel(place, columns, partial, first, theirs, loss, other_loss, out, row_loss):
+    here = partial[...] + first[...].astype(F32) + columns[3][:, :1] * theirs[...].astype(F32)
+    out[...] = here.astype(BF16)
     lower = place[5] == 0
     row_loss[: out.shape[0]] = jnp.where(lower, loss[...], other_loss[...])[0]
     row_loss[out.shape[0] :] = jnp.where(lower, other_loss[...], loss[...])[0]
@@ -286,41 +312,48 @@
     def after(a, b):
         return lax.optimization_barrier((a, b))[0]
 
-    def call(kernel, outs, ins, *args, scratch=()):
+    def call(kernel, outs, ins, *args, scratch=(), aliases=None):
         return pl.pallas_call(
             kernel,
             out_shape=outs,
             in_specs=ins,
             out_specs=jax.tree.map(lambda _: VMEM, outs),
             scratch_shapes=list(scratch),
+            input_output_aliases=aliases or {},
             compiler_params=LIMIT,
         )(*args)
 
     def shape(*dims, dtype=F32):
         return jax.ShapeDtypeStruct(dims, dtype)
 
-    place = [tz ^ k for k in range(tensors)] + [(px * tensors + tz) * vocab_dev, px]
+    place = [tz ^ k for k in range(tensors)] + [(px * tensors + tz) * vocab_dev, px, lax.axis_index("dp") % 2]
     place = jnp.stack(place).astype(jnp.int32)
     piece = shape(rows, width, dtype=BF16)
     two = shape(2 * rows, width, dtype=BF16)
-    tailed = shape(rows + 32, width, dtype=BF16)
+    tailed = shape(rows + 16, width, dtype=BF16)
     wide = shape(rows, 128, dtype=jnp.int32)
 
+    weight = pltpu.with_memory_space_constraint(weight, pltpu.HBM)
+    dma = [pltpu.SemaphoreType.DMA]
+    kept = call(fetch_kernel, pltpu.VMEM(weight.shape, BF16), [SMEM, HBM], place, weight, scratch=dma)
+    hidden = after(hidden, kept)
     z2 = along(hidden, 2)
     z1 = along(hidden, 1)
     x0 = across(hidden)
-    kept, mine, other, scale, mine_rows, *other_rows, sent_rows = call(
-        fetch_kernel,
-        [pltpu.VMEM(weight.shape, BF16), wide, wide, shape(1, rows),
-         shape(3, rows, width, dtype=BF16), piece, piece, piece, two],
-        [SMEM, HBM, VMEM, VMEM],
-        place, pltpu.with_memory_space_constraint(weight, pltpu.HBM), targets.reshape(1, -1), row_weight.reshape(1, -1),
-        scratch=[pltpu.SemaphoreType.DMA((4,))],
+    kept, mine, other, scale = call(
+        targets_kernel,
+        [pltpu.VMEM(weight.shape, BF16), wide, wide, shape(1, rows)],
+        [SMEM, HBM, VMEM, VMEM, VMEM],
+        place, weight, targets, row_weight, kept, scratch=dma, aliases={4: 0},
     )
     z2 = after(z2, scale)
     z3 = along(z2, 1)
     x12 = across(call(stack_kernel, two, [VMEM] * 2, after(z1, x0), z2))
-    x3 = across(z3)
+    mine_rows, *other_rows, sent_rows = call(
+        pick_kernel, [shape(3, rows, width, dtype=BF16), piece, piece, piece, two], [SMEM] + [VMEM] * 3,
+        after(place, z2), kept, mine, other,
+    )
+    x3 = across(after(z3, sent_rows))
 
     relayed_rows = along(after(sent_rows, z3), 1)
 
@@ -333,30 +366,29 @@
     block0, block21, block3 = call(
         peer_kernel, [piece, two, tailed], [SMEM] + [VMEM] * 4, place, kept, other, partial, x3
     )
-
-    far_rows = along(call(add_kernel, piece, [VMEM] * 2, other_rows[2], relayed_rows), 2)
-    near_rows = along(after(other_rows[1], partial), 1)
+    far_rows = along(call(add_kernel, shape(rows + 32, width, dtype=BF16), [VMEM] * 2, other_rows[2], relayed_rows), 2)
     got3 = across(block3)
-    got21 = across(after(block21, got3))
-    pair, relayed = call(pair_kernel, [shape(8, rows), tailed], [VMEM] * 3, after(own_stats, near_rows), got3, sums)
+    pair, relayed = call(pair_kernel, [shape(8, rows), tailed], [VMEM] * 3, own_stats, got3, sums)
     relayed = along(relayed, 1)
-    half = call(join_kernel, shape(8, rows), [VMEM] * 2, pair, relayed)
+    got21 = across(after(block21, pair))
+    half = call(join_kernel, shape(8, rows), [VMEM] * 2, pair, after(relayed, far_rows))
     far = along(half, 2)
+    near_rows = along(after(other_rows[1], half), 1)
     loss, columns, second, first = call(
         scale_kernel,
         [shape(1, rows), shape(4, rows, 128), piece, piece],
         [VMEM] * 9,
-        scale, pair, half, after(far, far_rows), sums, got21, relayed, mine_rows, relayed_rows,
+        scale, pair, half, far, sums, got21, relayed, mine_rows, relayed_rows,
     )
     second = along(second, 2)
     got0 = across(block0)
-    first = along(after(first, got0), 1)
-    picked = call(add_kernel, piece, [VMEM] * 3, other_rows[0], near_rows, far_rows)
-    picked = across(after(picked, got0))
-    other_loss = across(after(loss, first))
+    picked = across(call(last_rows_kernel, piece, [VMEM] * 3, other_rows[0], near_rows, far_rows))
+    first = along(first, 1)
+    other_loss = across(loss)
+    partial = call(second_kernel, shape(rows, width), [VMEM] * 5, columns, sums, got0, mine_rows, second)
     grad, row_loss = call(
-        last_kernel, [piece, shape(2 * rows)], [SMEM] + [VMEM] * 9,
-        place, columns, sums, got0, mine_rows, picked, first, second, loss, other_loss,
+        last_kernel, [piece, shape(2 * rows)], [SMEM] + [VMEM] * 6,
+        place, columns, partial, first, picked, loss, other_loss,
     )
     return grad, row_loss
 

time: 67.8 us -> 64.4 us (0.950)
  starting transfers between devices: 32.8 us -> 26.8 us
  waiting for transfers between devices: 17.2 us -> 19.6 us
  Pallas kernels: 15.4 us -> 17 us
  local copies, waits for them, and re-layouts: 1.45 us -> 0.1 us
    ppermute x10, starting transfers between devices: 23.8 us -> 15.7 us  [along(): return lax.ppermute(a, 'tensor', partners(tensors, k))]
    ppermute x10, waiting for transfers between devices: 13.2 us -> 17.4 us  [along(): return lax.ppermute(a, 'tensor', partners(tensors, k))]
    ppermute x8, starting transfers between devices: 9.01 us -> 11.2 us  [across(): return lax.ppermute(a, 'pipe', [(0, 1), (1, 0)])]
    ppermute x8, waiting for transfers between devices: 4 us -> 2.21 us  [across(): return lax.ppermute(a, 'pipe', [(0, 1), (1, 0)])]
    pallas_call x11 -> x14, Pallas kernels: 15.4 us -> 17 us  [call(): pl.pallas_call(kernel, out_shape=outs, in_specs=ins, out_specs=jax.tree.m...]
    reshape x2 -> x0, local copies, waits for them, and re-layouts: 1.37 us -> none  [the longest x1 0.68 us: two_by_four(): targets.reshape(1, -1)]
  transfers between devices with their start and end apart: 18 -> 18, of which waited for: 9 -> 12; matrix products, arithmetic and copies ran while one was open for 2% -> 0% of each run, Pallas kernels for 16% -> 15%
where the time goes in v3:
time: 64.4 us; the launch traced here: 64.3 us
  starting transfers between devices  26.8 us (42%)
  waiting for transfers between devices  19.6 us (30%)
  Pallas kernels  17 us (26%)
  between operations  0.77 us (1%)
    ppermute x10, waiting for transfers between devices, along(): return lax.ppermute(a, 'tensor', partners(tensors, k))  17.4 us
    pallas_call x14, Pallas kernels, call(): pl.pallas_call(kernel, out_shape=outs, in_specs=ins, out_specs=jax.tree.m...  17 us
    ppermute x10, starting transfers between devices, along(): return lax.ppermute(a, 'tensor', partners(tensors, k))  15.7 us
    ppermute x8, starting transfers between devices, across(): return lax.ppermute(a, 'pipe', [(0, 1), (1, 0)])  11.2 us
    ppermute x8, waiting for transfers between devices, across(): return lax.ppermute(a, 'pipe', [(0, 1), (1, 0)])  2.21 us
  transfers between devices with their start and end apart: 18, of which 12 were waited for; matrix products, arithmetic and copies ran while one was open for 0% of the time, Pallas kernels for 15%

profile of v3, /device:TPU:0, one launch (start us, length us, event | category | flops | bytes accessed | tf_op | source)
XLA Modules:
  0.0 64.3 jit_solution(17794128373814252599)
XLA Ops:
  0.6 0.1 stack.31.place
  0.7 0.0 copy-start.2
  0.7 2.9 %shard_map.59.fetched = bf16[2048,1152]{1,0:T(8,128)(2,1)S(1)} custom-call(s32[7]{0:T(128)S(1)} %stack.31.place, bf16[2048,1152]{1,0:T(8,128)(2,1)} %weight.3), custom_call_target="tpu_custom_call" | custom-call | tf_op jit(solution)/shard_map/pallas_call | solution.py:316
  3.7 4.1 %collective-permute-start.1 = (bf16[192,512]{1,0:T(8,128)(2,1)S(1)}, bf16[192,512]{1,0:T(8,128)(2,1)S(1)}, u32[]{:S(2)}, u32[]{:S(2)}) collective-permute-start(bf16[192,512]{1,0:T(8,128)(2,1)S(1)} %copy-done), channel_id=1, source_target_pairs={{0,2},{1,3},{2,0},{3,1},{4,6},{5,7},{6,4},{7,5},{8,10},{9,11},{10,... | collective-permute-start | bytes 589832 | tf_op jit(solution)/shard_map/ppermute | solution.py:307
  7.8 1.6 %collective-permute-start = (bf16[192,512]{1,0:T(8,128)(2,1)S(1)}, bf16[192,512]{1,0:T(8,128)(2,1)S(1)}, u32[]{:S(2)}, u32[]{:S(2)}) collective-permute-start(bf16[192,512]{1,0:T(8,128)(2,1)S(1)} %copy-done), channel_id=1, source_target_pairs={{0,1},{1,0},{2,3},{3,2},{4,5},{5,4},{6,7},{7,6},{8,9},{9,8},{10,11... | collective-permute-start | bytes 589832 | tf_op jit(solution)/shard_map/ppermute | solution.py:307
  9.3 1.5 %collective-permute-start.4 = (bf16[192,512]{1,0:T(8,128)(2,1)S(1)}, bf16[192,512]{1,0:T(8,128)(2,1)S(1)}, u32[]{:S(2)}, u32[]{:S(2)}) collective-permute-start(bf16[192,512]{1,0:T(8,128)(2,1)S(1)} %copy-done), channel_id=1, source_target_pairs={{0,4},{4,0},{1,5},{5,1},{2,6},{6,2},{3,7},{7,3},{8,12},{12,8},{9,1... | collective-permute-start | bytes 589832 | tf_op jit(solution)/shard_map/ppermute | solution.py:310
  10.8 0.8 %shard_map.60 = (bf16[2048,1152]{1,0:T(8,128)(2,1)S(1)}, s32[192,128]{1,0:T(8,128)S(1)}, s32[192,128]{1,0:T(8,128)S(1)}, f32[1,192]{1,0:T(1,128)S(1)}) custom-call(s32[7]{0:T(128)S(1)} %stack.31.place, bf16[2048,1152]{1,0:T(8,128)(2,1)} %weight.3, s32[384]{0:T(512)S(1)} %copy-done.1, f32[384]{0:T(512)S(1)} %copy-done.2, ...), custom_call_target="tpu_custom_call", output_to_operand_aliasing={{0}: (4, {})} | custom-call | tf_op jit(solution)/shard_map/pallas_call | solution.py:316
  11.7 3.3 %collective-permute-done.1.c.b = bf16[192,512]{1,0:T(8,128)(2,1)S(1)} collective-permute-done((bf16[192,512]{1,0:T(8,128)(2,1)S(1)}, bf16[192,512]{1,0:T(8,128)(2,1)S(1)}, u32[]{:S(2)}, u32[]{:S(2)}) %collective-permute-start.1) | collective-permute-done | bytes 196640 | tf_op jit(solution)/shard_map/ppermute | solution.py:307
  15.0 0.6 collective-permute-start.2
  15.5 0.0 collective-permute-done.b.a
  15.5 0.0 collective-permute-done.4.a
  15.6 1.6 %collective-permute-start.5 = (bf16[384,512]{1,0:T(8,128)(2,1)S(1)}, bf16[384,512]{1,0:T(8,128)(2,1)S(1)}, u32[]{:S(2)}, u32[]{:S(2)}) collective-permute-start(bf16[384,512]{1,0:T(8,128)(2,1)S(1)} %shard_map.63), channel_id=1, source_target_pairs={{0,4},{4,0},{1,5},{5,1},{2,6},{6,2},{3,7},{7,3},{8,12},{12,8},{9,1... | collective-permute-start | bytes 1179656 | tf_op jit(solution)/shard_map/ppermute | solution.py:310
  17.1 2.8 %shard_map.62 = (bf16[3,192,512]{2,1,0:T(8,128)(2,1)S(1)}, bf16[192,512]{1,0:T(8,128)(2,1)S(1)}, bf16[192,512]{1,0:T(8,128)(2,1)S(1)}, bf16[192,512]{1,0:T(8,128)(2,1)S(1)}, bf16[384,512]{1,0:T(8,128)(2,1)S(1)}) custom-call(s32[7]{0:T(128)S(1)} %stack.31.place, bf16[2048,1152]{1,0:T(8,128)(2,1)S(1)} %get-tuple-element.33.kept, ...), custom_call_target="tpu_custom_call" | custom-call | tf_op jit(solution)/shard_map/pallas_call | solution.py:316
  19.9 0.7 %collective-permute-done.2.d = bf16[192,512]{1,0:T(8,128)(2,1)S(1)} collective-permute-done((bf16[192,512]{1,0:T(8,128)(2,1)S(1)}, bf16[192,512]{1,0:T(8,128)(2,1)S(1)}, u32[]{:S(2)}, u32[]{:S(2)}) %collective-permute-start.2) | collective-permute-done | bytes 196640 | tf_op jit(solution)/shard_map/ppermute | solution.py:307
  20.6 0.9 %collective-permute-start.3 = (bf16[384,512]{1,0:T(8,128)(2,1)S(1)}, bf16[384,512]{1,0:T(8,128)(2,1)S(1)}, u32[]{:S(2)}, u32[]{:S(2)}) collective-permute-start(bf16[384,512]{1,0:T(8,128)(2,1)S(1)} %get-tuple-element.41), channel_id=1, source_target_pairs={{0,1},{1,0},{2,3},{3,2},{4,5},{5,4},{6,7},{7,6},{8,9},{9,8},{10,11... | collective-permute-start | bytes 1179656 | tf_op jit(solution)/shard_map/ppermute | solution.py:307
  21.5 1.5 %collective-permute-start.6 = (bf16[192,512]{1,0:T(8,128)(2,1)S(1)}, bf16[192,512]{1,0:T(8,128)(2,1)S(1)}, u32[]{:S(2)}, u32[]{:S(2)}) collective-permute-start(bf16[192,512]{1,0:T(8,128)(2,1)S(1)} %collective-permute-done.2.d), channel_id=1, source_target_pairs={{0,4},{4,0},{1,5},{5,1},{2,6},{6,2},{3,7},{7,3},{8,12},{12,8},{9,1... | collective-permute-start | bytes 589832 | tf_op jit(solution)/shard_map/ppermute | solution.py:310
  23.0 3.6 %shard_map.61 = (f32[8,192]{1,0:T(8,128)S(1)}, f32[4,192,512]{2,1,0:T(8,128)S(1)}) custom-call(s32[7]{0:T(128)S(1)} %stack.31.place, bf16[2048,1152]{1,0:T(8,128)(2,1)S(1)} %get-tuple-element.33.kept, s32[192,128]{1,0:T(8,128)S(1)} %get-tuple-element.34.targets.mine, bf16[192,512]{1,0:T(8,128)(2,1)S(1)} %copy-done, ...), custom_call_target="tpu_custom_call" | custom-call | tf_op jit(solution)/shard_map/pallas_call | solution.py:316
  26.6 0.6 collective-permute-done.5.bc
  27.2 1.5 %shard_map.64.partial = f32[192,1152]{1,0:T(8,128)S(1)} custom-call(s32[7]{0:T(128)S(1)} %stack.31.place, bf16[2048,1152]{1,0:T(8,128)(2,1)S(1)} %get-tuple-element.33.kept, bf16[192,512]{1,0:T(8,128)(2,1)S(1)} %collective-permute-done.4.a, bf16[384,512]{1,0:T(8,128)(2,1)S(1)} %collective-permute-done.5.bc), custom_call_target="tpu_custom_call" | custom-call | tf_op jit(solution)/shard_map/pallas_call | solution.py:316
  28.7 0.5 collective-permute-done.3.b.near_picked
  29.2 0.1 collective-permute-done.6.d
  29.3 2.9 %shard_map.65 = (bf16[192,512]{1,0:T(8,128)(2,1)S(1)}, bf16[384,512]{1,0:T(8,128)(2,1)S(1)}, bf16[208,512]{1,0:T(8,128)(2,1)S(1)}) custom-call(s32[7]{0:T(128)S(1)} %stack.31.place, bf16[2048,1152]{1,0:T(8,128)(2,1)S(1)} %get-tuple-element.33.kept, s32[192,128]{1,0:T(8,128)S(1)} %get-tuple-element.42.other.targets, f32[192,1152]{1,0:T(8,128)S(1)} %shard_map.64.partial, ...), custom_call_target="tpu_custom_call" | custom-call | tf_op jit(solution)/shard_map/pallas_call | solution.py:316
  32.2 1.6 %collective-permute-start.7 = (bf16[208,512]{1,0:T(8,128)(2,1)S(1)}, bf16[208,512]{1,0:T(8,128)(2,1)S(1)}, u32[]{:S(2)}, u32[]{:S(2)}) collective-permute-start(bf16[208,512]{1,0:T(8,128)(2,1)S(1)} %get-tuple-element.45), channel_id=1, source_target_pairs={{0,4},{4,0},{1,5},{5,1},{2,6},{6,2},{3,7},{7,3},{8,12},{12,8},{9,1... | collective-permute-start | bytes 638984 | tf_op jit(solution)/shard_map/ppermute | solution.py:310
  33.8 3.6 %collective-permute-start.9 = (bf16[224,512]{1,0:T(8,128)(2,1)S(1)}, bf16[224,512]{1,0:T(8,128)(2,1)S(1)}, u32[]{:S(2)}, u32[]{:S(2)}) collective-permute-start(bf16[224,512]{1,0:T(8,128)(2,1)S(1)} %shard_map.67), channel_id=1, source_target_pairs={{0,2},{1,3},{2,0},{3,1},{4,6},{5,7},{6,4},{7,5},{8,10},{9,11},{10,... | collective-permute-start | bytes 688136 | tf_op jit(solution)/shard_map/ppermute | solution.py:307
  37.4 1.1 %collective-permute-done.7.got = bf16[208,512]{1,0:T(8,128)(2,1)S(1)} collective-permute-done((bf16[208,512]{1,0:T(8,128)(2,1)S(1)}, bf16[208,512]{1,0:T(8,128)(2,1)S(1)}, u32[]{:S(2)}, u32[]{:S(2)}) %collective-permute-start.7) | collective-permute-done | bytes 213024 | tf_op jit(solution)/shard_map/ppermute | solution.py:310
  38.5 0.3 shard_map.66
  38.7 0.6 collective-permute-start.8
  39.3 1.2 %collective-permute-start.11 = (bf16[384,512]{1,0:T(8,128)(2,1)S(1)}, bf16[384,512]{1,0:T(8,128)(2,1)S(1)}, u32[]{:S(2)}, u32[]{:S(2)}) collective-permute-start(bf16[384,512]{1,0:T(8,128)(2,1)S(1)} %get-tuple-element.52), channel_id=1, source_target_pairs={{0,4},{4,0},{1,5},{5,1},{2,6},{6,2},{3,7},{7,3},{8,12},{12,8},{9,1... | collective-permute-start | bytes 1179656 | tf_op jit(solution)/shard_map/ppermute | solution.py:310
  40.6 5.0 %collective-permute-done.9.c = bf16[224,512]{1,0:T(8,128)(2,1)S(1)} collective-permute-done((bf16[224,512]{1,0:T(8,128)(2,1)S(1)}, bf16[224,512]{1,0:T(8,128)(2,1)S(1)}, u32[]{:S(2)}, u32[]{:S(2)}) %collective-permute-start.9) | collective-permute-done | bytes 229408 | tf_op jit(solution)/shard_map/ppermute | solution.py:307
  45.6 2.4 %collective-permute-done.8.got.relayed = bf16[208,512]{1,0:T(8,128)(2,1)S(1)} collective-permute-done((bf16[208,512]{1,0:T(8,128)(2,1)S(1)}, bf16[208,512]{1,0:T(8,128)(2,1)S(1)}, u32[]{:S(2)}, u32[]{:S(2)}) %collective-permute-start.8) | collective-permute-done | bytes 213024 | tf_op jit(solution)/shard_map/ppermute | solution.py:307
  48.0 0.1 collective-permute-start.15
  48.1 2.1 %collective-permute-start.10 = (f32[8,192]{1,0:T(8,128)S(1)}, f32[8,192]{1,0:T(8,128)S(1)}, u32[]{:S(2)}, u32[]{:S(2)}) collective-permute-start(f32[8,192]{1,0:T(8,128)S(1)} %shard_map.68.half), channel_id=1, source_target_pairs={{0,2},{1,3},{2,0},{3,1},{4,6},{5,7},{6,4},{7,5},{8,10},{9,11},{10,... | collective-permute-start | bytes 18440 | tf_op jit(solution)/shard_map/ppermute | solution.py:307
  50.3 1.7 %collective-permute-start.12 = (bf16[192,512]{1,0:T(8,128)(2,1)S(1)}, bf16[192,512]{1,0:T(8,128)(2,1)S(1)}, u32[]{:S(2)}, u32[]{:S(2)}) collective-permute-start(bf16[192,512]{1,0:T(8,128)(2,1)S(1)} %get-tuple-element.55), channel_id=1, source_target_pairs={{0,4},{4,0},{1,5},{5,1},{2,6},{6,2},{3,7},{7,3},{8,12},{12,8},{9,1... | collective-permute-start | bytes 589832 | tf_op jit(solution)/shard_map/ppermute | solution.py:310
  52.0 0.9 %collective-permute-done.10.far = f32[8,192]{1,0:T(8,128)S(1)} collective-permute-done((f32[8,192]{1,0:T(8,128)S(1)}, f32[8,192]{1,0:T(8,128)S(1)}, u32[]{:S(2)}, u32[]{:S(2)}) %collective-permute-start.10) | collective-permute-done | bytes 6176 | tf_op jit(solution)/shard_map/ppermute | solution.py:307
  52.9 0.0 collective-permute-done.11.got
  52.9 0.5 shard_map.69
  53.4 2.1 %collective-permute-start.13 = (bf16[192,512]{1,0:T(8,128)(2,1)S(1)}, bf16[192,512]{1,0:T(8,128)(2,1)S(1)}, u32[]{:S(2)}, u32[]{:S(2)}) collective-permute-start(bf16[192,512]{1,0:T(8,128)(2,1)S(1)} %get-tuple-element.56), channel_id=1, source_target_pairs={{0,2},{1,3},{2,0},{3,1},{4,6},{5,7},{6,4},{7,5},{8,10},{9,11},{10,... | collective-permute-start | bytes 589832 | tf_op jit(solution)/shard_map/ppermute | solution.py:307
  55.5 0.1 collective-permute-start.14
  55.6 1.5 %collective-permute-done.15.b = bf16[192,512]{1,0:T(8,128)(2,1)S(1)} collective-permute-done((bf16[192,512]{1,0:T(8,128)(2,1)S(1)}, bf16[192,512]{1,0:T(8,128)(2,1)S(1)}, u32[]{:S(2)}, u32[]{:S(2)}) %collective-permute-start.15) | collective-permute-done | bytes 196640 | tf_op jit(solution)/shard_map/ppermute | solution.py:307
  57.1 0.6 collective-permute-start.16
  57.8 1.5 %collective-permute-start.17 = (f32[1,192]{1,0:T(1,128)S(1)}, f32[1,192]{1,0:T(1,128)S(1)}, u32[]{:S(2)}, u32[]{:S(2)}) collective-permute-start(f32[1,192]{1,0:T(1,128)S(1)} %get-tuple-element.61.loss), channel_id=1, source_target_pairs={{0,4},{4,0},{1,5},{5,1},{2,6},{6,2},{3,7},{7,3},{8,12},{12,8},{9,1... | collective-permute-start | bytes 2312 | tf_op jit(solution)/shard_map/ppermute | solution.py:310
  59.2 0.0 collective-permute-done.12.got
  59.2 3.0 %collective-permute-done.13.second = bf16[192,512]{1,0:T(8,128)(2,1)S(1)} collective-permute-done((bf16[192,512]{1,0:T(8,128)(2,1)S(1)}, bf16[192,512]{1,0:T(8,128)(2,1)S(1)}, u32[]{:S(2)}, u32[]{:S(2)}) %collective-permute-start.13) | collective-permute-done | bytes 196640 | tf_op jit(solution)/shard_map/ppermute | solution.py:307
  62.3 0.2 shard_map.70.partial
  62.5 0.4 collective-permute-done.17.other_loss
  62.9 0.0 collective-permute-done.14.first
  62.9 0.0 collective-permute-done.16.theirs
  62.9 1.3 %shard_map.72 = (bf16[192,512]{1,0:T(8,128)(2,1)}, f32[384]{0:T(512)}) custom-call(s32[7]{0:T(128)S(1)} %stack.31.place, f32[4,192,128]{2,1,0:T(8,128)S(1)} %get-tuple-element.54.columns, f32[192,512]{1,0:T(8,128)S(1)} %shard_map.70.partial, bf16[192,512]{1,0:T(8,128)(2,1)S(1)} %collective-permute-done.14.first, ...), custom_call_target="tpu_custom_call" | custom-call | tf_op jit(solution)/shard_map/pallas_call | solution.py:316
  (9 shorter events, 0.1 us)
Async XLA Ops:
  0.7 2.9 %copy-start = (bf16[192,512]{1,0:T(8,128)(2,1)S(1)}, bf16[192,512]{1,0:T(8,128)(2,1)}, u32[]{:S(2)}) copy-start(bf16[192,512]{1,0:T(8,128)(2,1)} %a) | copy-start | bytes 589828
  0.7 10.1 %copy-start.1 = (s32[384]{0:T(512)S(1)}, s32[384]{0:T(512)}, u32[]{:S(2)}) copy-start(s32[384]{0:T(512)} %targets.1) | copy-start | bytes 4612
  0.7 10.1 %copy-start.2 = (f32[384]{0:T(512)S(1)}, f32[384]{0:T(512)}, u32[]{:S(2)}) copy-start(f32[384]{0:T(512)} %scale.1) | copy-start | bytes 4612
  3.7 11.3 %collective-permute-start.1 = (bf16[192,512]{1,0:T(8,128)(2,1)S(1)}, bf16[192,512]{1,0:T(8,128)(2,1)S(1)}, u32[]{:S(2)}, u32[]{:S(2)}) collective-permute-start(bf16[192,512]{1,0:T(8,128)(2,1)S(1)} %copy-done), channel_id=1, source_target_pairs={{0,2},{1,3},{2,0},{3,1},{4,6},{5,7},{6,4},{7,5},{8,10},{9,11},{10,... | collective-permute-start | bytes 589832 | tf_op jit(solution)/shard_map/ppermute | solution.py:307
  7.8 7.8 %collective-permute-start = (bf16[192,512]{1,0:T(8,128)(2,1)S(1)}, bf16[192,512]{1,0:T(8,128)(2,1)S(1)}, u32[]{:S(2)}, u32[]{:S(2)}) collective-permute-start(bf16[192,512]{1,0:T(8,128)(2,1)S(1)} %copy-done), channel_id=1, source_target_pairs={{0,1},{1,0},{2,3},{3,2},{4,5},{5,4},{6,7},{7,6},{8,9},{9,8},{10,11... | collective-permute-start | bytes 589832 | tf_op jit(solution)/shard_map/ppermute | solution.py:307
  9.3 6.2 %collective-permute-start.4 = (bf16[192,512]{1,0:T(8,128)(2,1)S(1)}, bf16[192,512]{1,0:T(8,128)(2,1)S(1)}, u32[]{:S(2)}, u32[]{:S(2)}) collective-permute-start(bf16[192,512]{1,0:T(8,128)(2,1)S(1)} %copy-done), channel_id=1, source_target_pairs={{0,4},{4,0},{1,5},{5,1},{2,6},{6,2},{3,7},{7,3},{8,12},{12,8},{9,1... | collective-permute-start | bytes 589832 | tf_op jit(solution)/shard_map/ppermute | solution.py:310
  15.0 5.7 %collective-permute-start.2 = (bf16[192,512]{1,0:T(8,128)(2,1)S(1)}, bf16[192,512]{1,0:T(8,128)(2,1)S(1)}, u32[]{:S(2)}, u32[]{:S(2)}) collective-permute-start(bf16[192,512]{1,0:T(8,128)(2,1)S(1)} %collective-permute-done.1.c.b), channel_id=1, source_target_pairs={{0,1},{1,0},{2,3},{3,2},{4,5},{5,4},{6,7},{7,6},{8,9},{9,8},{10,11... | collective-permute-start | bytes 589832 | tf_op jit(solution)/shard_map/ppermute | solution.py:307
  15.6 11.6 %collective-permute-start.5 = (bf16[384,512]{1,0:T(8,128)(2,1)S(1)}, bf16[384,512]{1,0:T(8,128)(2,1)S(1)}, u32[]{:S(2)}, u32[]{:S(2)}) collective-permute-start(bf16[384,512]{1,0:T(8,128)(2,1)S(1)} %shard_map.63), channel_id=1, source_target_pairs={{0,4},{4,0},{1,5},{5,1},{2,6},{6,2},{3,7},{7,3},{8,12},{12,8},{9,1... | collective-permute-start | bytes 1179656 | tf_op jit(solution)/shard_map/ppermute | solution.py:310
  20.6 8.6 %collective-permute-start.3 = (bf16[384,512]{1,0:T(8,128)(2,1)S(1)}, bf16[384,512]{1,0:T(8,128)(2,1)S(1)}, u32[]{:S(2)}, u32[]{:S(2)}) collective-permute-start(bf16[384,512]{1,0:T(8,128)(2,1)S(1)} %get-tuple-element.41), channel_id=1, source_target_pairs={{0,1},{1,0},{2,3},{3,2},{4,5},{5,4},{6,7},{7,6},{8,9},{9,8},{10,11... | collective-permute-start | bytes 1179656 | tf_op jit(solution)/shard_map/ppermute | solution.py:307
  21.5 7.8 %collective-permute-start.6 = (bf16[192,512]{1,0:T(8,128)(2,1)S(1)}, bf16[192,512]{1,0:T(8,128)(2,1)S(1)}, u32[]{:S(2)}, u32[]{:S(2)}) collective-permute-start(bf16[192,512]{1,0:T(8,128)(2,1)S(1)} %collective-permute-done.2.d), channel_id=1, source_target_pairs={{0,4},{4,0},{1,5},{5,1},{2,6},{6,2},{3,7},{7,3},{8,12},{12,8},{9,1... | collective-permute-start | bytes 589832 | tf_op jit(solution)/shard_map/ppermute | solution.py:310
  32.2 6.2 %collective-permute-start.7 = (bf16[208,512]{1,0:T(8,128)(2,1)S(1)}, bf16[208,512]{1,0:T(8,128)(2,1)S(1)}, u32[]{:S(2)}, u32[]{:S(2)}) collective-permute-start(bf16[208,512]{1,0:T(8,128)(2,1)S(1)} %get-tuple-element.45), channel_id=1, source_target_pairs={{0,4},{4,0},{1,5},{5,1},{2,6},{6,2},{3,7},{7,3},{8,12},{12,8},{9,1... | collective-permute-start | bytes 638984 | tf_op jit(solution)/shard_map/ppermute | solution.py:310
  33.8 11.8 %collective-permute-start.9 = (bf16[224,512]{1,0:T(8,128)(2,1)S(1)}, bf16[224,512]{1,0:T(8,128)(2,1)S(1)}, u32[]{:S(2)}, u32[]{:S(2)}) collective-permute-start(bf16[224,512]{1,0:T(8,128)(2,1)S(1)} %shard_map.67), channel_id=1, source_target_pairs={{0,2},{1,3},{2,0},{3,1},{4,6},{5,7},{6,4},{7,5},{8,10},{9,11},{10,... | collective-permute-start | bytes 688136 | tf_op jit(solution)/shard_map/ppermute | solution.py:307
  38.7 9.3 %collective-permute-start.8 = (bf16[208,512]{1,0:T(8,128)(2,1)S(1)}, bf16[208,512]{1,0:T(8,128)(2,1)S(1)}, u32[]{:S(2)}, u32[]{:S(2)}) collective-permute-start(bf16[208,512]{1,0:T(8,128)(2,1)S(1)} %get-tuple-element.48), channel_id=1, source_target_pairs={{0,1},{1,0},{2,3},{3,2},{4,5},{5,4},{6,7},{7,6},{8,9},{9,8},{10,11... | collective-permute-start | bytes 638984 | tf_op jit(solution)/shard_map/ppermute | solution.py:307
  39.3 13.6 %collective-permute-start.11 = (bf16[384,512]{1,0:T(8,128)(2,1)S(1)}, bf16[384,512]{1,0:T(8,128)(2,1)S(1)}, u32[]{:S(2)}, u32[]{:S(2)}) collective-permute-start(bf16[384,512]{1,0:T(8,128)(2,1)S(1)} %get-tuple-element.52), channel_id=1, source_target_pairs={{0,4},{4,0},{1,5},{5,1},{2,6},{6,2},{3,7},{7,3},{8,12},{12,8},{9,1... | collective-permute-start | bytes 1179656 | tf_op jit(solution)/shard_map/ppermute | solution.py:310
  48.0 9.1 %collective-permute-start.15 = (bf16[192,512]{1,0:T(8,128)(2,1)S(1)}, bf16[192,512]{1,0:T(8,128)(2,1)S(1)}, u32[]{:S(2)}, u32[]{:S(2)}) collective-permute-start(bf16[192,512]{1,0:T(8,128)(2,1)S(1)} %get-tuple-element.60), channel_id=1, source_target_pairs={{0,1},{1,0},{2,3},{3,2},{4,5},{5,4},{6,7},{7,6},{8,9},{9,8},{10,11... | collective-permute-start | bytes 589832 | tf_op jit(solution)/shard_map/ppermute | solution.py:307
  48.1 4.8 %collective-permute-start.10 = (f32[8,192]{1,0:T(8,128)S(1)}, f32[8,192]{1,0:T(8,128)S(1)}, u32[]{:S(2)}, u32[]{:S(2)}) collective-permute-start(f32[8,192]{1,0:T(8,128)S(1)} %shard_map.68.half), channel_id=1, source_target_pairs={{0,2},{1,3},{2,0},{3,1},{4,6},{5,7},{6,4},{7,5},{8,10},{9,11},{10,... | collective-permute-start | bytes 18440 | tf_op jit(solution)/shard_map/ppermute | solution.py:307
  50.3 9.0 %collective-permute-start.12 = (bf16[192,512]{1,0:T(8,128)(2,1)S(1)}, bf16[192,512]{1,0:T(8,128)(2,1)S(1)}, u32[]{:S(2)}, u32[]{:S(2)}) collective-permute-start(bf16[192,512]{1,0:T(8,128)(2,1)S(1)} %get-tuple-element.55), channel_id=1, source_target_pairs={{0,4},{4,0},{1,5},{5,1},{2,6},{6,2},{3,7},{7,3},{8,12},{12,8},{9,1... | collective-permute-start | bytes 589832 | tf_op jit(solution)/shard_map/ppermute | solution.py:310
  53.4 8.9 %collective-permute-start.13 = (bf16[192,512]{1,0:T(8,128)(2,1)S(1)}, bf16[192,512]{1,0:T(8,128)(2,1)S(1)}, u32[]{:S(2)}, u32[]{:S(2)}) collective-permute-start(bf16[192,512]{1,0:T(8,128)(2,1)S(1)} %get-tuple-element.56), channel_id=1, source_target_pairs={{0,2},{1,3},{2,0},{3,1},{4,6},{5,7},{6,4},{7,5},{8,10},{9,11},{10,... | collective-permute-start | bytes 589832 | tf_op jit(solution)/shard_map/ppermute | solution.py:307
  55.5 7.4 %collective-permute-start.14 = (bf16[192,512]{1,0:T(8,128)(2,1)S(1)}, bf16[192,512]{1,0:T(8,128)(2,1)S(1)}, u32[]{:S(2)}, u32[]{:S(2)}) collective-permute-start(bf16[192,512]{1,0:T(8,128)(2,1)S(1)} %get-tuple-element.57), channel_id=1, source_target_pairs={{0,1},{1,0},{2,3},{3,2},{4,5},{5,4},{6,7},{7,6},{8,9},{9,8},{10,11... | collective-permute-start | bytes 589832 | tf_op jit(solution)/shard_map/ppermute | solution.py:307
  57.1 5.8 %collective-permute-start.16 = (bf16[192,512]{1,0:T(8,128)(2,1)S(1)}, bf16[192,512]{1,0:T(8,128)(2,1)S(1)}, u32[]{:S(2)}, u32[]{:S(2)}) collective-permute-start(bf16[192,512]{1,0:T(8,128)(2,1)S(1)} %shard_map.71), channel_id=1, source_target_pairs={{0,4},{4,0},{1,5},{5,1},{2,6},{6,2},{3,7},{7,3},{8,12},{12,8},{9,1... | collective-permute-start | bytes 589832 | tf_op jit(solution)/shard_map/ppermute | solution.py:310
  57.8 5.2 %collective-permute-start.17 = (f32[1,192]{1,0:T(1,128)S(1)}, f32[1,192]{1,0:T(1,128)S(1)}, u32[]{:S(2)}, u32[]{:S(2)}) collective-permute-start(f32[1,192]{1,0:T(1,128)S(1)} %get-tuple-element.61.loss), channel_id=1, source_target_pairs={{0,4},{4,0},{1,5},{5,1},{2,6},{6,2},{3,7},{7,3},{8,12},{12,8},{9,1... | collective-permute-start | bytes 2312 | tf_op jit(solution)/shard_map/ppermute | solution.py:310

commit v4 on v3

--- a/solution.py
+++ b/solution.py
@@ -212,14 +212,21 @@
     out[...] = acc
 
 
-def peer_kernel(place, kept, targets, partial, d, block0, block21, block3):
+def peer_kernel(place, kept, targets, partial, d, block3, others):
     rows, width = d.shape
     acc = partial[...] + jnp.dot(d[...], block(kept, place, 3, width), preferred_element_type=F32)
-    stats, others = softmax_part(acc, targets)
+    stats, shifted = softmax_part(acc, targets)
     block3[rows:] = with_tail(as_rows(stats), width)
-    for k, out in ((3, block3.at[:rows]), (2, block21.at[:rows]), (1, block21.at[rows:]), (0, block0)):
+    weights = block(kept, place, 3, width)
+    block3[:rows] = lax.dot_general(shifted, weights, ROWS_BY_ROWS, preferred_element_type=F32).astype(BF16)
+    others[...] = shifted
+
+
+def rest_kernel(place, kept, others, block0, block21):
+    rows, width = block0.shape
+    for k, out in ((2, block21.at[:rows]), (1, block21.at[rows:]), (0, block0)):
         weights = block(kept, place, k, width)
-        out[...] = lax.dot_general(others, weights, ROWS_BY_ROWS, preferred_element_type=F32).astype(BF16)
+        out[...] = lax.dot_general(others[...], weights, ROWS_BY_ROWS, preferred_element_type=F32).astype(BF16)
 
 
 def join(a, b):
@@ -252,14 +259,13 @@
     both = join(mine, theirs)
     stats = jnp.concatenate(list(both) + [mine[0], theirs[0]] + [jnp.zeros((3, rows), F32)], axis=0)
     pair[...] = stats
-    sent[rows:] = with_tail(both, sent.shape[1])
     near, far = columns_of([jnp.exp(mine[0] - both[0]), jnp.exp(theirs[0] - both[0])])
-    sent[:rows] = (near * sums[3] + far * got[:rows].astype(F32)).astype(BF16)
+    sent[...] = (near * sums[3] + far * got[:rows].astype(F32)).astype(BF16)
 
 
 def join_kernel(pair, got, out):
     rows = pair.shape[1]
-    near = from_tail(got, rows)
+    near = as_rows(got[...])
     both = join(as_rows(pair[...]), near)
     out[...] = jnp.concatenate(list(both) + [near[0], jnp.zeros((4, rows), F32)], axis=0)
 
@@ -268,8 +274,8 @@
     return by[0] * sums[k] + by[1] * got[...].astype(F32) + by[3] * picked[k].astype(F32)
 
 
-def scale_kernel(scale, pair, half, far, sums, got, relayed, picked, near_picked, loss, columns, second, first):
-    rows = first.shape[0]
+def scale_kernel(scale, pair, half, far, sums, got, relayed, picked, near_picked, loss, columns, second):
+    rows = second.shape[0]
     top, total, label = join(as_rows(half[...]), as_rows(far[...]))
     loss[...] = jnp.log(total) + top - label
     weighted = scale[...] / total
@@ -279,9 +285,14 @@
     for i, column in enumerate(by):
         columns[i] = jnp.broadcast_to(column, columns.shape[1:])
     here = block_sum(by, sums, got.at[:rows], picked, 2)
-    here += by[2] * relayed[:rows].astype(F32) + by[3] * near_picked[rows:].astype(F32)
+    here += by[2] * relayed[...].astype(F32) + by[3] * near_picked[rows:].astype(F32)
     second[...] = here.astype(BF16)
-    first[...] = block_sum(by, sums, got.at[rows:], picked, 1).astype(BF16)
+
+
+def first_kernel(columns, sums, got, picked, out):
+    by = [columns[i][:, :1] for i in range(4)]
+    rows = out.shape[0]
+    out[...] = block_sum(by, sums, got.at[rows:], picked, 1).astype(BF16)
 
 
 def second_kernel(columns, sums, got, picked, second, out):
@@ -292,9 +303,10 @@
 def last_kernel(place, columns, partial, first, theirs, loss, other_loss, out, row_loss):
     here = partial[...] + first[...].astype(F32) + columns[3][:, :1] * theirs[...].astype(F32)
     out[...] = here.astype(BF16)
+    rows = out.shape[0]
     lower = place[5] == 0
-    row_loss[: out.shape[0]] = jnp.where(lower, loss[...], other_loss[...])[0]
-    row_loss[out.shape[0] :] = jnp.where(lower, other_loss[...], loss[...])[0]
+    row_loss[:rows] = jnp.where(lower, loss[...], other_loss[...])[0]
+    row_loss[rows:] = jnp.where(lower, other_loss[...], loss[...])[0]
 
 
 def two_by_four(hidden, weight, targets, row_weight):
@@ -335,8 +347,11 @@
 
     weight = pltpu.with_memory_space_constraint(weight, pltpu.HBM)
     dma = [pltpu.SemaphoreType.DMA]
+    column_sums = shape(tensors, rows, width)
+
     kept = call(fetch_kernel, pltpu.VMEM(weight.shape, BF16), [SMEM, HBM], place, weight, scratch=dma)
-    hidden = after(hidden, kept)
+    hidden = after(hidden, [kept])
+
     z2 = along(hidden, 2)
     z1 = along(hidden, 1)
     x0 = across(hidden)
@@ -346,51 +361,53 @@
         [SMEM, HBM, VMEM, VMEM, VMEM],
         place, weight, targets, row_weight, kept, scratch=dma, aliases={4: 0},
     )
-    z2 = after(z2, scale)
-    z3 = along(z2, 1)
-    x12 = across(call(stack_kernel, two, [VMEM] * 2, after(z1, x0), z2))
-    mine_rows, *other_rows, sent_rows = call(
+    z3 = along(after(z2, [scale]), 1)
+    x12 = across(call(stack_kernel, two, [VMEM] * 2, after(z1, [x0]), after(z2, [scale])))
+
+    mine_rows, rows0, rows1, rows2, rows3 = call(
         pick_kernel, [shape(3, rows, width, dtype=BF16), piece, piece, piece, two], [SMEM] + [VMEM] * 3,
-        after(place, z2), kept, mine, other,
-    )
-    x3 = across(after(z3, sent_rows))
-
-    relayed_rows = along(after(sent_rows, z3), 1)
+        after(place, [z2]), kept, mine, other,
+    )
+    x3 = across(after(z3, [rows3]))
+    relayed_rows = along(after(rows3, [z3]), 1)
 
     own_stats, sums = call(
-        own_kernel, [shape(8, rows), shape(tensors, rows, width)], [SMEM] + [VMEM] * 6,
-        place, kept, mine, hidden, z1, z2, z3,
+        own_kernel, [shape(8, rows), column_sums], [SMEM] + [VMEM] * 6, place, kept, mine, hidden, z1, z2, z3
     )
     partial = call(start_kernel, shape(rows, vocab_dev), [SMEM] + [VMEM] * 3, place, kept, x0, x12)
-    other = after(other, (own_stats, relayed_rows))
-    block0, block21, block3 = call(
-        peer_kernel, [piece, two, tailed], [SMEM] + [VMEM] * 4, place, kept, other, partial, x3
-    )
-    far_rows = along(call(add_kernel, shape(rows + 32, width, dtype=BF16), [VMEM] * 2, other_rows[2], relayed_rows), 2)
+    block3, others = call(
+        peer_kernel, [tailed, shape(rows, vocab_dev, dtype=BF16)], [SMEM] + [VMEM] * 4,
+        place, kept, after(other, [own_stats, relayed_rows]), partial, x3,
+    )
+
+    far_rows = call(add_kernel, shape(rows + 32, width, dtype=BF16), [VMEM] * 2, rows2, relayed_rows)
+    far_rows = along(far_rows, 2)
     got3 = across(block3)
-    pair, relayed = call(pair_kernel, [shape(8, rows), tailed], [VMEM] * 3, own_stats, got3, sums)
+    block0, block21 = call(rest_kernel, [piece, two], [SMEM] + [VMEM] * 2, place, kept, others)
+    pair, relayed = call(pair_kernel, [shape(8, rows), piece], [VMEM] * 3, own_stats, got3, sums)
+    near = along(pair, 1)
     relayed = along(relayed, 1)
-    got21 = across(after(block21, pair))
-    half = call(join_kernel, shape(8, rows), [VMEM] * 2, pair, after(relayed, far_rows))
+    got21 = across(after(block21, [pair]))
+    half = call(join_kernel, shape(8, rows), [VMEM] * 2, after(pair, [far_rows]), near)
     far = along(half, 2)
-    near_rows = along(after(other_rows[1], half), 1)
-    loss, columns, second, first = call(
+    loss, columns, second = call(
         scale_kernel,
-        [shape(1, rows), shape(4, rows, 128), piece, piece],
+        [shape(1, rows), shape(4, rows, 128), piece],
         [VMEM] * 9,
         scale, pair, half, far, sums, got21, relayed, mine_rows, relayed_rows,
     )
+    near_rows = along(after(rows1, [half]), 1)
     second = along(second, 2)
-    got0 = across(block0)
-    picked = across(call(last_rows_kernel, piece, [VMEM] * 3, other_rows[0], near_rows, far_rows))
-    first = along(first, 1)
+    got0 = across(after(block0, [got21]))
+    picked = call(last_rows_kernel, piece, [VMEM] * 3, after(rows0, [got21]), near_rows, far_rows)
+    picked = across(picked)
     other_loss = across(loss)
-    partial = call(second_kernel, shape(rows, width), [VMEM] * 5, columns, sums, got0, mine_rows, second)
-    grad, row_loss = call(
+    first = along(call(first_kernel, piece, [VMEM] * 4, columns, sums, got21, mine_rows), 1)
+    total = call(second_kernel, shape(rows, width), [VMEM] * 5, columns, sums, got0, mine_rows, second)
+    return call(
         last_kernel, [piece, shape(2 * rows)], [SMEM] + [VMEM] * 6,
-        place, columns, partial, first, picked, loss, other_loss,
-    )
-    return grad, row_loss
+        place, columns, total, first, picked, loss, other_loss,
+    )
 
 
 def per_device(hidden, weight, targets, row_weight):

time: 64.4 us -> 62.6 us (0.972)
  waiting for transfers between devices: 19.6 us -> 14.5 us
  starting transfers between devices: 26.8 us -> 29.3 us
  Pallas kernels: 17 us -> 17.8 us
    ppermute x10 -> x11, waiting for transfers between devices: 17.4 us -> 13.7 us  [along(): return lax.ppermute(a, 'tensor', partners(tensors, k))]
    ppermute x10 -> x11, starting transfers between devices: 15.7 us -> 19.2 us  [along(): return lax.ppermute(a, 'tensor', partners(tensors, k))]
    ppermute x8, waiting for transfers between devices: 2.21 us -> 0.75 us  [across(): return lax.ppermute(a, 'pipe', [(0, 1), (1, 0)])]
    ppermute x8, starting transfers between devices: 11.2 us -> 10.1 us  [across(): return lax.ppermute(a, 'pipe', [(0, 1), (1, 0)])]
    pallas_call x14 -> x16, Pallas kernels: 17 us -> 17.8 us  [call(): pl.pallas_call(kernel, out_shape=outs, in_specs=ins, out_specs=jax.tree.m...]
  transfers between devices with their start and end apart: 18 -> 19, of which waited for: 12 -> 10; matrix products, arithmetic and copies ran while one was open for 0% -> 0% of each run, Pallas kernels for 15% -> 19%
where the time goes in v4:
time: 62.6 us; the launch traced here: 62.5 us
  starting transfers between devices  29.3 us (47%)
  Pallas kernels  17.8 us (28%)
  waiting for transfers between devices  14.5 us (23%)
  between operations  0.81 us (1%)
    ppermute x11, starting transfers between devices, along(): return lax.ppermute(a, 'tensor', partners(tensors, k))  19.2 us
    pallas_call x16, Pallas kernels, call(): pl.pallas_call(kernel, out_shape=outs, in_specs=ins, out_specs=jax.tree.m...  17.8 us
    ppermute x11, waiting for transfers between devices, along(): return lax.ppermute(a, 'tensor', partners(tensors, k))  13.7 us
    ppermute x8, starting transfers between devices, across(): return lax.ppermute(a, 'pipe', [(0, 1), (1, 0)])  10.1 us
  transfers between devices with their start and end apart: 19, of which 10 were waited for; matrix products, arithmetic and copies ran while one was open for 0% of the time, Pallas kernels for 19%

profile of v4, /device:TPU:0, one launch (start us, length us, event | category | flops | bytes accessed | tf_op | source)
XLA Modules:
  0.0 62.5 jit_solution(16607145103123625717)
XLA Ops:
  0.6 0.1 stack.31.place
  0.7 0.0 copy-start.2
  0.7 2.9 %shard_map.59.fetched = bf16[2048,1152]{1,0:T(8,128)(2,1)S(1)} custom-call(s32[7]{0:T(128)S(1)} %stack.31.place, bf16[2048,1152]{1,0:T(8,128)(2,1)} %weight.3), custom_call_target="tpu_custom_call" | custom-call | tf_op jit(solution)/shard_map/pallas_call | solution.py:328
  3.7 4.1 %collective-permute-start.1 = (bf16[192,512]{1,0:T(8,128)(2,1)S(1)}, bf16[192,512]{1,0:T(8,128)(2,1)S(1)}, u32[]{:S(2)}, u32[]{:S(2)}) collective-permute-start(bf16[192,512]{1,0:T(8,128)(2,1)S(1)} %copy-done), channel_id=1, source_target_pairs={{0,2},{1,3},{2,0},{3,1},{4,6},{5,7},{6,4},{7,5},{8,10},{9,11},{10,... | collective-permute-start | bytes 589832 | tf_op jit(solution)/shard_map/ppermute | solution.py:319
  7.8 1.6 %collective-permute-start = (bf16[192,512]{1,0:T(8,128)(2,1)S(1)}, bf16[192,512]{1,0:T(8,128)(2,1)S(1)}, u32[]{:S(2)}, u32[]{:S(2)}) collective-permute-start(bf16[192,512]{1,0:T(8,128)(2,1)S(1)} %copy-done), channel_id=1, source_target_pairs={{0,1},{1,0},{2,3},{3,2},{4,5},{5,4},{6,7},{7,6},{8,9},{9,8},{10,11... | collective-permute-start | bytes 589832 | tf_op jit(solution)/shard_map/ppermute | solution.py:319
  9.3 1.5 %collective-permute-start.4 = (bf16[192,512]{1,0:T(8,128)(2,1)S(1)}, bf16[192,512]{1,0:T(8,128)(2,1)S(1)}, u32[]{:S(2)}, u32[]{:S(2)}) collective-permute-start(bf16[192,512]{1,0:T(8,128)(2,1)S(1)} %copy-done), channel_id=1, source_target_pairs={{0,4},{4,0},{1,5},{5,1},{2,6},{6,2},{3,7},{7,3},{8,12},{12,8},{9,1... | collective-permute-start | bytes 589832 | tf_op jit(solution)/shard_map/ppermute | solution.py:322
  10.8 0.8 %shard_map.60 = (bf16[2048,1152]{1,0:T(8,128)(2,1)S(1)}, s32[192,128]{1,0:T(8,128)S(1)}, s32[192,128]{1,0:T(8,128)S(1)}, f32[1,192]{1,0:T(1,128)S(1)}) custom-call(s32[7]{0:T(128)S(1)} %stack.31.place, bf16[2048,1152]{1,0:T(8,128)(2,1)} %weight.3, s32[384]{0:T(512)S(1)} %copy-done.1, f32[384]{0:T(512)S(1)} %copy-done.2, ...), custom_call_target="tpu_custom_call", output_to_operand_aliasing={{0}: (4, {})} | custom-call | tf_op jit(solution)/shard_map/pallas_call | solution.py:328
  11.7 3.3 %collective-permute-done.1.c.b = bf16[192,512]{1,0:T(8,128)(2,1)S(1)} collective-permute-done((bf16[192,512]{1,0:T(8,128)(2,1)S(1)}, bf16[192,512]{1,0:T(8,128)(2,1)S(1)}, u32[]{:S(2)}, u32[]{:S(2)}) %collective-permute-start.1) | collective-permute-done | bytes 196640 | tf_op jit(solution)/shard_map/ppermute | solution.py:319
  15.0 0.6 collective-permute-start.2
  15.5 0.0 collective-permute-done.b.a
  15.5 0.0 collective-permute-done.4.a
  15.6 1.6 %collective-permute-start.5 = (bf16[384,512]{1,0:T(8,128)(2,1)S(1)}, bf16[384,512]{1,0:T(8,128)(2,1)S(1)}, u32[]{:S(2)}, u32[]{:S(2)}) collective-permute-start(bf16[384,512]{1,0:T(8,128)(2,1)S(1)} %shard_map.63), channel_id=1, source_target_pairs={{0,4},{4,0},{1,5},{5,1},{2,6},{6,2},{3,7},{7,3},{8,12},{12,8},{9,1... | collective-permute-start | bytes 1179656 | tf_op jit(solution)/shard_map/ppermute | solution.py:322
  17.1 2.8 %shard_map.62 = (bf16[3,192,512]{2,1,0:T(8,128)(2,1)S(1)}, bf16[192,512]{1,0:T(8,128)(2,1)S(1)}, bf16[192,512]{1,0:T(8,128)(2,1)S(1)}, bf16[192,512]{1,0:T(8,128)(2,1)S(1)}, bf16[384,512]{1,0:T(8,128)(2,1)S(1)}) custom-call(s32[7]{0:T(128)S(1)} %stack.31.place, bf16[2048,1152]{1,0:T(8,128)(2,1)S(1)} %get-tuple-element.35.kept, ...), custom_call_target="tpu_custom_call" | custom-call | tf_op jit(solution)/shard_map/pallas_call | solution.py:328
  19.9 0.7 %collective-permute-done.2.d = bf16[192,512]{1,0:T(8,128)(2,1)S(1)} collective-permute-done((bf16[192,512]{1,0:T(8,128)(2,1)S(1)}, bf16[192,512]{1,0:T(8,128)(2,1)S(1)}, u32[]{:S(2)}, u32[]{:S(2)}) %collective-permute-start.2) | collective-permute-done | bytes 196640 | tf_op jit(solution)/shard_map/ppermute | solution.py:319
  20.6 0.9 %collective-permute-start.3 = (bf16[384,512]{1,0:T(8,128)(2,1)S(1)}, bf16[384,512]{1,0:T(8,128)(2,1)S(1)}, u32[]{:S(2)}, u32[]{:S(2)}) collective-permute-start(bf16[384,512]{1,0:T(8,128)(2,1)S(1)} %get-tuple-element.43), channel_id=1, source_target_pairs={{0,1},{1,0},{2,3},{3,2},{4,5},{5,4},{6,7},{7,6},{8,9},{9,8},{10,11... | collective-permute-start | bytes 1179656 | tf_op jit(solution)/shard_map/ppermute | solution.py:319
  21.5 1.5 %collective-permute-start.6 = (bf16[192,512]{1,0:T(8,128)(2,1)S(1)}, bf16[192,512]{1,0:T(8,128)(2,1)S(1)}, u32[]{:S(2)}, u32[]{:S(2)}) collective-permute-start(bf16[192,512]{1,0:T(8,128)(2,1)S(1)} %collective-permute-done.2.d), channel_id=1, source_target_pairs={{0,4},{4,0},{1,5},{5,1},{2,6},{6,2},{3,7},{7,3},{8,12},{12,8},{9,1... | collective-permute-start | bytes 589832 | tf_op jit(solution)/shard_map/ppermute | solution.py:322
  23.0 3.6 %shard_map.61 = (f32[8,192]{1,0:T(8,128)S(1)}, f32[4,192,512]{2,1,0:T(8,128)S(1)}) custom-call(s32[7]{0:T(128)S(1)} %stack.31.place, bf16[2048,1152]{1,0:T(8,128)(2,1)S(1)} %get-tuple-element.35.kept, s32[192,128]{1,0:T(8,128)S(1)} %get-tuple-element.36.targets.mine, bf16[192,512]{1,0:T(8,128)(2,1)S(1)} %copy-done, ...), custom_call_target="tpu_custom_call" | custom-call | tf_op jit(solution)/shard_map/pallas_call | solution.py:328
  26.6 0.6 collective-permute-done.5.bc
  27.2 1.5 %shard_map.64.partial = f32[192,1152]{1,0:T(8,128)S(1)} custom-call(s32[7]{0:T(128)S(1)} %stack.31.place, bf16[2048,1152]{1,0:T(8,128)(2,1)S(1)} %get-tuple-element.35.kept, bf16[192,512]{1,0:T(8,128)(2,1)S(1)} %collective-permute-done.4.a, bf16[384,512]{1,0:T(8,128)(2,1)S(1)} %collective-permute-done.5.bc), custom_call_target="tpu_custom_call" | custom-call | tf_op jit(solution)/shard_map/pallas_call | solution.py:328
  28.7 0.5 collective-permute-done.3.b.near_picked
  29.2 0.1 collective-permute-done.6.d
  29.3 1.8 %shard_map.65 = (bf16[208,512]{1,0:T(8,128)(2,1)S(1)}, bf16[192,1152]{1,0:T(8,128)(2,1)S(1)}) custom-call(s32[7]{0:T(128)S(1)} %stack.31.place, bf16[2048,1152]{1,0:T(8,128)(2,1)S(1)} %get-tuple-element.35.kept, s32[192,128]{1,0:T(8,128)S(1)} %get-tuple-element.44.other.targets, f32[192,1152]{1,0:T(8,128)S(1)} %shard_map.64.partial, ...), custom_call_target="tpu_custom_call" | custom-call | tf_op jit(solution)/shard_map/pallas_call | solution.py:328
  31.1 1.6 %collective-permute-start.7 = (bf16[208,512]{1,0:T(8,128)(2,1)S(1)}, bf16[208,512]{1,0:T(8,128)(2,1)S(1)}, u32[]{:S(2)}, u32[]{:S(2)}) collective-permute-start(bf16[208,512]{1,0:T(8,128)(2,1)S(1)} %get-tuple-element.47), channel_id=1, source_target_pairs={{0,4},{4,0},{1,5},{5,1},{2,6},{6,2},{3,7},{7,3},{8,12},{12,8},{9,1... | collective-permute-start | bytes 638984 | tf_op jit(solution)/shard_map/ppermute | solution.py:322
  32.7 3.6 %collective-permute-start.8 = (bf16[224,512]{1,0:T(8,128)(2,1)S(1)}, bf16[224,512]{1,0:T(8,128)(2,1)S(1)}, u32[]{:S(2)}, u32[]{:S(2)}) collective-permute-start(bf16[224,512]{1,0:T(8,128)(2,1)S(1)} %shard_map.67), channel_id=1, source_target_pairs={{0,2},{1,3},{2,0},{3,1},{4,6},{5,7},{6,4},{7,5},{8,10},{9,11},{10,... | collective-permute-start | bytes 688136 | tf_op jit(solution)/shard_map/ppermute | solution.py:319
  36.3 1.9 %shard_map.69 = (bf16[192,512]{1,0:T(8,128)(2,1)S(1)}, bf16[384,512]{1,0:T(8,128)(2,1)S(1)}) custom-call(s32[7]{0:T(128)S(1)} %stack.31.place, bf16[2048,1152]{1,0:T(8,128)(2,1)S(1)} %get-tuple-element.35.kept, bf16[192,1152]{1,0:T(8,128)(2,1)S(1)} %get-tuple-element.52.others), custom_call_target="tpu_custom_call" | custom-call | tf_op jit(solution)/shard_map/pallas_call | solution.py:328
  38.1 0.0 collective-permute-done.7.got
  38.2 0.3 shard_map.66
  38.5 0.6 collective-permute-start.11
  39.0 0.5 collective-permute-start.9
  39.5 1.5 %collective-permute-start.12 = (bf16[192,512]{1,0:T(8,128)(2,1)S(1)}, bf16[192,512]{1,0:T(8,128)(2,1)S(1)}, u32[]{:S(2)}, u32[]{:S(2)}) collective-permute-start(bf16[192,512]{1,0:T(8,128)(2,1)S(1)} %get-tuple-element.55), channel_id=1, source_target_pairs={{0,1},{1,0},{2,3},{3,2},{4,5},{5,4},{6,7},{7,6},{8,9},{9,8},{10,11... | collective-permute-start | bytes 589832 | tf_op jit(solution)/shard_map/ppermute | solution.py:319
  41.1 3.4 %collective-permute-done.8.c = bf16[224,512]{1,0:T(8,128)(2,1)S(1)} collective-permute-done((bf16[224,512]{1,0:T(8,128)(2,1)S(1)}, bf16[224,512]{1,0:T(8,128)(2,1)S(1)}, u32[]{:S(2)}, u32[]{:S(2)}) %collective-permute-start.8) | collective-permute-done | bytes 229408 | tf_op jit(solution)/shard_map/ppermute | solution.py:319
  44.4 0.2 collective-permute-done.9.got
  44.7 0.1 collective-permute-start.16
  44.8 3.1 %collective-permute-start.10 = (f32[8,192]{1,0:T(8,128)S(1)}, f32[8,192]{1,0:T(8,128)S(1)}, u32[]{:S(2)}, u32[]{:S(2)}) collective-permute-start(f32[8,192]{1,0:T(8,128)S(1)} %shard_map.68.half), channel_id=1, source_target_pairs={{0,2},{1,3},{2,0},{3,1},{4,6},{5,7},{6,4},{7,5},{8,10},{9,11},{10,... | collective-permute-start | bytes 18440 | tf_op jit(solution)/shard_map/ppermute | solution.py:319
  47.9 0.6 %collective-permute-start.13 = (bf16[192,512]{1,0:T(8,128)(2,1)S(1)}, bf16[192,512]{1,0:T(8,128)(2,1)S(1)}, u32[]{:S(2)}, u32[]{:S(2)}) collective-permute-start(bf16[192,512]{1,0:T(8,128)(2,1)S(1)} %get-tuple-element.59), channel_id=1, source_target_pairs={{0,4},{4,0},{1,5},{5,1},{2,6},{6,2},{3,7},{7,3},{8,12},{12,8},{9,1... | collective-permute-start | bytes 589832 | tf_op jit(solution)/shard_map/ppermute | solution.py:322
  48.5 1.1 %collective-permute-done.10.far = f32[8,192]{1,0:T(8,128)S(1)} collective-permute-done((f32[8,192]{1,0:T(8,128)S(1)}, f32[8,192]{1,0:T(8,128)S(1)}, u32[]{:S(2)}, u32[]{:S(2)}) %collective-permute-start.10) | collective-permute-done | bytes 6176 | tf_op jit(solution)/shard_map/ppermute | solution.py:319
  49.6 0.4 shard_map.70
  50.1 2.9 %collective-permute-start.14 = (bf16[192,512]{1,0:T(8,128)(2,1)S(1)}, bf16[192,512]{1,0:T(8,128)(2,1)S(1)}, u32[]{:S(2)}, u32[]{:S(2)}) collective-permute-start(bf16[192,512]{1,0:T(8,128)(2,1)S(1)} %get-tuple-element.60), channel_id=1, source_target_pairs={{0,2},{1,3},{2,0},{3,1},{4,6},{5,7},{6,4},{7,5},{8,10},{9,11},{10,... | collective-permute-start | bytes 589832 | tf_op jit(solution)/shard_map/ppermute | solution.py:319
  52.9 0.0 collective-permute-done.16.b
  53.0 1.2 %collective-permute-start.17 = (bf16[192,512]{1,0:T(8,128)(2,1)S(1)}, bf16[192,512]{1,0:T(8,128)(2,1)S(1)}, u32[]{:S(2)}, u32[]{:S(2)}) collective-permute-start(bf16[192,512]{1,0:T(8,128)(2,1)S(1)} %shard_map.73), channel_id=1, source_target_pairs={{0,4},{4,0},{1,5},{5,1},{2,6},{6,2},{3,7},{7,3},{8,12},{12,8},{9,1... | collective-permute-start | bytes 589832 | tf_op jit(solution)/shard_map/ppermute | solution.py:322
  54.1 0.2 shard_map.72
  54.3 0.4 collective-permute-start.15
  54.7 1.6 %collective-permute-start.18 = (f32[1,192]{1,0:T(1,128)S(1)}, f32[1,192]{1,0:T(1,128)S(1)}, u32[]{:S(2)}, u32[]{:S(2)}) collective-permute-start(f32[1,192]{1,0:T(1,128)S(1)} %get-tuple-element.65.loss), channel_id=1, source_target_pairs={{0,4},{4,0},{1,5},{5,1},{2,6},{6,2},{3,7},{7,3},{8,12},{12,8},{9,1... | collective-permute-start | bytes 2312 | tf_op jit(solution)/shard_map/ppermute | solution.py:322
  56.3 3.4 %collective-permute-done.14.second = bf16[192,512]{1,0:T(8,128)(2,1)S(1)} collective-permute-done((bf16[192,512]{1,0:T(8,128)(2,1)S(1)}, bf16[192,512]{1,0:T(8,128)(2,1)S(1)}, u32[]{:S(2)}, u32[]{:S(2)}) %collective-permute-start.14) | collective-permute-done | bytes 196640 | tf_op jit(solution)/shard_map/ppermute | solution.py:319
  59.7 0.2 shard_map.71.partial
  59.9 0.0 collective-permute-done.17.theirs
  60.0 1.2 %collective-permute-done.15.first = bf16[192,512]{1,0:T(8,128)(2,1)S(1)} collective-permute-done((bf16[192,512]{1,0:T(8,128)(2,1)S(1)}, bf16[192,512]{1,0:T(8,128)(2,1)S(1)}, u32[]{:S(2)}, u32[]{:S(2)}) %collective-permute-start.15) | collective-permute-done | bytes 196640 | tf_op jit(solution)/shard_map/ppermute | solution.py:319
  61.1 1.3 %shard_map.74 = (bf16[192,512]{1,0:T(8,128)(2,1)}, f32[384]{0:T(512)}) custom-call(s32[7]{0:T(128)S(1)} %stack.31.place, f32[4,192,128]{2,1,0:T(8,128)S(1)} %get-tuple-element.57.columns, f32[192,512]{1,0:T(8,128)S(1)} %shard_map.71.partial, bf16[192,512]{1,0:T(8,128)(2,1)S(1)} %collective-permute-done.15.first, ...), custom_call_target="tpu_custom_call" | custom-call | tf_op jit(solution)/shard_map/pallas_call | solution.py:328
  (13 shorter events, 0.1 us)
Async XLA Ops:
  0.7 2.9 %copy-start = (bf16[192,512]{1,0:T(8,128)(2,1)S(1)}, bf16[192,512]{1,0:T(8,128)(2,1)}, u32[]{:S(2)}) copy-start(bf16[192,512]{1,0:T(8,128)(2,1)} %a) | copy-start | bytes 589828
  0.7 10.1 %copy-start.1 = (s32[384]{0:T(512)S(1)}, s32[384]{0:T(512)}, u32[]{:S(2)}) copy-start(s32[384]{0:T(512)} %targets.1) | copy-start | bytes 4612
  0.7 10.1 %copy-start.2 = (f32[384]{0:T(512)S(1)}, f32[384]{0:T(512)}, u32[]{:S(2)}) copy-start(f32[384]{0:T(512)} %scale.1) | copy-start | bytes 4612
  3.7 11.3 %collective-permute-start.1 = (bf16[192,512]{1,0:T(8,128)(2,1)S(1)}, bf16[192,512]{1,0:T(8,128)(2,1)S(1)}, u32[]{:S(2)}, u32[]{:S(2)}) collective-permute-start(bf16[192,512]{1,0:T(8,128)(2,1)S(1)} %copy-done), channel_id=1, source_target_pairs={{0,2},{1,3},{2,0},{3,1},{4,6},{5,7},{6,4},{7,5},{8,10},{9,11},{10,... | collective-permute-start | bytes 589832 | tf_op jit(solution)/shard_map/ppermute | solution.py:319
  7.8 7.8 %collective-permute-start = (bf16[192,512]{1,0:T(8,128)(2,1)S(1)}, bf16[192,512]{1,0:T(8,128)(2,1)S(1)}, u32[]{:S(2)}, u32[]{:S(2)}) collective-permute-start(bf16[192,512]{1,0:T(8,128)(2,1)S(1)} %copy-done), channel_id=1, source_target_pairs={{0,1},{1,0},{2,3},{3,2},{4,5},{5,4},{6,7},{7,6},{8,9},{9,8},{10,11... | collective-permute-start | bytes 589832 | tf_op jit(solution)/shard_map/ppermute | solution.py:319
  9.3 6.2 %collective-permute-start.4 = (bf16[192,512]{1,0:T(8,128)(2,1)S(1)}, bf16[192,512]{1,0:T(8,128)(2,1)S(1)}, u32[]{:S(2)}, u32[]{:S(2)}) collective-permute-start(bf16[192,512]{1,0:T(8,128)(2,1)S(1)} %copy-done), channel_id=1, source_target_pairs={{0,4},{4,0},{1,5},{5,1},{2,6},{6,2},{3,7},{7,3},{8,12},{12,8},{9,1... | collective-permute-start | bytes 589832 | tf_op jit(solution)/shard_map/ppermute | solution.py:322
  15.0 5.7 %collective-permute-start.2 = (bf16[192,512]{1,0:T(8,128)(2,1)S(1)}, bf16[192,512]{1,0:T(8,128)(2,1)S(1)}, u32[]{:S(2)}, u32[]{:S(2)}) collective-permute-start(bf16[192,512]{1,0:T(8,128)(2,1)S(1)} %collective-permute-done.1.c.b), channel_id=1, source_target_pairs={{0,1},{1,0},{2,3},{3,2},{4,5},{5,4},{6,7},{7,6},{8,9},{9,8},{10,11... | collective-permute-start | bytes 589832 | tf_op jit(solution)/shard_map/ppermute | solution.py:319
  15.6 11.6 %collective-permute-start.5 = (bf16[384,512]{1,0:T(8,128)(2,1)S(1)}, bf16[384,512]{1,0:T(8,128)(2,1)S(1)}, u32[]{:S(2)}, u32[]{:S(2)}) collective-permute-start(bf16[384,512]{1,0:T(8,128)(2,1)S(1)} %shard_map.63), channel_id=1, source_target_pairs={{0,4},{4,0},{1,5},{5,1},{2,6},{6,2},{3,7},{7,3},{8,12},{12,8},{9,1... | collective-permute-start | bytes 1179656 | tf_op jit(solution)/shard_map/ppermute | solution.py:322
  20.6 8.6 %collective-permute-start.3 = (bf16[384,512]{1,0:T(8,128)(2,1)S(1)}, bf16[384,512]{1,0:T(8,128)(2,1)S(1)}, u32[]{:S(2)}, u32[]{:S(2)}) collective-permute-start(bf16[384,512]{1,0:T(8,128)(2,1)S(1)} %get-tuple-element.43), channel_id=1, source_target_pairs={{0,1},{1,0},{2,3},{3,2},{4,5},{5,4},{6,7},{7,6},{8,9},{9,8},{10,11... | collective-permute-start | bytes 1179656 | tf_op jit(solution)/shard_map/ppermute | solution.py:319
  21.5 7.8 %collective-permute-start.6 = (bf16[192,512]{1,0:T(8,128)(2,1)S(1)}, bf16[192,512]{1,0:T(8,128)(2,1)S(1)}, u32[]{:S(2)}, u32[]{:S(2)}) collective-permute-start(bf16[192,512]{1,0:T(8,128)(2,1)S(1)} %collective-permute-done.2.d), channel_id=1, source_target_pairs={{0,4},{4,0},{1,5},{5,1},{2,6},{6,2},{3,7},{7,3},{8,12},{12,8},{9,1... | collective-permute-start | bytes 589832 | tf_op jit(solution)/shard_map/ppermute | solution.py:322
  31.1 7.0 %collective-permute-start.7 = (bf16[208,512]{1,0:T(8,128)(2,1)S(1)}, bf16[208,512]{1,0:T(8,128)(2,1)S(1)}, u32[]{:S(2)}, u32[]{:S(2)}) collective-permute-start(bf16[208,512]{1,0:T(8,128)(2,1)S(1)} %get-tuple-element.47), channel_id=1, source_target_pairs={{0,4},{4,0},{1,5},{5,1},{2,6},{6,2},{3,7},{7,3},{8,12},{12,8},{9,1... | collective-permute-start | bytes 638984 | tf_op jit(solution)/shard_map/ppermute | solution.py:322
  32.7 11.8 %collective-permute-start.8 = (bf16[224,512]{1,0:T(8,128)(2,1)S(1)}, bf16[224,512]{1,0:T(8,128)(2,1)S(1)}, u32[]{:S(2)}, u32[]{:S(2)}) collective-permute-start(bf16[224,512]{1,0:T(8,128)(2,1)S(1)} %shard_map.67), channel_id=1, source_target_pairs={{0,2},{1,3},{2,0},{3,1},{4,6},{5,7},{6,4},{7,5},{8,10},{9,11},{10,... | collective-permute-start | bytes 688136 | tf_op jit(solution)/shard_map/ppermute | solution.py:319
  38.5 9.4 %collective-permute-start.11 = (bf16[384,512]{1,0:T(8,128)(2,1)S(1)}, bf16[384,512]{1,0:T(8,128)(2,1)S(1)}, u32[]{:S(2)}, u32[]{:S(2)}) collective-permute-start(bf16[384,512]{1,0:T(8,128)(2,1)S(1)} %get-tuple-element.54), channel_id=1, source_target_pairs={{0,4},{4,0},{1,5},{5,1},{2,6},{6,2},{3,7},{7,3},{8,12},{12,8},{9,1... | collective-permute-start | bytes 1179656 | tf_op jit(solution)/shard_map/ppermute | solution.py:322
  39.0 5.6 %collective-permute-start.9 = (f32[8,192]{1,0:T(8,128)S(1)}, f32[8,192]{1,0:T(8,128)S(1)}, u32[]{:S(2)}, u32[]{:S(2)}) collective-permute-start(f32[8,192]{1,0:T(8,128)S(1)} %get-tuple-element.51.pair), channel_id=1, source_target_pairs={{0,1},{1,0},{2,3},{3,2},{4,5},{5,4},{6,7},{7,6},{8,9},{9,8},{10,11... | collective-permute-start | bytes 18440 | tf_op jit(solution)/shard_map/ppermute | solution.py:319
  39.5 10.1 %collective-permute-start.12 = (bf16[192,512]{1,0:T(8,128)(2,1)S(1)}, bf16[192,512]{1,0:T(8,128)(2,1)S(1)}, u32[]{:S(2)}, u32[]{:S(2)}) collective-permute-start(bf16[192,512]{1,0:T(8,128)(2,1)S(1)} %get-tuple-element.55), channel_id=1, source_target_pairs={{0,1},{1,0},{2,3},{3,2},{4,5},{5,4},{6,7},{7,6},{8,9},{9,8},{10,11... | collective-permute-start | bytes 589832 | tf_op jit(solution)/shard_map/ppermute | solution.py:319
  44.7 8.2 %collective-permute-start.16 = (bf16[192,512]{1,0:T(8,128)(2,1)S(1)}, bf16[192,512]{1,0:T(8,128)(2,1)S(1)}, u32[]{:S(2)}, u32[]{:S(2)}) collective-permute-start(bf16[192,512]{1,0:T(8,128)(2,1)S(1)} %get-tuple-element.64), channel_id=1, source_target_pairs={{0,1},{1,0},{2,3},{3,2},{4,5},{5,4},{6,7},{7,6},{8,9},{9,8},{10,11... | collective-permute-start | bytes 589832 | tf_op jit(solution)/shard_map/ppermute | solution.py:319
  44.8 4.8 %collective-permute-start.10 = (f32[8,192]{1,0:T(8,128)S(1)}, f32[8,192]{1,0:T(8,128)S(1)}, u32[]{:S(2)}, u32[]{:S(2)}) collective-permute-start(f32[8,192]{1,0:T(8,128)S(1)} %shard_map.68.half), channel_id=1, source_target_pairs={{0,2},{1,3},{2,0},{3,1},{4,6},{5,7},{6,4},{7,5},{8,10},{9,11},{10,... | collective-permute-start | bytes 18440 | tf_op jit(solution)/shard_map/ppermute | solution.py:319
  47.9 8.5 %collective-permute-start.13 = (bf16[192,512]{1,0:T(8,128)(2,1)S(1)}, bf16[192,512]{1,0:T(8,128)(2,1)S(1)}, u32[]{:S(2)}, u32[]{:S(2)}) collective-permute-start(bf16[192,512]{1,0:T(8,128)(2,1)S(1)} %get-tuple-element.59), channel_id=1, source_target_pairs={{0,4},{4,0},{1,5},{5,1},{2,6},{6,2},{3,7},{7,3},{8,12},{12,8},{9,1... | collective-permute-start | bytes 589832 | tf_op jit(solution)/shard_map/ppermute | solution.py:322
  50.1 9.7 %collective-permute-start.14 = (bf16[192,512]{1,0:T(8,128)(2,1)S(1)}, bf16[192,512]{1,0:T(8,128)(2,1)S(1)}, u32[]{:S(2)}, u32[]{:S(2)}) collective-permute-start(bf16[192,512]{1,0:T(8,128)(2,1)S(1)} %get-tuple-element.60), channel_id=1, source_target_pairs={{0,2},{1,3},{2,0},{3,1},{4,6},{5,7},{6,4},{7,5},{8,10},{9,11},{10,... | collective-permute-start | bytes 589832 | tf_op jit(solution)/shard_map/ppermute | solution.py:319
  53.0 7.0 %collective-permute-start.17 = (bf16[192,512]{1,0:T(8,128)(2,1)S(1)}, bf16[192,512]{1,0:T(8,128)(2,1)S(1)}, u32[]{:S(2)}, u32[]{:S(2)}) collective-permute-start(bf16[192,512]{1,0:T(8,128)(2,1)S(1)} %shard_map.73), channel_id=1, source_target_pairs={{0,4},{4,0},{1,5},{5,1},{2,6},{6,2},{3,7},{7,3},{8,12},{12,8},{9,1... | collective-permute-start | bytes 589832 | tf_op jit(solution)/shard_map/ppermute | solution.py:322
  54.3 6.8 %collective-permute-start.15 = (bf16[192,512]{1,0:T(8,128)(2,1)S(1)}, bf16[192,512]{1,0:T(8,128)(2,1)S(1)}, u32[]{:S(2)}, u32[]{:S(2)}) collective-permute-start(bf16[192,512]{1,0:T(8,128)(2,1)S(1)} %shard_map.72), channel_id=1, source_target_pairs={{0,1},{1,0},{2,3},{3,2},{4,5},{5,4},{6,7},{7,6},{8,9},{9,8},{10,11... | collective-permute-start | bytes 589832 | tf_op jit(solution)/shard_map/ppermute | solution.py:319
  54.7 5.2 %collective-permute-start.18 = (f32[1,192]{1,0:T(1,128)S(1)}, f32[1,192]{1,0:T(1,128)S(1)}, u32[]{:S(2)}, u32[]{:S(2)}) collective-permute-start(f32[1,192]{1,0:T(1,128)S(1)} %get-tuple-element.65.loss), channel_id=1, source_target_pairs={{0,4},{4,0},{1,5},{5,1},{2,6},{6,2},{3,7},{7,3},{8,12},{12,8},{9,1... | collective-permute-start | bytes 2312 | tf_op jit(solution)/shard_map/ppermute | solution.py:322

commit v5 on v4

--- a/solution.py
+++ b/solution.py
@@ -1,3 +1,5 @@
+import functools
+
 import jax
 import jax.numpy as jnp
 from jax import lax
@@ -222,9 +224,10 @@
     others[...] = shifted
 
 
-def rest_kernel(place, kept, others, block0, block21):
-    rows, width = block0.shape
-    for k, out in ((2, block21.at[:rows]), (1, block21.at[rows:]), (0, block0)):
+def rest_kernel(ks, place, kept, others, blocks):
+    rows, width = others.shape[0], blocks.shape[1]
+    for i, k in enumerate(ks):
+        out = blocks.at[i * rows : (i + 1) * rows]
         weights = block(kept, place, k, width)
         out[...] = lax.dot_general(others[...], weights, ROWS_BY_ROWS, preferred_element_type=F32).astype(BF16)
 
@@ -274,7 +277,7 @@
     return by[0] * sums[k] + by[1] * got[...].astype(F32) + by[3] * picked[k].astype(F32)
 
 
-def scale_kernel(scale, pair, half, far, sums, got, relayed, picked, near_picked, loss, columns, second):
+def scale_kernel(scale, pair, half, far, sums, got, relayed, picked, near_picked, loss, columns, second, first):
     rows = second.shape[0]
     top, total, label = join(as_rows(half[...]), as_rows(far[...]))
     loss[...] = jnp.log(total) + top - label
@@ -287,12 +290,7 @@
     here = block_sum(by, sums, got.at[:rows], picked, 2)
     here += by[2] * relayed[...].astype(F32) + by[3] * near_picked[rows:].astype(F32)
     second[...] = here.astype(BF16)
-
-
-def first_kernel(columns, sums, got, picked, out):
-    by = [columns[i][:, :1] for i in range(4)]
-    rows = out.shape[0]
-    out[...] = block_sum(by, sums, got.at[rows:], picked, 1).astype(BF16)
+    first[...] = block_sum(by, sums, got.at[rows:], picked, 1).astype(BF16)
 
 
 def second_kernel(columns, sums, got, picked, second, out):
@@ -383,26 +381,29 @@
     far_rows = call(add_kernel, shape(rows + 32, width, dtype=BF16), [VMEM] * 2, rows2, relayed_rows)
     far_rows = along(far_rows, 2)
     got3 = across(block3)
-    block0, block21 = call(rest_kernel, [piece, two], [SMEM] + [VMEM] * 2, place, kept, others)
+    block21 = call(functools.partial(rest_kernel, (2, 1)), two, [SMEM] + [VMEM] * 2, place, kept, others)
     pair, relayed = call(pair_kernel, [shape(8, rows), piece], [VMEM] * 3, own_stats, got3, sums)
     near = along(pair, 1)
     relayed = along(relayed, 1)
     got21 = across(after(block21, [pair]))
+    block0 = call(
+        functools.partial(rest_kernel, (0,)), piece, [SMEM] + [VMEM] * 2, after(place, [pair]), kept, others
+    )
     half = call(join_kernel, shape(8, rows), [VMEM] * 2, after(pair, [far_rows]), near)
     far = along(half, 2)
-    loss, columns, second = call(
+    loss, columns, second, first = call(
         scale_kernel,
-        [shape(1, rows), shape(4, rows, 128), piece],
+        [shape(1, rows), shape(4, rows, 128), piece, piece],
         [VMEM] * 9,
         scale, pair, half, far, sums, got21, relayed, mine_rows, relayed_rows,
     )
     near_rows = along(after(rows1, [half]), 1)
     second = along(second, 2)
+    first = along(first, 1)
     got0 = across(after(block0, [got21]))
     picked = call(last_rows_kernel, piece, [VMEM] * 3, after(rows0, [got21]), near_rows, far_rows)
     picked = across(picked)
     other_loss = across(loss)
-    first = along(call(first_kernel, piece, [VMEM] * 4, columns, sums, got21, mine_rows), 1)
     total = call(second_kernel, shape(rows, width), [VMEM] * 5, columns, sums, got0, mine_rows, second)
     return call(
         last_kernel, [piece, shape(2 * rows)], [SMEM] + [VMEM] * 6,

time: 62.6 us -> 62.4 us (level)
  waiting for transfers between devices: 14.5 us -> 13.4 us
    ppermute x11, waiting for transfers between devices: 13.7 us -> 12.7 us  [along(): return lax.ppermute(a, 'tensor', partners(tensors, k))]
  transfers between devices with their start and end apart: 19 -> 19, of which waited for: 10 -> 9; matrix products, arithmetic and copies ran while one was open for 0% -> 0% of each run, Pallas kernels for 19% -> 20%
where the time goes in v5:
time: 62.4 us; the launch traced here: 62.3 us
  starting transfers between devices  29.5 us (47%)
  Pallas kernels  18.4 us (29%)
  waiting for transfers between devices  13.4 us (21%)
  between operations  0.82 us (1%)
    ppermute x11, starting transfers between devices, along(): return lax.ppermute(a, 'tensor', partners(tensors, k))  19.3 us
    pallas_call x16, Pallas kernels, call(): pl.pallas_call(kernel, out_shape=outs, in_specs=ins, out_specs=jax.tree.m...  18.4 us
    ppermute x11, waiting for transfers between devices, along(): return lax.ppermute(a, 'tensor', partners(tensors, k))  12.7 us
    ppermute x8, starting transfers between devices, across(): return lax.ppermute(a, 'pipe', [(0, 1), (1, 0)])  10.2 us
  transfers between devices with their start and end apart: 19, of which 9 were waited for; matrix products, arithmetic and copies ran while one was open for 0% of the time, Pallas kernels for 20%

profile of v5, /device:TPU:0, one launch (start us, length us, event | category | flops | bytes accessed | tf_op | source)
XLA Modules:
  0.0 62.3 jit_solution(1806706297792170006)
XLA Ops:
  0.6 0.1 stack.31.place
  0.7 0.0 copy-start.2
  0.7 2.9 %shard_map.59.fetched = bf16[2048,1152]{1,0:T(8,128)(2,1)S(1)} custom-call(s32[7]{0:T(128)S(1)} %stack.31.place, bf16[2048,1152]{1,0:T(8,128)(2,1)} %weight.3), custom_call_target="tpu_custom_call" | custom-call | tf_op jit(solution)/shard_map/pallas_call | solution.py:326
  3.7 4.1 %collective-permute-start.1 = (bf16[192,512]{1,0:T(8,128)(2,1)S(1)}, bf16[192,512]{1,0:T(8,128)(2,1)S(1)}, u32[]{:S(2)}, u32[]{:S(2)}) collective-permute-start(bf16[192,512]{1,0:T(8,128)(2,1)S(1)} %copy-done), channel_id=1, source_target_pairs={{0,2},{1,3},{2,0},{3,1},{4,6},{5,7},{6,4},{7,5},{8,10},{9,11},{10,... | collective-permute-start | bytes 589832 | tf_op jit(solution)/shard_map/ppermute | solution.py:317
  7.8 1.6 %collective-permute-start = (bf16[192,512]{1,0:T(8,128)(2,1)S(1)}, bf16[192,512]{1,0:T(8,128)(2,1)S(1)}, u32[]{:S(2)}, u32[]{:S(2)}) collective-permute-start(bf16[192,512]{1,0:T(8,128)(2,1)S(1)} %copy-done), channel_id=1, source_target_pairs={{0,1},{1,0},{2,3},{3,2},{4,5},{5,4},{6,7},{7,6},{8,9},{9,8},{10,11... | collective-permute-start | bytes 589832 | tf_op jit(solution)/shard_map/ppermute | solution.py:317
  9.3 1.5 %collective-permute-start.4 = (bf16[192,512]{1,0:T(8,128)(2,1)S(1)}, bf16[192,512]{1,0:T(8,128)(2,1)S(1)}, u32[]{:S(2)}, u32[]{:S(2)}) collective-permute-start(bf16[192,512]{1,0:T(8,128)(2,1)S(1)} %copy-done), channel_id=1, source_target_pairs={{0,4},{4,0},{1,5},{5,1},{2,6},{6,2},{3,7},{7,3},{8,12},{12,8},{9,1... | collective-permute-start | bytes 589832 | tf_op jit(solution)/shard_map/ppermute | solution.py:320
  10.8 0.8 %shard_map.60 = (bf16[2048,1152]{1,0:T(8,128)(2,1)S(1)}, s32[192,128]{1,0:T(8,128)S(1)}, s32[192,128]{1,0:T(8,128)S(1)}, f32[1,192]{1,0:T(1,128)S(1)}) custom-call(s32[7]{0:T(128)S(1)} %stack.31.place, bf16[2048,1152]{1,0:T(8,128)(2,1)} %weight.3, s32[384]{0:T(512)S(1)} %copy-done.1, f32[384]{0:T(512)S(1)} %copy-done.2, ...), custom_call_target="tpu_custom_call", output_to_operand_aliasing={{0}: (4, {})} | custom-call | tf_op jit(solution)/shard_map/pallas_call | solution.py:326
  11.7 3.3 %collective-permute-done.1.c.b = bf16[192,512]{1,0:T(8,128)(2,1)S(1)} collective-permute-done((bf16[192,512]{1,0:T(8,128)(2,1)S(1)}, bf16[192,512]{1,0:T(8,128)(2,1)S(1)}, u32[]{:S(2)}, u32[]{:S(2)}) %collective-permute-start.1) | collective-permute-done | bytes 196640 | tf_op jit(solution)/shard_map/ppermute | solution.py:317
  15.0 0.6 collective-permute-start.2
  15.5 0.0 collective-permute-done.b.a
  15.5 0.0 collective-permute-done.4.a
  15.6 1.6 %collective-permute-start.5 = (bf16[384,512]{1,0:T(8,128)(2,1)S(1)}, bf16[384,512]{1,0:T(8,128)(2,1)S(1)}, u32[]{:S(2)}, u32[]{:S(2)}) collective-permute-start(bf16[384,512]{1,0:T(8,128)(2,1)S(1)} %shard_map.63), channel_id=1, source_target_pairs={{0,4},{4,0},{1,5},{5,1},{2,6},{6,2},{3,7},{7,3},{8,12},{12,8},{9,1... | collective-permute-start | bytes 1179656 | tf_op jit(solution)/shard_map/ppermute | solution.py:320
  17.1 2.8 %shard_map.62 = (bf16[3,192,512]{2,1,0:T(8,128)(2,1)S(1)}, bf16[192,512]{1,0:T(8,128)(2,1)S(1)}, bf16[192,512]{1,0:T(8,128)(2,1)S(1)}, bf16[192,512]{1,0:T(8,128)(2,1)S(1)}, bf16[384,512]{1,0:T(8,128)(2,1)S(1)}) custom-call(s32[7]{0:T(128)S(1)} %stack.31.place, bf16[2048,1152]{1,0:T(8,128)(2,1)S(1)} %get-tuple-element.35.kept, ...), custom_call_target="tpu_custom_call" | custom-call | tf_op jit(solution)/shard_map/pallas_call | solution.py:326
  19.9 0.7 %collective-permute-done.2.d = bf16[192,512]{1,0:T(8,128)(2,1)S(1)} collective-permute-done((bf16[192,512]{1,0:T(8,128)(2,1)S(1)}, bf16[192,512]{1,0:T(8,128)(2,1)S(1)}, u32[]{:S(2)}, u32[]{:S(2)}) %collective-permute-start.2) | collective-permute-done | bytes 196640 | tf_op jit(solution)/shard_map/ppermute | solution.py:317
  20.6 0.9 %collective-permute-start.3 = (bf16[384,512]{1,0:T(8,128)(2,1)S(1)}, bf16[384,512]{1,0:T(8,128)(2,1)S(1)}, u32[]{:S(2)}, u32[]{:S(2)}) collective-permute-start(bf16[384,512]{1,0:T(8,128)(2,1)S(1)} %get-tuple-element.43), channel_id=1, source_target_pairs={{0,1},{1,0},{2,3},{3,2},{4,5},{5,4},{6,7},{7,6},{8,9},{9,8},{10,11... | collective-permute-start | bytes 1179656 | tf_op jit(solution)/shard_map/ppermute | solution.py:317
  21.5 1.5 %collective-permute-start.6 = (bf16[192,512]{1,0:T(8,128)(2,1)S(1)}, bf16[192,512]{1,0:T(8,128)(2,1)S(1)}, u32[]{:S(2)}, u32[]{:S(2)}) collective-permute-start(bf16[192,512]{1,0:T(8,128)(2,1)S(1)} %collective-permute-done.2.d), channel_id=1, source_target_pairs={{0,4},{4,0},{1,5},{5,1},{2,6},{6,2},{3,7},{7,3},{8,12},{12,8},{9,1... | collective-permute-start | bytes 589832 | tf_op jit(solution)/shard_map/ppermute | solution.py:320
  23.0 3.6 %shard_map.61 = (f32[8,192]{1,0:T(8,128)S(1)}, f32[4,192,512]{2,1,0:T(8,128)S(1)}) custom-call(s32[7]{0:T(128)S(1)} %stack.31.place, bf16[2048,1152]{1,0:T(8,128)(2,1)S(1)} %get-tuple-element.35.kept, s32[192,128]{1,0:T(8,128)S(1)} %get-tuple-element.36.targets.mine, bf16[192,512]{1,0:T(8,128)(2,1)S(1)} %copy-done, ...), custom_call_target="tpu_custom_call" | custom-call | tf_op jit(solution)/shard_map/pallas_call | solution.py:326
  26.6 0.6 collective-permute-done.5.bc
  27.2 1.5 %shard_map.64.partial = f32[192,1152]{1,0:T(8,128)S(1)} custom-call(s32[7]{0:T(128)S(1)} %stack.31.place, bf16[2048,1152]{1,0:T(8,128)(2,1)S(1)} %get-tuple-element.35.kept, bf16[192,512]{1,0:T(8,128)(2,1)S(1)} %collective-permute-done.4.a, bf16[384,512]{1,0:T(8,128)(2,1)S(1)} %collective-permute-done.5.bc), custom_call_target="tpu_custom_call" | custom-call | tf_op jit(solution)/shard_map/pallas_call | solution.py:326
  28.7 0.5 collective-permute-done.3.b.near_picked
  29.2 0.1 collective-permute-done.6.d
  29.3 1.8 %shard_map.65 = (bf16[208,512]{1,0:T(8,128)(2,1)S(1)}, bf16[192,1152]{1,0:T(8,128)(2,1)S(1)}) custom-call(s32[7]{0:T(128)S(1)} %stack.31.place, bf16[2048,1152]{1,0:T(8,128)(2,1)S(1)} %get-tuple-element.35.kept, s32[192,128]{1,0:T(8,128)S(1)} %get-tuple-element.44.other.targets, f32[192,1152]{1,0:T(8,128)S(1)} %shard_map.64.partial, ...), custom_call_target="tpu_custom_call" | custom-call | tf_op jit(solution)/shard_map/pallas_call | solution.py:326
  31.1 1.5 %collective-permute-start.7 = (bf16[208,512]{1,0:T(8,128)(2,1)S(1)}, bf16[208,512]{1,0:T(8,128)(2,1)S(1)}, u32[]{:S(2)}, u32[]{:S(2)}) collective-permute-start(bf16[208,512]{1,0:T(8,128)(2,1)S(1)} %get-tuple-element.47), channel_id=1, source_target_pairs={{0,4},{4,0},{1,5},{5,1},{2,6},{6,2},{3,7},{7,3},{8,12},{12,8},{9,1... | collective-permute-start | bytes 638984 | tf_op jit(solution)/shard_map/ppermute | solution.py:320
  32.7 3.6 %collective-permute-start.8 = (bf16[224,512]{1,0:T(8,128)(2,1)S(1)}, bf16[224,512]{1,0:T(8,128)(2,1)S(1)}, u32[]{:S(2)}, u32[]{:S(2)}) collective-permute-start(bf16[224,512]{1,0:T(8,128)(2,1)S(1)} %shard_map.67), channel_id=1, source_target_pairs={{0,2},{1,3},{2,0},{3,1},{4,6},{5,7},{6,4},{7,5},{8,10},{9,11},{10,... | collective-permute-start | bytes 688136 | tf_op jit(solution)/shard_map/ppermute | solution.py:317
  36.3 1.5 %shard_map.69 = bf16[384,512]{1,0:T(8,128)(2,1)S(1)} custom-call(s32[7]{0:T(128)S(1)} %stack.31.place, bf16[2048,1152]{1,0:T(8,128)(2,1)S(1)} %get-tuple-element.35.kept, bf16[192,1152]{1,0:T(8,128)(2,1)S(1)} %get-tuple-element.52.others), custom_call_target="tpu_custom_call" | custom-call | tf_op jit(solution)/shard_map/pallas_call | solution.py:326
  37.8 0.0 collective-permute-done.7.got
  37.8 0.3 shard_map.66
  38.1 0.8 %collective-permute-start.11 = (bf16[384,512]{1,0:T(8,128)(2,1)S(1)}, bf16[384,512]{1,0:T(8,128)(2,1)S(1)}, u32[]{:S(2)}, u32[]{:S(2)}) collective-permute-start(bf16[384,512]{1,0:T(8,128)(2,1)S(1)} %shard_map.69), channel_id=1, source_target_pairs={{0,4},{4,0},{1,5},{5,1},{2,6},{6,2},{3,7},{7,3},{8,12},{12,8},{9,1... | collective-permute-start | bytes 1179656 | tf_op jit(solution)/shard_map/ppermute | solution.py:320
  38.9 0.5 collective-permute-start.9
  39.4 1.6 %collective-permute-start.12 = (bf16[192,512]{1,0:T(8,128)(2,1)S(1)}, bf16[192,512]{1,0:T(8,128)(2,1)S(1)}, u32[]{:S(2)}, u32[]{:S(2)}) collective-permute-start(bf16[192,512]{1,0:T(8,128)(2,1)S(1)} %get-tuple-element.54), channel_id=1, source_target_pairs={{0,1},{1,0},{2,3},{3,2},{4,5},{5,4},{6,7},{7,6},{8,9},{9,8},{10,11... | collective-permute-start | bytes 589832 | tf_op jit(solution)/shard_map/ppermute | solution.py:317
  40.9 3.5 %collective-permute-done.8.c = bf16[224,512]{1,0:T(8,128)(2,1)S(1)} collective-permute-done((bf16[224,512]{1,0:T(8,128)(2,1)S(1)}, bf16[224,512]{1,0:T(8,128)(2,1)S(1)}, u32[]{:S(2)}, u32[]{:S(2)}) %collective-permute-start.8) | collective-permute-done | bytes 229408 | tf_op jit(solution)/shard_map/ppermute | solution.py:317
  44.4 0.2 collective-permute-done.9.got
  44.6 0.1 collective-permute-start.16
  44.7 3.0 %collective-permute-start.10 = (f32[8,192]{1,0:T(8,128)S(1)}, f32[8,192]{1,0:T(8,128)S(1)}, u32[]{:S(2)}, u32[]{:S(2)}) collective-permute-start(f32[8,192]{1,0:T(8,128)S(1)} %shard_map.68.half), channel_id=1, source_target_pairs={{0,2},{1,3},{2,0},{3,1},{4,6},{5,7},{6,4},{7,5},{8,10},{9,11},{10,... | collective-permute-start | bytes 18440 | tf_op jit(solution)/shard_map/ppermute | solution.py:317
  47.8 1.1 %shard_map.71 = bf16[192,512]{1,0:T(8,128)(2,1)S(1)} custom-call(s32[7]{0:T(128)S(1)} %stack.31.place, bf16[2048,1152]{1,0:T(8,128)(2,1)S(1)} %get-tuple-element.35.kept, bf16[192,1152]{1,0:T(8,128)(2,1)S(1)} %get-tuple-element.52.others), custom_call_target="tpu_custom_call" | custom-call | tf_op jit(solution)/shard_map/pallas_call | solution.py:326
  48.9 0.8 %collective-permute-start.13 = (bf16[192,512]{1,0:T(8,128)(2,1)S(1)}, bf16[192,512]{1,0:T(8,128)(2,1)S(1)}, u32[]{:S(2)}, u32[]{:S(2)}) collective-permute-start(bf16[192,512]{1,0:T(8,128)(2,1)S(1)} %shard_map.71), channel_id=1, source_target_pairs={{0,4},{4,0},{1,5},{5,1},{2,6},{6,2},{3,7},{7,3},{8,12},{12,8},{9,1... | collective-permute-start | bytes 589832 | tf_op jit(solution)/shard_map/ppermute | solution.py:320
  49.7 0.5 shard_map.70
  50.2 2.7 %collective-permute-start.14 = (bf16[192,512]{1,0:T(8,128)(2,1)S(1)}, bf16[192,512]{1,0:T(8,128)(2,1)S(1)}, u32[]{:S(2)}, u32[]{:S(2)}) collective-permute-start(bf16[192,512]{1,0:T(8,128)(2,1)S(1)} %get-tuple-element.59), channel_id=1, source_target_pairs={{0,2},{1,3},{2,0},{3,1},{4,6},{5,7},{6,4},{7,5},{8,10},{9,11},{10,... | collective-permute-start | bytes 589832 | tf_op jit(solution)/shard_map/ppermute | solution.py:317
  52.9 0.0 collective-permute-done.16.b
  52.9 0.9 %collective-permute-start.17 = (bf16[192,512]{1,0:T(8,128)(2,1)S(1)}, bf16[192,512]{1,0:T(8,128)(2,1)S(1)}, u32[]{:S(2)}, u32[]{:S(2)}) collective-permute-start(bf16[192,512]{1,0:T(8,128)(2,1)S(1)} %shard_map.73), channel_id=1, source_target_pairs={{0,4},{4,0},{1,5},{5,1},{2,6},{6,2},{3,7},{7,3},{8,12},{12,8},{9,1... | collective-permute-start | bytes 589832 | tf_op jit(solution)/shard_map/ppermute | solution.py:320
  53.8 0.7 %collective-permute-start.15 = (bf16[192,512]{1,0:T(8,128)(2,1)S(1)}, bf16[192,512]{1,0:T(8,128)(2,1)S(1)}, u32[]{:S(2)}, u32[]{:S(2)}) collective-permute-start(bf16[192,512]{1,0:T(8,128)(2,1)S(1)} %get-tuple-element.60), channel_id=1, source_target_pairs={{0,1},{1,0},{2,3},{3,2},{4,5},{5,4},{6,7},{7,6},{8,9},{9,8},{10,11... | collective-permute-start | bytes 589832 | tf_op jit(solution)/shard_map/ppermute | solution.py:317
  54.6 1.6 %collective-permute-start.18 = (f32[1,192]{1,0:T(1,128)S(1)}, f32[1,192]{1,0:T(1,128)S(1)}, u32[]{:S(2)}, u32[]{:S(2)}) collective-permute-start(f32[1,192]{1,0:T(1,128)S(1)} %get-tuple-element.65.loss), channel_id=1, source_target_pairs={{0,4},{4,0},{1,5},{5,1},{2,6},{6,2},{3,7},{7,3},{8,12},{12,8},{9,1... | collective-permute-start | bytes 2312 | tf_op jit(solution)/shard_map/ppermute | solution.py:320
  56.1 3.5 %collective-permute-done.14.second = bf16[192,512]{1,0:T(8,128)(2,1)S(1)} collective-permute-done((bf16[192,512]{1,0:T(8,128)(2,1)S(1)}, bf16[192,512]{1,0:T(8,128)(2,1)S(1)}, u32[]{:S(2)}, u32[]{:S(2)}) %collective-permute-start.14) | collective-permute-done | bytes 196640 | tf_op jit(solution)/shard_map/ppermute | solution.py:317
  59.6 0.2 shard_map.72.partial
  59.8 0.0 collective-permute-done.18.other_loss
  59.9 0.0 collective-permute-done.17.theirs
  59.9 1.1 %collective-permute-done.15.first = bf16[192,512]{1,0:T(8,128)(2,1)S(1)} collective-permute-done((bf16[192,512]{1,0:T(8,128)(2,1)S(1)}, bf16[192,512]{1,0:T(8,128)(2,1)S(1)}, u32[]{:S(2)}, u32[]{:S(2)}) %collective-permute-start.15) | collective-permute-done | bytes 196640 | tf_op jit(solution)/shard_map/ppermute | solution.py:317
  60.9 1.3 %shard_map.74 = (bf16[192,512]{1,0:T(8,128)(2,1)}, f32[384]{0:T(512)}) custom-call(s32[7]{0:T(128)S(1)} %stack.31.place, f32[4,192,128]{2,1,0:T(8,128)S(1)} %get-tuple-element.56.columns, f32[192,512]{1,0:T(8,128)S(1)} %shard_map.72.partial, bf16[192,512]{1,0:T(8,128)(2,1)S(1)} %collective-permute-done.15.first, ...), custom_call_target="tpu_custom_call" | custom-call | tf_op jit(solution)/shard_map/pallas_call | solution.py:326
  (13 shorter events, 0.1 us)
Async XLA Ops:
  0.7 2.9 %copy-start = (bf16[192,512]{1,0:T(8,128)(2,1)S(1)}, bf16[192,512]{1,0:T(8,128)(2,1)}, u32[]{:S(2)}) copy-start(bf16[192,512]{1,0:T(8,128)(2,1)} %a) | copy-start | bytes 589828
  0.7 10.1 %copy-start.1 = (s32[384]{0:T(512)S(1)}, s32[384]{0:T(512)}, u32[]{:S(2)}) copy-start(s32[384]{0:T(512)} %targets.1) | copy-start | bytes 4612
  0.7 10.1 %copy-start.2 = (f32[384]{0:T(512)S(1)}, f32[384]{0:T(512)}, u32[]{:S(2)}) copy-start(f32[384]{0:T(512)} %scale.1) | copy-start | bytes 4612
  3.7 11.3 %collective-permute-start.1 = (bf16[192,512]{1,0:T(8,128)(2,1)S(1)}, bf16[192,512]{1,0:T(8,128)(2,1)S(1)}, u32[]{:S(2)}, u32[]{:S(2)}) collective-permute-start(bf16[192,512]{1,0:T(8,128)(2,1)S(1)} %copy-done), channel_id=1, source_target_pairs={{0,2},{1,3},{2,0},{3,1},{4,6},{5,7},{6,4},{7,5},{8,10},{9,11},{10,... | collective-permute-start | bytes 589832 | tf_op jit(solution)/shard_map/ppermute | solution.py:317
  7.8 7.8 %collective-permute-start = (bf16[192,512]{1,0:T(8,128)(2,1)S(1)}, bf16[192,512]{1,0:T(8,128)(2,1)S(1)}, u32[]{:S(2)}, u32[]{:S(2)}) collective-permute-start(bf16[192,512]{1,0:T(8,128)(2,1)S(1)} %copy-done), channel_id=1, source_target_pairs={{0,1},{1,0},{2,3},{3,2},{4,5},{5,4},{6,7},{7,6},{8,9},{9,8},{10,11... | collective-permute-start | bytes 589832 | tf_op jit(solution)/shard_map/ppermute | solution.py:317
  9.3 6.2 %collective-permute-start.4 = (bf16[192,512]{1,0:T(8,128)(2,1)S(1)}, bf16[192,512]{1,0:T(8,128)(2,1)S(1)}, u32[]{:S(2)}, u32[]{:S(2)}) collective-permute-start(bf16[192,512]{1,0:T(8,128)(2,1)S(1)} %copy-done), channel_id=1, source_target_pairs={{0,4},{4,0},{1,5},{5,1},{2,6},{6,2},{3,7},{7,3},{8,12},{12,8},{9,1... | collective-permute-start | bytes 589832 | tf_op jit(solution)/shard_map/ppermute | solution.py:320
  15.0 5.7 %collective-permute-start.2 = (bf16[192,512]{1,0:T(8,128)(2,1)S(1)}, bf16[192,512]{1,0:T(8,128)(2,1)S(1)}, u32[]{:S(2)}, u32[]{:S(2)}) collective-permute-start(bf16[192,512]{1,0:T(8,128)(2,1)S(1)} %collective-permute-done.1.c.b), channel_id=1, source_target_pairs={{0,1},{1,0},{2,3},{3,2},{4,5},{5,4},{6,7},{7,6},{8,9},{9,8},{10,11... | collective-permute-start | bytes 589832 | tf_op jit(solution)/shard_map/ppermute | solution.py:317
  15.6 11.6 %collective-permute-start.5 = (bf16[384,512]{1,0:T(8,128)(2,1)S(1)}, bf16[384,512]{1,0:T(8,128)(2,1)S(1)}, u32[]{:S(2)}, u32[]{:S(2)}) collective-permute-start(bf16[384,512]{1,0:T(8,128)(2,1)S(1)} %shard_map.63), channel_id=1, source_target_pairs={{0,4},{4,0},{1,5},{5,1},{2,6},{6,2},{3,7},{7,3},{8,12},{12,8},{9,1... | collective-permute-start | bytes 1179656 | tf_op jit(solution)/shard_map/ppermute | solution.py:320
  20.6 8.6 %collective-permute-start.3 = (bf16[384,512]{1,0:T(8,128)(2,1)S(1)}, bf16[384,512]{1,0:T(8,128)(2,1)S(1)}, u32[]{:S(2)}, u32[]{:S(2)}) collective-permute-start(bf16[384,512]{1,0:T(8,128)(2,1)S(1)} %get-tuple-element.43), channel_id=1, source_target_pairs={{0,1},{1,0},{2,3},{3,2},{4,5},{5,4},{6,7},{7,6},{8,9},{9,8},{10,11... | collective-permute-start | bytes 1179656 | tf_op jit(solution)/shard_map/ppermute | solution.py:317
  21.5 7.8 %collective-permute-start.6 = (bf16[192,512]{1,0:T(8,128)(2,1)S(1)}, bf16[192,512]{1,0:T(8,128)(2,1)S(1)}, u32[]{:S(2)}, u32[]{:S(2)}) collective-permute-start(bf16[192,512]{1,0:T(8,128)(2,1)S(1)} %collective-permute-done.2.d), channel_id=1, source_target_pairs={{0,4},{4,0},{1,5},{5,1},{2,6},{6,2},{3,7},{7,3},{8,12},{12,8},{9,1... | collective-permute-start | bytes 589832 | tf_op jit(solution)/shard_map/ppermute | solution.py:320
  31.1 6.7 %collective-permute-start.7 = (bf16[208,512]{1,0:T(8,128)(2,1)S(1)}, bf16[208,512]{1,0:T(8,128)(2,1)S(1)}, u32[]{:S(2)}, u32[]{:S(2)}) collective-permute-start(bf16[208,512]{1,0:T(8,128)(2,1)S(1)} %get-tuple-element.47), channel_id=1, source_target_pairs={{0,4},{4,0},{1,5},{5,1},{2,6},{6,2},{3,7},{7,3},{8,12},{12,8},{9,1... | collective-permute-start | bytes 638984 | tf_op jit(solution)/shard_map/ppermute | solution.py:320
  32.7 11.8 %collective-permute-start.8 = (bf16[224,512]{1,0:T(8,128)(2,1)S(1)}, bf16[224,512]{1,0:T(8,128)(2,1)S(1)}, u32[]{:S(2)}, u32[]{:S(2)}) collective-permute-start(bf16[224,512]{1,0:T(8,128)(2,1)S(1)} %shard_map.67), channel_id=1, source_target_pairs={{0,2},{1,3},{2,0},{3,1},{4,6},{5,7},{6,4},{7,5},{8,10},{9,11},{10,... | collective-permute-start | bytes 688136 | tf_op jit(solution)/shard_map/ppermute | solution.py:317
  38.1 10.8 %collective-permute-start.11 = (bf16[384,512]{1,0:T(8,128)(2,1)S(1)}, bf16[384,512]{1,0:T(8,128)(2,1)S(1)}, u32[]{:S(2)}, u32[]{:S(2)}) collective-permute-start(bf16[384,512]{1,0:T(8,128)(2,1)S(1)} %shard_map.69), channel_id=1, source_target_pairs={{0,4},{4,0},{1,5},{5,1},{2,6},{6,2},{3,7},{7,3},{8,12},{12,8},{9,1... | collective-permute-start | bytes 1179656 | tf_op jit(solution)/shard_map/ppermute | solution.py:320
  38.9 5.7 %collective-permute-start.9 = (f32[8,192]{1,0:T(8,128)S(1)}, f32[8,192]{1,0:T(8,128)S(1)}, u32[]{:S(2)}, u32[]{:S(2)}) collective-permute-start(f32[8,192]{1,0:T(8,128)S(1)} %get-tuple-element.51.pair), channel_id=1, source_target_pairs={{0,1},{1,0},{2,3},{3,2},{4,5},{5,4},{6,7},{7,6},{8,9},{9,8},{10,11... | collective-permute-start | bytes 18440 | tf_op jit(solution)/shard_map/ppermute | solution.py:317
  39.4 10.3 %collective-permute-start.12 = (bf16[192,512]{1,0:T(8,128)(2,1)S(1)}, bf16[192,512]{1,0:T(8,128)(2,1)S(1)}, u32[]{:S(2)}, u32[]{:S(2)}) collective-permute-start(bf16[192,512]{1,0:T(8,128)(2,1)S(1)} %get-tuple-element.54), channel_id=1, source_target_pairs={{0,1},{1,0},{2,3},{3,2},{4,5},{5,4},{6,7},{7,6},{8,9},{9,8},{10,11... | collective-permute-start | bytes 589832 | tf_op jit(solution)/shard_map/ppermute | solution.py:317
  44.6 8.3 %collective-permute-start.16 = (bf16[192,512]{1,0:T(8,128)(2,1)S(1)}, bf16[192,512]{1,0:T(8,128)(2,1)S(1)}, u32[]{:S(2)}, u32[]{:S(2)}) collective-permute-start(bf16[192,512]{1,0:T(8,128)(2,1)S(1)} %get-tuple-element.64), channel_id=1, source_target_pairs={{0,1},{1,0},{2,3},{3,2},{4,5},{5,4},{6,7},{7,6},{8,9},{9,8},{10,11... | collective-permute-start | bytes 589832 | tf_op jit(solution)/shard_map/ppermute | solution.py:317
  44.7 5.0 %collective-permute-start.10 = (f32[8,192]{1,0:T(8,128)S(1)}, f32[8,192]{1,0:T(8,128)S(1)}, u32[]{:S(2)}, u32[]{:S(2)}) collective-permute-start(f32[8,192]{1,0:T(8,128)S(1)} %shard_map.68.half), channel_id=1, source_target_pairs={{0,2},{1,3},{2,0},{3,1},{4,6},{5,7},{6,4},{7,5},{8,10},{9,11},{10,... | collective-permute-start | bytes 18440 | tf_op jit(solution)/shard_map/ppermute | solution.py:317
  48.9 7.3 %collective-permute-start.13 = (bf16[192,512]{1,0:T(8,128)(2,1)S(1)}, bf16[192,512]{1,0:T(8,128)(2,1)S(1)}, u32[]{:S(2)}, u32[]{:S(2)}) collective-permute-start(bf16[192,512]{1,0:T(8,128)(2,1)S(1)} %shard_map.71), channel_id=1, source_target_pairs={{0,4},{4,0},{1,5},{5,1},{2,6},{6,2},{3,7},{7,3},{8,12},{12,8},{9,1... | collective-permute-start | bytes 589832 | tf_op jit(solution)/shard_map/ppermute | solution.py:320
  50.2 9.4 %collective-permute-start.14 = (bf16[192,512]{1,0:T(8,128)(2,1)S(1)}, bf16[192,512]{1,0:T(8,128)(2,1)S(1)}, u32[]{:S(2)}, u32[]{:S(2)}) collective-permute-start(bf16[192,512]{1,0:T(8,128)(2,1)S(1)} %get-tuple-element.59), channel_id=1, source_target_pairs={{0,2},{1,3},{2,0},{3,1},{4,6},{5,7},{6,4},{7,5},{8,10},{9,11},{10,... | collective-permute-start | bytes 589832 | tf_op jit(solution)/shard_map/ppermute | solution.py:317
  52.9 6.9 %collective-permute-start.17 = (bf16[192,512]{1,0:T(8,128)(2,1)S(1)}, bf16[192,512]{1,0:T(8,128)(2,1)S(1)}, u32[]{:S(2)}, u32[]{:S(2)}) collective-permute-start(bf16[192,512]{1,0:T(8,128)(2,1)S(1)} %shard_map.73), channel_id=1, source_target_pairs={{0,4},{4,0},{1,5},{5,1},{2,6},{6,2},{3,7},{7,3},{8,12},{12,8},{9,1... | collective-permute-start | bytes 589832 | tf_op jit(solution)/shard_map/ppermute | solution.py:320
  53.8 7.1 %collective-permute-start.15 = (bf16[192,512]{1,0:T(8,128)(2,1)S(1)}, bf16[192,512]{1,0:T(8,128)(2,1)S(1)}, u32[]{:S(2)}, u32[]{:S(2)}) collective-permute-start(bf16[192,512]{1,0:T(8,128)(2,1)S(1)} %get-tuple-element.60), channel_id=1, source_target_pairs={{0,1},{1,0},{2,3},{3,2},{4,5},{5,4},{6,7},{7,6},{8,9},{9,8},{10,11... | collective-permute-start | bytes 589832 | tf_op jit(solution)/shard_map/ppermute | solution.py:317
  54.6 5.3 %collective-permute-start.18 = (f32[1,192]{1,0:T(1,128)S(1)}, f32[1,192]{1,0:T(1,128)S(1)}, u32[]{:S(2)}, u32[]{:S(2)}) collective-permute-start(f32[1,192]{1,0:T(1,128)S(1)} %get-tuple-element.65.loss), channel_id=1, source_target_pairs={{0,4},{4,0},{1,5},{5,1},{2,6},{6,2},{3,7},{7,3},{8,12},{12,8},{9,1... | collective-permute-start | bytes 2312 | tf_op jit(solution)/shard_map/ppermute | solution.py:320

commit v6 on v5

--- a/solution.py
+++ b/solution.py
@@ -293,18 +293,18 @@
     first[...] = block_sum(by, sums, got.at[rows:], picked, 1).astype(BF16)
 
 
-def second_kernel(columns, sums, got, picked, second, out):
+def second_kernel(place, columns, sums, got, picked, second, loss, other_loss, out, row_loss):
     by = [columns[i][:, :1] for i in range(4)]
     out[...] = block_sum(by, sums, got, picked, 0) + second[...].astype(F32)
-
-
-def last_kernel(place, columns, partial, first, theirs, loss, other_loss, out, row_loss):
-    here = partial[...] + first[...].astype(F32) + columns[3][:, :1] * theirs[...].astype(F32)
-    out[...] = here.astype(BF16)
     rows = out.shape[0]
     lower = place[5] == 0
     row_loss[:rows] = jnp.where(lower, loss[...], other_loss[...])[0]
     row_loss[rows:] = jnp.where(lower, other_loss[...], loss[...])[0]
+
+
+def last_kernel(columns, partial, first, theirs, out):
+    here = partial[...] + first[...].astype(F32) + columns[3][:, :1] * theirs[...].astype(F32)
+    out[...] = here.astype(BF16)
 
 
 def two_by_four(hidden, weight, targets, row_weight):
@@ -404,11 +404,11 @@
     picked = call(last_rows_kernel, piece, [VMEM] * 3, after(rows0, [got21]), near_rows, far_rows)
     picked = across(picked)
     other_loss = across(loss)
-    total = call(second_kernel, shape(rows, width), [VMEM] * 5, columns, sums, got0, mine_rows, second)
-    return call(
-        last_kernel, [piece, shape(2 * rows)], [SMEM] + [VMEM] * 6,
-        place, columns, total, first, picked, loss, other_loss,
-    )
+    total, row_loss = call(
+        second_kernel, [shape(rows, width), shape(2 * rows)], [SMEM] + [VMEM] * 7,
+        place, columns, sums, got0, mine_rows, second, loss, other_loss,
+    )
+    return call(last_kernel, piece, [VMEM] * 4, columns, total, first, picked), row_loss
 
 
 def per_device(hidden, weight, targets, row_weight):

time: 62.4 us -> 61.8 us (level)
  waiting for transfers between devices: 13.4 us -> 12.3 us
    ppermute x11, waiting for transfers between devices: 12.7 us -> 8.84 us  [along(): return lax.ppermute(a, 'tensor', partners(tensors, k))]
    ppermute x8, waiting for transfers between devices: 0.73 us -> 3.49 us  [across(): return lax.ppermute(a, 'pipe', [(0, 1), (1, 0)])]
  transfers between devices with their start and end apart: 19 -> 19, of which waited for: 9 -> 9; matrix products, arithmetic and copies ran while one was open for 0% -> 0% of each run, Pallas kernels for 20% -> 22%
where the time goes in v6:
time: 61.8 us; the launch traced here: 61.7 us
  starting transfers between devices  29.5 us (48%)
  Pallas kernels  18.9 us (31%)
  waiting for transfers between devices  12.3 us (20%)
  between operations  0.8 us (1%)
    ppermute x11, starting transfers between devices, along(): return lax.ppermute(a, 'tensor', partners(tensors, k))  19.3 us
    pallas_call x16, Pallas kernels, call(): pl.pallas_call(kernel, out_shape=outs, in_specs=ins, out_specs=jax.tree.m...  18.9 us
    ppermute x8, starting transfers between devices, across(): return lax.ppermute(a, 'pipe', [(0, 1), (1, 0)])  10.2 us
    ppermute x11, waiting for transfers between devices, along(): return lax.ppermute(a, 'tensor', partners(tensors, k))  8.84 us
    ppermute x8, waiting for transfers between devices, across(): return lax.ppermute(a, 'pipe', [(0, 1), (1, 0)])  3.49 us
  transfers between devices with their start and end apart: 19, of which 9 were waited for; matrix products, arithmetic and copies ran while one was open for 0% of the time, Pallas kernels for 22%

profile of v6, /device:TPU:0, one launch (start us, length us, event | category | flops | bytes accessed | tf_op | source)
XLA Modules:
  0.0 61.7 jit_solution(10972481495730666322)
XLA Ops:
  0.6 0.1 stack.31.place
  0.7 0.0 copy-start.2
  0.7 2.9 %shard_map.59.fetched = bf16[2048,1152]{1,0:T(8,128)(2,1)S(1)} custom-call(s32[7]{0:T(128)S(1)} %stack.31.place, bf16[2048,1152]{1,0:T(8,128)(2,1)} %weight.3), custom_call_target="tpu_custom_call" | custom-call | tf_op jit(solution)/shard_map/pallas_call | solution.py:326
  3.7 4.1 %collective-permute-start.1 = (bf16[192,512]{1,0:T(8,128)(2,1)S(1)}, bf16[192,512]{1,0:T(8,128)(2,1)S(1)}, u32[]{:S(2)}, u32[]{:S(2)}) collective-permute-start(bf16[192,512]{1,0:T(8,128)(2,1)S(1)} %copy-done), channel_id=1, source_target_pairs={{0,2},{1,3},{2,0},{3,1},{4,6},{5,7},{6,4},{7,5},{8,10},{9,11},{10,... | collective-permute-start | bytes 589832 | tf_op jit(solution)/shard_map/ppermute | solution.py:317
  7.8 1.6 %collective-permute-start = (bf16[192,512]{1,0:T(8,128)(2,1)S(1)}, bf16[192,512]{1,0:T(8,128)(2,1)S(1)}, u32[]{:S(2)}, u32[]{:S(2)}) collective-permute-start(bf16[192,512]{1,0:T(8,128)(2,1)S(1)} %copy-done), channel_id=1, source_target_pairs={{0,1},{1,0},{2,3},{3,2},{4,5},{5,4},{6,7},{7,6},{8,9},{9,8},{10,11... | collective-permute-start | bytes 589832 | tf_op jit(solution)/shard_map/ppermute | solution.py:317
  9.3 1.5 %collective-permute-start.4 = (bf16[192,512]{1,0:T(8,128)(2,1)S(1)}, bf16[192,512]{1,0:T(8,128)(2,1)S(1)}, u32[]{:S(2)}, u32[]{:S(2)}) collective-permute-start(bf16[192,512]{1,0:T(8,128)(2,1)S(1)} %copy-done), channel_id=1, source_target_pairs={{0,4},{4,0},{1,5},{5,1},{2,6},{6,2},{3,7},{7,3},{8,12},{12,8},{9,1... | collective-permute-start | bytes 589832 | tf_op jit(solution)/shard_map/ppermute | solution.py:320
  10.8 0.8 %shard_map.60 = (bf16[2048,1152]{1,0:T(8,128)(2,1)S(1)}, s32[192,128]{1,0:T(8,128)S(1)}, s32[192,128]{1,0:T(8,128)S(1)}, f32[1,192]{1,0:T(1,128)S(1)}) custom-call(s32[7]{0:T(128)S(1)} %stack.31.place, bf16[2048,1152]{1,0:T(8,128)(2,1)} %weight.3, s32[384]{0:T(512)S(1)} %copy-done.1, f32[384]{0:T(512)S(1)} %copy-done.2, ...), custom_call_target="tpu_custom_call", output_to_operand_aliasing={{0}: (4, {})} | custom-call | tf_op jit(solution)/shard_map/pallas_call | solution.py:326
  11.7 3.3 %collective-permute-done.1.c.b = bf16[192,512]{1,0:T(8,128)(2,1)S(1)} collective-permute-done((bf16[192,512]{1,0:T(8,128)(2,1)S(1)}, bf16[192,512]{1,0:T(8,128)(2,1)S(1)}, u32[]{:S(2)}, u32[]{:S(2)}) %collective-permute-start.1) | collective-permute-done | bytes 196640 | tf_op jit(solution)/shard_map/ppermute | solution.py:317
  15.0 0.6 collective-permute-start.2
  15.5 0.0 collective-permute-done.b.a
  15.5 0.0 collective-permute-done.4.a
  15.6 1.6 %collective-permute-start.5 = (bf16[384,512]{1,0:T(8,128)(2,1)S(1)}, bf16[384,512]{1,0:T(8,128)(2,1)S(1)}, u32[]{:S(2)}, u32[]{:S(2)}) collective-permute-start(bf16[384,512]{1,0:T(8,128)(2,1)S(1)} %shard_map.63), channel_id=1, source_target_pairs={{0,4},{4,0},{1,5},{5,1},{2,6},{6,2},{3,7},{7,3},{8,12},{12,8},{9,1... | collective-permute-start | bytes 1179656 | tf_op jit(solution)/shard_map/ppermute | solution.py:320
  17.1 2.8 %shard_map.62 = (bf16[3,192,512]{2,1,0:T(8,128)(2,1)S(1)}, bf16[192,512]{1,0:T(8,128)(2,1)S(1)}, bf16[192,512]{1,0:T(8,128)(2,1)S(1)}, bf16[192,512]{1,0:T(8,128)(2,1)S(1)}, bf16[384,512]{1,0:T(8,128)(2,1)S(1)}) custom-call(s32[7]{0:T(128)S(1)} %stack.31.place, bf16[2048,1152]{1,0:T(8,128)(2,1)S(1)} %get-tuple-element.37.kept, ...), custom_call_target="tpu_custom_call" | custom-call | tf_op jit(solution)/shard_map/pallas_call | solution.py:326
  19.9 0.7 %collective-permute-done.2.d = bf16[192,512]{1,0:T(8,128)(2,1)S(1)} collective-permute-done((bf16[192,512]{1,0:T(8,128)(2,1)S(1)}, bf16[192,512]{1,0:T(8,128)(2,1)S(1)}, u32[]{:S(2)}, u32[]{:S(2)}) %collective-permute-start.2) | collective-permute-done | bytes 196640 | tf_op jit(solution)/shard_map/ppermute | solution.py:317
  20.6 0.9 %collective-permute-start.3 = (bf16[384,512]{1,0:T(8,128)(2,1)S(1)}, bf16[384,512]{1,0:T(8,128)(2,1)S(1)}, u32[]{:S(2)}, u32[]{:S(2)}) collective-permute-start(bf16[384,512]{1,0:T(8,128)(2,1)S(1)} %get-tuple-element.45), channel_id=1, source_target_pairs={{0,1},{1,0},{2,3},{3,2},{4,5},{5,4},{6,7},{7,6},{8,9},{9,8},{10,11... | collective-permute-start | bytes 1179656 | tf_op jit(solution)/shard_map/ppermute | solution.py:317
  21.5 1.5 %collective-permute-start.6 = (bf16[192,512]{1,0:T(8,128)(2,1)S(1)}, bf16[192,512]{1,0:T(8,128)(2,1)S(1)}, u32[]{:S(2)}, u32[]{:S(2)}) collective-permute-start(bf16[192,512]{1,0:T(8,128)(2,1)S(1)} %collective-permute-done.2.d), channel_id=1, source_target_pairs={{0,4},{4,0},{1,5},{5,1},{2,6},{6,2},{3,7},{7,3},{8,12},{12,8},{9,1... | collective-permute-start | bytes 589832 | tf_op jit(solution)/shard_map/ppermute | solution.py:320
  23.0 3.6 %shard_map.61 = (f32[8,192]{1,0:T(8,128)S(1)}, f32[4,192,512]{2,1,0:T(8,128)S(1)}) custom-call(s32[7]{0:T(128)S(1)} %stack.31.place, bf16[2048,1152]{1,0:T(8,128)(2,1)S(1)} %get-tuple-element.37.kept, s32[192,128]{1,0:T(8,128)S(1)} %get-tuple-element.38.targets.mine, bf16[192,512]{1,0:T(8,128)(2,1)S(1)} %copy-done, ...), custom_call_target="tpu_custom_call" | custom-call | tf_op jit(solution)/shard_map/pallas_call | solution.py:326
  26.6 0.6 %collective-permute-done.5.bc = bf16[384,512]{1,0:T(8,128)(2,1)S(1)} collective-permute-done((bf16[384,512]{1,0:T(8,128)(2,1)S(1)}, bf16[384,512]{1,0:T(8,128)(2,1)S(1)}, u32[]{:S(2)}, u32[]{:S(2)}) %collective-permute-start.5) | collective-permute-done | bytes 393248 | tf_op jit(solution)/shard_map/ppermute | solution.py:320
  27.2 1.5 %shard_map.64.partial = f32[192,1152]{1,0:T(8,128)S(1)} custom-call(s32[7]{0:T(128)S(1)} %stack.31.place, bf16[2048,1152]{1,0:T(8,128)(2,1)S(1)} %get-tuple-element.37.kept, bf16[192,512]{1,0:T(8,128)(2,1)S(1)} %collective-permute-done.4.a, bf16[384,512]{1,0:T(8,128)(2,1)S(1)} %collective-permute-done.5.bc), custom_call_target="tpu_custom_call" | custom-call | tf_op jit(solution)/shard_map/pallas_call | solution.py:326
  28.7 0.5 collective-permute-done.3.b.near_picked
  29.2 0.1 collective-permute-done.6.d
  29.3 1.8 %shard_map.65 = (bf16[208,512]{1,0:T(8,128)(2,1)S(1)}, bf16[192,1152]{1,0:T(8,128)(2,1)S(1)}) custom-call(s32[7]{0:T(128)S(1)} %stack.31.place, bf16[2048,1152]{1,0:T(8,128)(2,1)S(1)} %get-tuple-element.37.kept, s32[192,128]{1,0:T(8,128)S(1)} %get-tuple-element.46.other.targets, f32[192,1152]{1,0:T(8,128)S(1)} %shard_map.64.partial, ...), custom_call_target="tpu_custom_call" | custom-call | tf_op jit(solution)/shard_map/pallas_call | solution.py:326
  31.1 1.6 %collective-permute-start.7 = (bf16[208,512]{1,0:T(8,128)(2,1)S(1)}, bf16[208,512]{1,0:T(8,128)(2,1)S(1)}, u32[]{:S(2)}, u32[]{:S(2)}) collective-permute-start(bf16[208,512]{1,0:T(8,128)(2,1)S(1)} %get-tuple-element.49), channel_id=1, source_target_pairs={{0,4},{4,0},{1,5},{5,1},{2,6},{6,2},{3,7},{7,3},{8,12},{12,8},{9,1... | collective-permute-start | bytes 638984 | tf_op jit(solution)/shard_map/ppermute | solution.py:320
  32.7 3.6 %collective-permute-start.8 = (bf16[224,512]{1,0:T(8,128)(2,1)S(1)}, bf16[224,512]{1,0:T(8,128)(2,1)S(1)}, u32[]{:S(2)}, u32[]{:S(2)}) collective-permute-start(bf16[224,512]{1,0:T(8,128)(2,1)S(1)} %shard_map.67), channel_id=1, source_target_pairs={{0,2},{1,3},{2,0},{3,1},{4,6},{5,7},{6,4},{7,5},{8,10},{9,11},{10,... | collective-permute-start | bytes 688136 | tf_op jit(solution)/shard_map/ppermute | solution.py:317
  36.3 1.5 %shard_map.69 = bf16[384,512]{1,0:T(8,128)(2,1)S(1)} custom-call(s32[7]{0:T(128)S(1)} %stack.31.place, bf16[2048,1152]{1,0:T(8,128)(2,1)S(1)} %get-tuple-element.37.kept, bf16[192,1152]{1,0:T(8,128)(2,1)S(1)} %get-tuple-element.54.others), custom_call_target="tpu_custom_call" | custom-call | tf_op jit(solution)/shard_map/pallas_call | solution.py:326
  37.8 0.3 shard_map.66
  38.1 0.9 %collective-permute-start.11 = (bf16[384,512]{1,0:T(8,128)(2,1)S(1)}, bf16[384,512]{1,0:T(8,128)(2,1)S(1)}, u32[]{:S(2)}, u32[]{:S(2)}) collective-permute-start(bf16[384,512]{1,0:T(8,128)(2,1)S(1)} %shard_map.69), channel_id=1, source_target_pairs={{0,4},{4,0},{1,5},{5,1},{2,6},{6,2},{3,7},{7,3},{8,12},{12,8},{9,1... | collective-permute-start | bytes 1179656 | tf_op jit(solution)/shard_map/ppermute | solution.py:320
  38.9 0.4 collective-permute-start.9
  39.4 1.6 %collective-permute-start.12 = (bf16[192,512]{1,0:T(8,128)(2,1)S(1)}, bf16[192,512]{1,0:T(8,128)(2,1)S(1)}, u32[]{:S(2)}, u32[]{:S(2)}) collective-permute-start(bf16[192,512]{1,0:T(8,128)(2,1)S(1)} %get-tuple-element.56), channel_id=1, source_target_pairs={{0,1},{1,0},{2,3},{3,2},{4,5},{5,4},{6,7},{7,6},{8,9},{9,8},{10,11... | collective-permute-start | bytes 589832 | tf_op jit(solution)/shard_map/ppermute | solution.py:317
  41.0 3.5 %collective-permute-done.8.c = bf16[224,512]{1,0:T(8,128)(2,1)S(1)} collective-permute-done((bf16[224,512]{1,0:T(8,128)(2,1)S(1)}, bf16[224,512]{1,0:T(8,128)(2,1)S(1)}, u32[]{:S(2)}, u32[]{:S(2)}) %collective-permute-start.8) | collective-permute-done | bytes 229408 | tf_op jit(solution)/shard_map/ppermute | solution.py:317
  44.4 0.2 collective-permute-done.9.got
  44.6 0.1 collective-permute-start.17
  44.7 3.0 %collective-permute-start.10 = (f32[8,192]{1,0:T(8,128)S(1)}, f32[8,192]{1,0:T(8,128)S(1)}, u32[]{:S(2)}, u32[]{:S(2)}) collective-permute-start(f32[8,192]{1,0:T(8,128)S(1)} %shard_map.68.half), channel_id=1, source_target_pairs={{0,2},{1,3},{2,0},{3,1},{4,6},{5,7},{6,4},{7,5},{8,10},{9,11},{10,... | collective-permute-start | bytes 18440 | tf_op jit(solution)/shard_map/ppermute | solution.py:317
  47.8 1.1 %shard_map.71 = bf16[192,512]{1,0:T(8,128)(2,1)S(1)} custom-call(s32[7]{0:T(128)S(1)} %stack.31.place, bf16[2048,1152]{1,0:T(8,128)(2,1)S(1)} %get-tuple-element.37.kept, bf16[192,1152]{1,0:T(8,128)(2,1)S(1)} %get-tuple-element.54.others), custom_call_target="tpu_custom_call" | custom-call | tf_op jit(solution)/shard_map/pallas_call | solution.py:326
  48.9 0.0 collective-permute-done.11.got
  48.9 0.8 %collective-permute-start.13 = (bf16[192,512]{1,0:T(8,128)(2,1)S(1)}, bf16[192,512]{1,0:T(8,128)(2,1)S(1)}, u32[]{:S(2)}, u32[]{:S(2)}) collective-permute-start(bf16[192,512]{1,0:T(8,128)(2,1)S(1)} %shard_map.71), channel_id=1, source_target_pairs={{0,4},{4,0},{1,5},{5,1},{2,6},{6,2},{3,7},{7,3},{8,12},{12,8},{9,1... | collective-permute-start | bytes 589832 | tf_op jit(solution)/shard_map/ppermute | solution.py:320
  49.7 0.0 collective-permute-done.12.relayed
  49.7 0.5 shard_map.70
  50.2 2.7 %collective-permute-start.14 = (bf16[192,512]{1,0:T(8,128)(2,1)S(1)}, bf16[192,512]{1,0:T(8,128)(2,1)S(1)}, u32[]{:S(2)}, u32[]{:S(2)}) collective-permute-start(bf16[192,512]{1,0:T(8,128)(2,1)S(1)} %get-tuple-element.61), channel_id=1, source_target_pairs={{0,2},{1,3},{2,0},{3,1},{4,6},{5,7},{6,4},{7,5},{8,10},{9,11},{10,... | collective-permute-start | bytes 589832 | tf_op jit(solution)/shard_map/ppermute | solution.py:317
  52.9 0.9 %collective-permute-start.18 = (bf16[192,512]{1,0:T(8,128)(2,1)S(1)}, bf16[192,512]{1,0:T(8,128)(2,1)S(1)}, u32[]{:S(2)}, u32[]{:S(2)}) collective-permute-start(bf16[192,512]{1,0:T(8,128)(2,1)S(1)} %shard_map.73), channel_id=1, source_target_pairs={{0,4},{4,0},{1,5},{5,1},{2,6},{6,2},{3,7},{7,3},{8,12},{12,8},{9,1... | collective-permute-start | bytes 589832 | tf_op jit(solution)/shard_map/ppermute | solution.py:320
  53.8 0.7 %collective-permute-start.16 = (bf16[192,512]{1,0:T(8,128)(2,1)S(1)}, bf16[192,512]{1,0:T(8,128)(2,1)S(1)}, u32[]{:S(2)}, u32[]{:S(2)}) collective-permute-start(bf16[192,512]{1,0:T(8,128)(2,1)S(1)} %get-tuple-element.64), channel_id=1, source_target_pairs={{0,1},{1,0},{2,3},{3,2},{4,5},{5,4},{6,7},{7,6},{8,9},{9,8},{10,11... | collective-permute-start | bytes 589832 | tf_op jit(solution)/shard_map/ppermute | solution.py:317
  54.5 1.6 %collective-permute-start.15 = (f32[1,192]{1,0:T(1,128)S(1)}, f32[1,192]{1,0:T(1,128)S(1)}, u32[]{:S(2)}, u32[]{:S(2)}) collective-permute-start(f32[1,192]{1,0:T(1,128)S(1)} %get-tuple-element.62.loss), channel_id=1, source_target_pairs={{0,4},{4,0},{1,5},{5,1},{2,6},{6,2},{3,7},{7,3},{8,12},{12,8},{9,1... | collective-permute-start | bytes 2312 | tf_op jit(solution)/shard_map/ppermute | solution.py:320
  56.1 2.7 %collective-permute-done.15.other_loss = f32[1,192]{1,0:T(1,128)S(1)} collective-permute-done((f32[1,192]{1,0:T(1,128)S(1)}, f32[1,192]{1,0:T(1,128)S(1)}, u32[]{:S(2)}, u32[]{:S(2)}) %collective-permute-start.15) | collective-permute-done | bytes 800 | tf_op jit(solution)/shard_map/ppermute | solution.py:320
  58.9 0.0 collective-permute-done.13.got
  58.9 0.7 %collective-permute-done.14.second = bf16[192,512]{1,0:T(8,128)(2,1)S(1)} collective-permute-done((bf16[192,512]{1,0:T(8,128)(2,1)S(1)}, bf16[192,512]{1,0:T(8,128)(2,1)S(1)}, u32[]{:S(2)}, u32[]{:S(2)}) %collective-permute-start.14) | collective-permute-done | bytes 196640 | tf_op jit(solution)/shard_map/ppermute | solution.py:317
  59.6 1.3 %shard_map.72 = (f32[192,512]{1,0:T(8,128)S(1)}, f32[384]{0:T(512)}) custom-call(s32[7]{0:T(128)S(1)} %stack.31.place, f32[4,192,128]{2,1,0:T(8,128)S(1)} %get-tuple-element.58.columns, f32[4,192,512]{2,1,0:T(8,128)S(1)} %get-tuple-element.50.sums, bf16[192,512]{1,0:T(8,128)(2,1)S(1)} %collective-permute-done.13.got, ...), custom_call_target="tpu_custom_call" | custom-call | tf_op jit(solution)/shard_map/pallas_call | solution.py:326
  60.9 0.0 collective-permute-done.16.first
  60.9 0.8 %shard_map.74 = bf16[192,512]{1,0:T(8,128)(2,1)} custom-call(f32[4,192,128]{2,1,0:T(8,128)S(1)} %get-tuple-element.58.columns, f32[192,512]{1,0:T(8,128)S(1)} %get-tuple-element.63.partial, bf16[192,512]{1,0:T(8,128)(2,1)S(1)} %collective-permute-done.16.first, bf16[192,512]{1,0:T(8,128)(2,1)S(1)} %collective-permute-done.18.theirs), custom_call_target="tpu_custom_call" | custom-call | tf_op jit(solution)/shard_map/pallas_call | solution.py:326
  (13 shorter events, 0.1 us)
Async XLA Ops:
  0.7 2.9 %copy-start = (bf16[192,512]{1,0:T(8,128)(2,1)S(1)}, bf16[192,512]{1,0:T(8,128)(2,1)}, u32[]{:S(2)}) copy-start(bf16[192,512]{1,0:T(8,128)(2,1)} %a) | copy-start | bytes 589828
  0.7 10.1 %copy-start.1 = (s32[384]{0:T(512)S(1)}, s32[384]{0:T(512)}, u32[]{:S(2)}) copy-start(s32[384]{0:T(512)} %targets.1) | copy-start | bytes 4612
  0.7 10.1 %copy-start.2 = (f32[384]{0:T(512)S(1)}, f32[384]{0:T(512)}, u32[]{:S(2)}) copy-start(f32[384]{0:T(512)} %scale.1) | copy-start | bytes 4612
  3.7 11.3 %collective-permute-start.1 = (bf16[192,512]{1,0:T(8,128)(2,1)S(1)}, bf16[192,512]{1,0:T(8,128)(2,1)S(1)}, u32[]{:S(2)}, u32[]{:S(2)}) collective-permute-start(bf16[192,512]{1,0:T(8,128)(2,1)S(1)} %copy-done), channel_id=1, source_target_pairs={{0,2},{1,3},{2,0},{3,1},{4,6},{5,7},{6,4},{7,5},{8,10},{9,11},{10,... | collective-permute-start | bytes 589832 | tf_op jit(solution)/shard_map/ppermute | solution.py:317
  7.8 7.8 %collective-permute-start = (bf16[192,512]{1,0:T(8,128)(2,1)S(1)}, bf16[192,512]{1,0:T(8,128)(2,1)S(1)}, u32[]{:S(2)}, u32[]{:S(2)}) collective-permute-start(bf16[192,512]{1,0:T(8,128)(2,1)S(1)} %copy-done), channel_id=1, source_target_pairs={{0,1},{1,0},{2,3},{3,2},{4,5},{5,4},{6,7},{7,6},{8,9},{9,8},{10,11... | collective-permute-start | bytes 589832 | tf_op jit(solution)/shard_map/ppermute | solution.py:317
  9.3 6.2 %collective-permute-start.4 = (bf16[192,512]{1,0:T(8,128)(2,1)S(1)}, bf16[192,512]{1,0:T(8,128)(2,1)S(1)}, u32[]{:S(2)}, u32[]{:S(2)}) collective-permute-start(bf16[192,512]{1,0:T(8,128)(2,1)S(1)} %copy-done), channel_id=1, source_target_pairs={{0,4},{4,0},{1,5},{5,1},{2,6},{6,2},{3,7},{7,3},{8,12},{12,8},{9,1... | collective-permute-start | bytes 589832 | tf_op jit(solution)/shard_map/ppermute | solution.py:320
  15.0 5.7 %collective-permute-start.2 = (bf16[192,512]{1,0:T(8,128)(2,1)S(1)}, bf16[192,512]{1,0:T(8,128)(2,1)S(1)}, u32[]{:S(2)}, u32[]{:S(2)}) collective-permute-start(bf16[192,512]{1,0:T(8,128)(2,1)S(1)} %collective-permute-done.1.c.b), channel_id=1, source_target_pairs={{0,1},{1,0},{2,3},{3,2},{4,5},{5,4},{6,7},{7,6},{8,9},{9,8},{10,11... | collective-permute-start | bytes 589832 | tf_op jit(solution)/shard_map/ppermute | solution.py:317
  15.6 11.6 %collective-permute-start.5 = (bf16[384,512]{1,0:T(8,128)(2,1)S(1)}, bf16[384,512]{1,0:T(8,128)(2,1)S(1)}, u32[]{:S(2)}, u32[]{:S(2)}) collective-permute-start(bf16[384,512]{1,0:T(8,128)(2,1)S(1)} %shard_map.63), channel_id=1, source_target_pairs={{0,4},{4,0},{1,5},{5,1},{2,6},{6,2},{3,7},{7,3},{8,12},{12,8},{9,1... | collective-permute-start | bytes 1179656 | tf_op jit(solution)/shard_map/ppermute | solution.py:320
  20.6 8.6 %collective-permute-start.3 = (bf16[384,512]{1,0:T(8,128)(2,1)S(1)}, bf16[384,512]{1,0:T(8,128)(2,1)S(1)}, u32[]{:S(2)}, u32[]{:S(2)}) collective-permute-start(bf16[384,512]{1,0:T(8,128)(2,1)S(1)} %get-tuple-element.45), channel_id=1, source_target_pairs={{0,1},{1,0},{2,3},{3,2},{4,5},{5,4},{6,7},{7,6},{8,9},{9,8},{10,11... | collective-permute-start | bytes 1179656 | tf_op jit(solution)/shard_map/ppermute | solution.py:317
  21.5 7.8 %collective-permute-start.6 = (bf16[192,512]{1,0:T(8,128)(2,1)S(1)}, bf16[192,512]{1,0:T(8,128)(2,1)S(1)}, u32[]{:S(2)}, u32[]{:S(2)}) collective-permute-start(bf16[192,512]{1,0:T(8,128)(2,1)S(1)} %collective-permute-done.2.d), channel_id=1, source_target_pairs={{0,4},{4,0},{1,5},{5,1},{2,6},{6,2},{3,7},{7,3},{8,12},{12,8},{9,1... | collective-permute-start | bytes 589832 | tf_op jit(solution)/shard_map/ppermute | solution.py:320
  31.1 6.7 %collective-permute-start.7 = (bf16[208,512]{1,0:T(8,128)(2,1)S(1)}, bf16[208,512]{1,0:T(8,128)(2,1)S(1)}, u32[]{:S(2)}, u32[]{:S(2)}) collective-permute-start(bf16[208,512]{1,0:T(8,128)(2,1)S(1)} %get-tuple-element.49), channel_id=1, source_target_pairs={{0,4},{4,0},{1,5},{5,1},{2,6},{6,2},{3,7},{7,3},{8,12},{12,8},{9,1... | collective-permute-start | bytes 638984 | tf_op jit(solution)/shard_map/ppermute | solution.py:320
  32.7 11.8 %collective-permute-start.8 = (bf16[224,512]{1,0:T(8,128)(2,1)S(1)}, bf16[224,512]{1,0:T(8,128)(2,1)S(1)}, u32[]{:S(2)}, u32[]{:S(2)}) collective-permute-start(bf16[224,512]{1,0:T(8,128)(2,1)S(1)} %shard_map.67), channel_id=1, source_target_pairs={{0,2},{1,3},{2,0},{3,1},{4,6},{5,7},{6,4},{7,5},{8,10},{9,11},{10,... | collective-permute-start | bytes 688136 | tf_op jit(solution)/shard_map/ppermute | solution.py:317
  38.1 10.8 %collective-permute-start.11 = (bf16[384,512]{1,0:T(8,128)(2,1)S(1)}, bf16[384,512]{1,0:T(8,128)(2,1)S(1)}, u32[]{:S(2)}, u32[]{:S(2)}) collective-permute-start(bf16[384,512]{1,0:T(8,128)(2,1)S(1)} %shard_map.69), channel_id=1, source_target_pairs={{0,4},{4,0},{1,5},{5,1},{2,6},{6,2},{3,7},{7,3},{8,12},{12,8},{9,1... | collective-permute-start | bytes 1179656 | tf_op jit(solution)/shard_map/ppermute | solution.py:320
  38.9 5.7 %collective-permute-start.9 = (f32[8,192]{1,0:T(8,128)S(1)}, f32[8,192]{1,0:T(8,128)S(1)}, u32[]{:S(2)}, u32[]{:S(2)}) collective-permute-start(f32[8,192]{1,0:T(8,128)S(1)} %get-tuple-element.53.pair), channel_id=1, source_target_pairs={{0,1},{1,0},{2,3},{3,2},{4,5},{5,4},{6,7},{7,6},{8,9},{9,8},{10,11... | collective-permute-start | bytes 18440 | tf_op jit(solution)/shard_map/ppermute | solution.py:317
  39.4 10.3 %collective-permute-start.12 = (bf16[192,512]{1,0:T(8,128)(2,1)S(1)}, bf16[192,512]{1,0:T(8,128)(2,1)S(1)}, u32[]{:S(2)}, u32[]{:S(2)}) collective-permute-start(bf16[192,512]{1,0:T(8,128)(2,1)S(1)} %get-tuple-element.56), channel_id=1, source_target_pairs={{0,1},{1,0},{2,3},{3,2},{4,5},{5,4},{6,7},{7,6},{8,9},{9,8},{10,11... | collective-permute-start | bytes 589832 | tf_op jit(solution)/shard_map/ppermute | solution.py:317
  44.6 8.2 %collective-permute-start.17 = (bf16[192,512]{1,0:T(8,128)(2,1)S(1)}, bf16[192,512]{1,0:T(8,128)(2,1)S(1)}, u32[]{:S(2)}, u32[]{:S(2)}) collective-permute-start(bf16[192,512]{1,0:T(8,128)(2,1)S(1)} %get-tuple-element.68), channel_id=1, source_target_pairs={{0,1},{1,0},{2,3},{3,2},{4,5},{5,4},{6,7},{7,6},{8,9},{9,8},{10,11... | collective-permute-start | bytes 589832 | tf_op jit(solution)/shard_map/ppermute | solution.py:317
  44.7 5.0 %collective-permute-start.10 = (f32[8,192]{1,0:T(8,128)S(1)}, f32[8,192]{1,0:T(8,128)S(1)}, u32[]{:S(2)}, u32[]{:S(2)}) collective-permute-start(f32[8,192]{1,0:T(8,128)S(1)} %shard_map.68.half), channel_id=1, source_target_pairs={{0,2},{1,3},{2,0},{3,1},{4,6},{5,7},{6,4},{7,5},{8,10},{9,11},{10,... | collective-permute-start | bytes 18440 | tf_op jit(solution)/shard_map/ppermute | solution.py:317
  48.9 10.0 %collective-permute-start.13 = (bf16[192,512]{1,0:T(8,128)(2,1)S(1)}, bf16[192,512]{1,0:T(8,128)(2,1)S(1)}, u32[]{:S(2)}, u32[]{:S(2)}) collective-permute-start(bf16[192,512]{1,0:T(8,128)(2,1)S(1)} %shard_map.71), channel_id=1, source_target_pairs={{0,4},{4,0},{1,5},{5,1},{2,6},{6,2},{3,7},{7,3},{8,12},{12,8},{9,1... | collective-permute-start | bytes 589832 | tf_op jit(solution)/shard_map/ppermute | solution.py:320
  50.2 9.4 %collective-permute-start.14 = (bf16[192,512]{1,0:T(8,128)(2,1)S(1)}, bf16[192,512]{1,0:T(8,128)(2,1)S(1)}, u32[]{:S(2)}, u32[]{:S(2)}) collective-permute-start(bf16[192,512]{1,0:T(8,128)(2,1)S(1)} %get-tuple-element.61), channel_id=1, source_target_pairs={{0,2},{1,3},{2,0},{3,1},{4,6},{5,7},{6,4},{7,5},{8,10},{9,11},{10,... | collective-permute-start | bytes 589832 | tf_op jit(solution)/shard_map/ppermute | solution.py:317
  52.9 8.0 %collective-permute-start.18 = (bf16[192,512]{1,0:T(8,128)(2,1)S(1)}, bf16[192,512]{1,0:T(8,128)(2,1)S(1)}, u32[]{:S(2)}, u32[]{:S(2)}) collective-permute-start(bf16[192,512]{1,0:T(8,128)(2,1)S(1)} %shard_map.73), channel_id=1, source_target_pairs={{0,4},{4,0},{1,5},{5,1},{2,6},{6,2},{3,7},{7,3},{8,12},{12,8},{9,1... | collective-permute-start | bytes 589832 | tf_op jit(solution)/shard_map/ppermute | solution.py:320
  53.8 7.1 %collective-permute-start.16 = (bf16[192,512]{1,0:T(8,128)(2,1)S(1)}, bf16[192,512]{1,0:T(8,128)(2,1)S(1)}, u32[]{:S(2)}, u32[]{:S(2)}) collective-permute-start(bf16[192,512]{1,0:T(8,128)(2,1)S(1)} %get-tuple-element.64), channel_id=1, source_target_pairs={{0,1},{1,0},{2,3},{3,2},{4,5},{5,4},{6,7},{7,6},{8,9},{9,8},{10,11... | collective-permute-start | bytes 589832 | tf_op jit(solution)/shard_map/ppermute | solution.py:317
  54.5 4.3 %collective-permute-start.15 = (f32[1,192]{1,0:T(1,128)S(1)}, f32[1,192]{1,0:T(1,128)S(1)}, u32[]{:S(2)}, u32[]{:S(2)}) collective-permute-start(f32[1,192]{1,0:T(1,128)S(1)} %get-tuple-element.62.loss), channel_id=1, source_target_pairs={{0,4},{4,0},{1,5},{5,1},{2,6},{6,2},{3,7},{7,3},{8,12},{12,8},{9,1... | collective-permute-start | bytes 2312 | tf_op jit(solution)/shard_map/ppermute | solution.py:320
